TPU v7x, 512 devices: a whole 4x8x8 slice. The times are simulated.
512 devices in a mesh: seq: 64 (over z_hi, y, core), head: 8 (over z_lo, x).
Axes of the slice: x: 4, y: 8, z: 8 (z_hi: 4, z_lo: 2; z = z_hi * 2 + z_lo), core: 2. Of those that a mesh axis runs over, the one named last changes fastest.
Arguments:
- queries: bfloat16 [16384, 8, 4, 128], P(('seq', 'head')), may hold values from -210 to 210
- keys: bfloat16 [16384, 8, 128], P(('seq', 'head')), may hold values from -6 to 6
- values: bfloat16 [16384, 8, 128], P(('seq', 'head')), may hold values from -6 to 6
- d_attended: bfloat16 [16384, 8, 4, 128], P(('seq', 'head')), may hold values from -12 to 12
- shift_amounts: int32 [8], replicated, may hold values from 0 to 1024, as said below
Outputs:
- attended: bfloat16 [16384, 8, 4, 128], P(('seq', 'head'))
- d_queries: bfloat16 [16384, 8, 4, 128], P(('seq', 'head'))
- d_keys: bfloat16 [16384, 8, 128], P(('seq', 'head'))
- d_values: bfloat16 [16384, 8, 128], P(('seq', 'head'))
Inputs may be any that keep to these rules, and one draw needn't show every extreme that they name: `shift_amounts`: each head's shift is 0 or 1024, and exactly half of the 8 heads have 2048 // 2.
All inputs are finite; a program needn't handle non-finite values.
Results may differ from a plain program's by a relative error of at most 0.034.
Values may be sent and summed in bfloat16 or wider, within the bound.
No kernel may reach another device: no remote copies, remote signals or barrier semaphores. Data moves between devices by JAX's collectives and lax.ppermute only.
A program may use at most 64 MiB of HBM per device.

v0:
```python
import math

import jax
import jax.numpy as jnp
from jax import lax
from jax.sharding import PartitionSpec as P

GROUP = 2048


MASKED_LOGIT = -1e30


def from_behind(value, axis, by):
    size = lax.axis_size(axis)
    return lax.ppermute(value, axis, [(i, (i + by) % size) for i in range(size)])


def local(queries, keys, values, d_attended, shift_amounts):
    local_q, local_k, local_v, local_d = (
        lax.all_to_all(queries, "head", split_axis=1, concat_axis=0, tiled=True),
        lax.all_to_all(keys, "head", split_axis=1, concat_axis=0, tiled=True),
        lax.all_to_all(values, "head", split_axis=1, concat_axis=0, tiled=True),
        lax.all_to_all(d_attended, "head", split_axis=1, concat_axis=0, tiled=True),
    )
    tok_rows, kv_heads, per_group, head_dim = local_q.shape
    scaling = 1.0 / math.sqrt(head_dim)
    n_seq = lax.axis_size("seq")
    seq_pos = lax.axis_index("seq")
    head_pos = lax.axis_index("head")
    seq_tokens = tok_rows * n_seq
    group_span = GROUP // tok_rows
    shifts = lax.dynamic_slice_in_dim(shift_amounts, head_pos * kv_heads, kv_heads)
    offsets = jnp.arange(tok_rows, dtype=jnp.int32)
    query_rank = (seq_pos * tok_rows + offsets[None, :] - shifts[:, None]) % seq_tokens

    def allowed_for(distance):
        source = (seq_pos - distance) % n_seq
        key_rank = (source * tok_rows + offsets[None, :] - shifts[:, None]) % seq_tokens
        same_group = query_rank[:, :, None] // GROUP == key_rank[:, None, :] // GROUP
        return same_group & (key_rank[:, None, :] <= query_rank[:, :, None])

    own_pair = jnp.stack((local_k, local_v), 0)
    blocks = [own_pair]
    for distance in range(1, group_span):
        blocks.append(from_behind(blocks[-1], "seq", 1))
    allowed_sets = [allowed_for(distance) for distance in range(group_span)]

    def logits_of(distance):
        logits = (
            jnp.einsum(
                "tkgd,ukd->kgtu", local_q, blocks[distance][0], preferred_element_type=jnp.float32
            )
            * scaling
        )
        return jnp.where(allowed_sets[distance][:, None], logits, MASKED_LOGIT)

    stats = (
        jnp.full((kv_heads, per_group, tok_rows), MASKED_LOGIT, jnp.float32),
        jnp.zeros((kv_heads, per_group, tok_rows), jnp.float32),
    )
    for distance in range(group_span):
        highest, totals = stats
        stats_logits = logits_of(distance)
        updated = jnp.maximum(highest, jnp.max(stats_logits, axis=3))
        totals = totals * jnp.exp(highest - updated) + jnp.sum(
            jnp.exp(stats_logits - updated[..., None]), axis=3
        )
        stats = (updated, totals)
    lse = stats[0] + jnp.log(stats[1])
    zero_part = jnp.zeros((tok_rows, kv_heads, head_dim), jnp.float32)
    accumulated = jnp.zeros((tok_rows, kv_heads, per_group, head_dim), jnp.float32)
    value_parts = []
    for distance in range(group_span):
        output_accumulated = accumulated
        prob_rounded = jnp.exp(logits_of(distance) - lse[..., None]).astype(jnp.bfloat16)
        output_accumulated = output_accumulated + jnp.einsum(
            "kgtu,ukd->tkgd", prob_rounded, blocks[distance][1], preferred_element_type=jnp.float32
        )
        portion = jnp.einsum(
            "kgtu,tkgd->ukd", prob_rounded, local_d, preferred_element_type=jnp.float32
        )
        accumulated, portion = (output_accumulated, portion)
        value_parts.append(portion)
    attended = accumulated.astype(jnp.bfloat16)
    row_dot = jnp.sum(local_d.astype(jnp.float32) * attended.astype(jnp.float32), axis=3)
    row_dot = jnp.transpose(row_dot, (1, 2, 0))

    def gradient_step(distance, carried):
        grad_q, unused_part = carried
        exact_probs = jnp.exp(logits_of(distance) - lse[..., None])
        d_probs = jnp.einsum(
            "tkgd,ukd->kgtu", local_d, blocks[distance][1], preferred_element_type=jnp.float32
        )
        d_scores = (exact_probs * (d_probs - row_dot[..., None])).astype(jnp.bfloat16)
        grad_q = grad_q + jnp.einsum(
            "kgtu,ukd->tkgd", d_scores, blocks[distance][0], preferred_element_type=jnp.float32
        )
        portion = (
            jnp.einsum("kgtu,tkgd->ukd", d_scores, local_q, preferred_element_type=jnp.float32)
            * scaling
        )
        return (grad_q, portion)

    grad_q = jnp.zeros((tok_rows, kv_heads, per_group, head_dim), jnp.float32)
    grad_q, portion = gradient_step(0, (grad_q, zero_part))
    carried = jnp.stack((portion, value_parts[0]), 0)
    for distance in range(1, group_span):
        carried = from_behind(carried, "seq", 1)
        grad_q, portion = gradient_step(distance, (grad_q, zero_part))
        carried = carried + jnp.stack((portion, value_parts[distance]), 0)
    carried = from_behind(carried.astype(jnp.bfloat16), "seq", 1 - group_span).astype(carried.dtype)
    grad_queries = (grad_q * scaling).astype(jnp.bfloat16)
    grad_keys = carried[0].astype(jnp.bfloat16)
    grad_values = carried[1].astype(jnp.bfloat16)
    result = (
        lax.all_to_all(attended, "head", split_axis=0, concat_axis=1, tiled=True),
        lax.all_to_all(grad_queries, "head", split_axis=0, concat_axis=1, tiled=True),
        lax.all_to_all(grad_keys, "head", split_axis=0, concat_axis=1, tiled=True),
        lax.all_to_all(grad_values, "head", split_axis=0, concat_axis=1, tiled=True),
    )
    return (result[0], result[1], result[2], result[3])


def solution(mesh):
    in_specs = (
        P(("seq", "head"), None, None, None),
        P(("seq", "head"), None, None),
        P(("seq", "head"), None, None),
        P(("seq", "head"), None, None, None),
        P(),
    )
    out_specs = (
        P(("seq", "head"), None, None, None),
        P(("seq", "head"), None, None, None),
        P(("seq", "head"), None, None),
        P(("seq", "head"), None, None),
    )
    return jax.shard_map(local, mesh=mesh, in_specs=in_specs, out_specs=out_specs, check_vma=False)
```

profile of v0, /device:TPU:185, one launch (start us, length us, event | category | flops | bytes accessed | tf_op | source)
XLA Modules:
  0.0 256.0 jit_solution(17022972138852590686)
XLA Ops:
  2.2 6.0 %all-to-all-start = ((bf16[32,8,128]{2,0,1:T(8,128)(2,1)}), bf16[32,8,128]{2,0,1:T(8,128)(2,1)S(1)}, u32[]{:S(2)}, u32[]{:S(2)}) async-start(bf16[32,8,128]{2,0,1:T(8,128)(2,1)} %copy.161), calls=%async_computation | async-start | bytes 131072 | tf_op jit(solution)/shard_map/all_to_all | solution.py:22
  10.6 2.7 %all-to-all-done = bf16[32,8,128]{2,0,1:T(8,128)(2,1)S(1)} async-done(((bf16[32,8,128]{2,0,1:T(8,128)(2,1)}), bf16[32,8,128]{2,0,1:T(8,128)(2,1)S(1)}, u32[]{:S(2)}, u32[]{:S(2)}) %all-to-all-start) | async-done | bytes 65568 | tf_op jit(solution)/shard_map/all_to_all | solution.py:22
  13.3 3.4 %all-to-all-start.2 = ((bf16[32,8,128]{2,0,1:T(8,128)(2,1)}), bf16[32,8,128]{2,0,1:T(8,128)(2,1)S(1)}, u32[]{:S(2)}, u32[]{:S(2)}) async-start(bf16[32,8,128]{2,0,1:T(8,128)(2,1)} %copy.164), calls=%async_computation.2 | async-start | bytes 131072 | tf_op jit(solution)/shard_map/all_to_all | solution.py:23
  18.7 3.1 %all-to-all-done.2 = bf16[32,8,128]{2,0,1:T(8,128)(2,1)S(1)} async-done(((bf16[32,8,128]{2,0,1:T(8,128)(2,1)}), bf16[32,8,128]{2,0,1:T(8,128)(2,1)S(1)}, u32[]{:S(2)}, u32[]{:S(2)}) %all-to-all-start.2) | async-done | bytes 65568 | tf_op jit(solution)/shard_map/all_to_all | solution.py:23
  21.8 3.4 %all-to-all-start.1 = ((bf16[32,8,4,128]{3,2,0,1:T(4,128)(2,1)}), bf16[32,8,4,128]{3,2,0,1:T(4,128)(2,1)S(1)}, u32[]{:S(2)}, u32[]{:S(2)}) async-start(bf16[32,8,4,128]{3,2,0,1:T(4,128)(2,1)} %copy.162), calls=%async_computation.1 | async-start | bytes 524288 | tf_op jit(solution)/shard_map/all_to_all | solution.py:21
  28.5 8.5 %collective-permute-start = (bf16[2,256,1,128]{3,1,2,0:T(8,128)(2,1)S(1)}, bf16[2,256,1,128]{3,1,2,0:T(8,128)(2,1)S(1)}, u32[]{:S(2)}, u32[]{:S(2)}) collective-permute-start(bf16[2,256,1,128]{3,1,2,0:T(8,128)(2,1)S(1)} %pad_maximum_fusion.1), channel_id=1, source_target_pairs={{0,8},{8,16},{16,24},{24,32},{32,40},{40,48},{48,56},{56,64},{64,7... | collective-permute-start | bytes 393224 | tf_op jit(solution)/shard_map/ppermute | solution.py:16
  37.0 5.4 %all-to-all-start.4 = ((bf16[32,8,4,128]{3,0,2,1:T(8,128)(2,1)}), bf16[32,8,4,128]{3,0,2,1:T(8,128)(2,1)S(1)}, u32[]{:S(2)}, u32[]{:S(2)}) async-start(bf16[32,8,4,128]{3,0,2,1:T(8,128)(2,1)} %copy.183), calls=%async_computation.4 | async-start | bytes 524288 | tf_op jit(solution)/shard_map/all_to_all | solution.py:24
  43.5 5.7 %collective-permute-start.1 = (bf16[2,256,1,128]{3,1,2,0:T(8,128)(2,1)S(1)}, bf16[2,256,1,128]{3,1,2,0:T(8,128)(2,1)S(1)}, u32[]{:S(2)}, u32[]{:S(2)}) collective-permute-start(bf16[2,256,1,128]{3,1,2,0:T(8,128)(2,1)S(1)} %collective-permute-done), channel_id=1, source_target_pairs={{0,8},{8,16},{16,24},{24,32},{32,40},{40,48},{48,56},{56,64},{64,7... | collective-permute-start | bytes 393224 | tf_op jit(solution)/shard_map/ppermute | solution.py:16
  51.1 9.9 %collective-permute-start.2 = (bf16[2,256,1,128]{3,1,2,0:T(8,128)(2,1)S(1)}, bf16[2,256,1,128]{3,1,2,0:T(8,128)(2,1)S(1)}, u32[]{:S(2)}, u32[]{:S(2)}) collective-permute-start(bf16[2,256,1,128]{3,1,2,0:T(8,128)(2,1)S(1)} %collective-permute-done.1), channel_id=1, source_target_pairs={{0,8},{8,16},{16,24},{24,32},{32,40},{40,48},{48,56},{56,64},{64,7... | collective-permute-start | bytes 393224 | tf_op jit(solution)/shard_map/ppermute | solution.py:16
  62.9 10.0 %collective-permute-start.3 = (bf16[2,256,1,128]{3,1,2,0:T(8,128)(2,1)S(1)}, bf16[2,256,1,128]{3,1,2,0:T(8,128)(2,1)S(1)}, u32[]{:S(2)}, u32[]{:S(2)}) collective-permute-start(bf16[2,256,1,128]{3,1,2,0:T(8,128)(2,1)S(1)} %collective-permute-done.2), channel_id=1, source_target_pairs={{0,8},{8,16},{16,24},{24,32},{32,40},{40,48},{48,56},{56,64},{64,7... | collective-permute-start | bytes 393224 | tf_op jit(solution)/shard_map/ppermute | solution.py:16
  74.8 9.9 %collective-permute-start.4 = (bf16[2,256,1,128]{3,1,2,0:T(8,128)(2,1)S(1)}, bf16[2,256,1,128]{3,1,2,0:T(8,128)(2,1)S(1)}, u32[]{:S(2)}, u32[]{:S(2)}) collective-permute-start(bf16[2,256,1,128]{3,1,2,0:T(8,128)(2,1)S(1)} %collective-permute-done.3), channel_id=1, source_target_pairs={{0,8},{8,16},{16,24},{24,32},{32,40},{40,48},{48,56},{56,64},{64,7... | collective-permute-start | bytes 393224 | tf_op jit(solution)/shard_map/ppermute | solution.py:16
  86.7 9.8 %collective-permute-start.5 = (bf16[2,256,1,128]{3,1,2,0:T(8,128)(2,1)S(1)}, bf16[2,256,1,128]{3,1,2,0:T(8,128)(2,1)S(1)}, u32[]{:S(2)}, u32[]{:S(2)}) collective-permute-start(bf16[2,256,1,128]{3,1,2,0:T(8,128)(2,1)S(1)} %collective-permute-done.4), channel_id=1, source_target_pairs={{0,8},{8,16},{16,24},{24,32},{32,40},{40,48},{48,56},{56,64},{64,7... | collective-permute-start | bytes 393224 | tf_op jit(solution)/shard_map/ppermute | solution.py:16
  98.4 9.7 %collective-permute-start.6 = (bf16[2,256,1,128]{3,1,2,0:T(8,128)(2,1)S(1)}, bf16[2,256,1,128]{3,1,2,0:T(8,128)(2,1)S(1)}, u32[]{:S(2)}, u32[]{:S(2)}) collective-permute-start(bf16[2,256,1,128]{3,1,2,0:T(8,128)(2,1)S(1)} %collective-permute-done.5), channel_id=1, source_target_pairs={{0,8},{8,16},{16,24},{24,32},{32,40},{40,48},{48,56},{56,64},{64,7... | collective-permute-start | bytes 393224 | tf_op jit(solution)/shard_map/ppermute | solution.py:16
  117.1 10.3 %collective-permute-start.7 = (f32[2,256,1,128]{3,1,2,0:T(8,128)}, f32[2,256,1,128]{3,1,2,0:T(8,128)}, u32[]{:S(2)}, u32[]{:S(2)}) collective-permute-start(f32[2,256,1,128]{3,1,2,0:T(8,128)} %pad_maximum_fusion), channel_id=1, source_target_pairs={{0,8},{8,16},{16,24},{24,32},{32,40},{40,48},{48,56},{56,64},{64,7... | collective-permute-start | bytes 786440 | tf_op jit(solution)/shard_map/ppermute | solution.py:16
  133.1 4.1 %all-to-all-start.5 = ((bf16[256,1,4,128]{3,2,1,0:T(4,128)(2,1)}), bf16[256,1,4,128]{3,2,1,0:T(4,128)(2,1)}, u32[]{:S(2)}, u32[]{:S(2)}) async-start(bf16[256,1,4,128]{3,2,1,0:T(4,128)(2,1)} %copy.208), calls=%async_computation.5 | async-start | bytes 524288 | tf_op jit(solution)/shard_map/all_to_all | solution.py:118
  142.0 1.9 collective-permute-start.8
  144.6 2.7 %collective-permute-done.8 = f32[2,256,1,128]{3,1,2,0:T(8,128)S(1)} collective-permute-done((f32[2,256,1,128]{3,1,2,0:T(8,128)S(1)}, f32[2,256,1,128]{3,1,2,0:T(8,128)S(1)}, u32[]{:S(2)}, u32[]{:S(2)}) %collective-permute-start.8) | collective-permute-done | bytes 262176 | tf_op jit(solution)/shard_map/ppermute | solution.py:16
  147.3 11.3 %collective-permute-start.9 = (f32[2,256,1,128]{3,1,2,0:T(8,128)S(1)}, f32[2,256,1,128]{3,1,2,0:T(8,128)S(1)}, u32[]{:S(2)}, u32[]{:S(2)}) collective-permute-start(f32[2,256,1,128]{3,1,2,0:T(8,128)S(1)} %maximum_add_fusion.1), channel_id=1, source_target_pairs={{0,8},{8,16},{16,24},{24,32},{32,40},{40,48},{48,56},{56,64},{64,7... | collective-permute-start | bytes 786440 | tf_op jit(solution)/shard_map/ppermute | solution.py:16
  159.2 2.7 %collective-permute-done.9 = f32[2,256,1,128]{3,1,2,0:T(8,128)S(1)} collective-permute-done((f32[2,256,1,128]{3,1,2,0:T(8,128)S(1)}, f32[2,256,1,128]{3,1,2,0:T(8,128)S(1)}, u32[]{:S(2)}, u32[]{:S(2)}) %collective-permute-start.9) | collective-permute-done | bytes 262176 | tf_op jit(solution)/shard_map/ppermute | solution.py:16
  161.9 11.4 %collective-permute-start.10 = (f32[2,256,1,128]{3,1,2,0:T(8,128)S(1)}, f32[2,256,1,128]{3,1,2,0:T(8,128)S(1)}, u32[]{:S(2)}, u32[]{:S(2)}) collective-permute-start(f32[2,256,1,128]{3,1,2,0:T(8,128)S(1)} %maximum_add_fusion.2), channel_id=1, source_target_pairs={{0,8},{8,16},{16,24},{24,32},{32,40},{40,48},{48,56},{56,64},{64,7... | collective-permute-start | bytes 786440 | tf_op jit(solution)/shard_map/ppermute | solution.py:16
  174.0 3.1 %collective-permute-done.10 = f32[2,256,1,128]{3,1,2,0:T(8,128)S(1)} collective-permute-done((f32[2,256,1,128]{3,1,2,0:T(8,128)S(1)}, f32[2,256,1,128]{3,1,2,0:T(8,128)S(1)}, u32[]{:S(2)}, u32[]{:S(2)}) %collective-permute-start.10) | collective-permute-done | bytes 262176 | tf_op jit(solution)/shard_map/ppermute | solution.py:16
  177.1 10.8 %collective-permute-start.11 = (f32[2,256,1,128]{3,1,2,0:T(8,128)S(1)}, f32[2,256,1,128]{3,1,2,0:T(8,128)S(1)}, u32[]{:S(2)}, u32[]{:S(2)}) collective-permute-start(f32[2,256,1,128]{3,1,2,0:T(8,128)S(1)} %maximum_add_fusion.3), channel_id=1, source_target_pairs={{0,8},{8,16},{16,24},{24,32},{32,40},{40,48},{48,56},{56,64},{64,7... | collective-permute-start | bytes 786440 | tf_op jit(solution)/shard_map/ppermute | solution.py:16
  188.5 3.3 %collective-permute-done.11 = f32[2,256,1,128]{3,1,2,0:T(8,128)S(1)} collective-permute-done((f32[2,256,1,128]{3,1,2,0:T(8,128)S(1)}, f32[2,256,1,128]{3,1,2,0:T(8,128)S(1)}, u32[]{:S(2)}, u32[]{:S(2)}) %collective-permute-start.11) | collective-permute-done | bytes 262176 | tf_op jit(solution)/shard_map/ppermute | solution.py:16
  191.8 10.4 %collective-permute-start.12 = (f32[2,256,1,128]{3,1,2,0:T(8,128)S(1)}, f32[2,256,1,128]{3,1,2,0:T(8,128)S(1)}, u32[]{:S(2)}, u32[]{:S(2)}) collective-permute-start(f32[2,256,1,128]{3,1,2,0:T(8,128)S(1)} %maximum_add_fusion.4), channel_id=1, source_target_pairs={{0,8},{8,16},{16,24},{24,32},{32,40},{40,48},{48,56},{56,64},{64,7... | collective-permute-start | bytes 786440 | tf_op jit(solution)/shard_map/ppermute | solution.py:16
  202.9 4.1 %collective-permute-done.12 = f32[2,256,1,128]{3,1,2,0:T(8,128)S(1)} collective-permute-done((f32[2,256,1,128]{3,1,2,0:T(8,128)S(1)}, f32[2,256,1,128]{3,1,2,0:T(8,128)S(1)}, u32[]{:S(2)}, u32[]{:S(2)}) %collective-permute-start.12) | collective-permute-done | bytes 262176 | tf_op jit(solution)/shard_map/ppermute | solution.py:16
  207.0 8.9 %collective-permute-start.13 = (f32[2,256,1,128]{3,1,2,0:T(8,128)S(1)}, f32[2,256,1,128]{3,1,2,0:T(8,128)S(1)}, u32[]{:S(2)}, u32[]{:S(2)}) collective-permute-start(f32[2,256,1,128]{3,1,2,0:T(8,128)S(1)} %maximum_add_fusion.5), channel_id=1, source_target_pairs={{0,8},{8,16},{16,24},{24,32},{32,40},{40,48},{48,56},{56,64},{64,7... | collective-permute-start | bytes 786440 | tf_op jit(solution)/shard_map/ppermute | solution.py:16
  216.6 3.8 %all-to-all-start.3 = ((bf16[256,1,4,128]{3,2,1,0:T(4,128)(2,1)}), bf16[256,1,4,128]{3,2,1,0:T(4,128)(2,1)S(1)}, u32[]{:S(2)}, u32[]{:S(2)}) async-start(bf16[256,1,4,128]{3,2,1,0:T(4,128)(2,1)} %copy.181), calls=%async_computation.3 | async-start | bytes 524288 | tf_op jit(solution)/shard_map/all_to_all | solution.py:117
  220.4 1.9 collective-permute-start.14
  222.4 11.7 %collective-permute-done.14 = bf16[2,256,1,128]{3,1,2,0:T(8,128)(2,1)S(1)} collective-permute-done((bf16[2,256,1,128]{3,1,2,0:T(8,128)(2,1)S(1)}, bf16[2,256,1,128]{3,1,2,0:T(8,128)(2,1)S(1)}, u32[]{:S(2)}, u32[]{:S(2)}) %collective-permute-start.14) | collective-permute-done | bytes 131104 | tf_op jit(solution)/shard_map/ppermute | solution.py:16
  236.0 5.6 %all-to-all-start.6 = ((bf16[8,2,2048]{2,1,0:T(2,128)(2,1)}), bf16[8,2,2048]{2,1,0:T(2,128)(2,1)S(1)}, u32[]{:S(2)}, u32[]{:S(2)}) async-start(bf16[8,2,2048]{2,1,0:T(2,128)(2,1)} %reshape.2131), calls=%async_computation.6 | async-start | bytes 131072 | tf_op jit(solution)/shard_map/all_to_all | solution.py:119
  242.9 3.9 %all-to-all-done.6 = bf16[8,2,2048]{2,1,0:T(2,128)(2,1)S(1)} async-done(((bf16[8,2,2048]{2,1,0:T(2,128)(2,1)}), bf16[8,2,2048]{2,1,0:T(2,128)(2,1)S(1)}, u32[]{:S(2)}, u32[]{:S(2)}) %all-to-all-start.6) | async-done | bytes 65568 | tf_op jit(solution)/shard_map/all_to_all | solution.py:119
  246.8 3.3 %all-to-all-start.7 = ((bf16[8,2,2048]{2,1,0:T(2,128)(2,1)}), bf16[8,2,2048]{2,1,0:T(2,128)(2,1)S(1)}, u32[]{:S(2)}, u32[]{:S(2)}) async-start(bf16[8,2,2048]{2,1,0:T(2,128)(2,1)} %reshape.2133), calls=%async_computation.7 | async-start | bytes 131072 | tf_op jit(solution)/shard_map/all_to_all | solution.py:120
  (179 shorter events, 51.6 us)
Async XLA Ops:
  2.2 15.1 %copy-start.27 = (bf16[32,8,4,128]{3,2,1,0:T(4,128)(2,1)S(1)}, bf16[32,8,4,128]{3,2,1,0:T(4,128)(2,1)}, u32[]{:S(2)}) copy-start(bf16[32,8,4,128]{3,2,1,0:T(4,128)(2,1)} %param.5) | copy-start | bytes 786436
  2.2 11.2 %all-to-all-start = ((bf16[32,8,128]{2,0,1:T(8,128)(2,1)}), bf16[32,8,128]{2,0,1:T(8,128)(2,1)S(1)}, u32[]{:S(2)}, u32[]{:S(2)}) async-start(bf16[32,8,128]{2,0,1:T(8,128)(2,1)} %copy.161), calls=%async_computation | async-start | bytes 131072 | tf_op jit(solution)/shard_map/all_to_all | solution.py:22
  13.3 8.5 %all-to-all-start.2 = ((bf16[32,8,128]{2,0,1:T(8,128)(2,1)}), bf16[32,8,128]{2,0,1:T(8,128)(2,1)S(1)}, u32[]{:S(2)}, u32[]{:S(2)}) async-start(bf16[32,8,128]{2,0,1:T(8,128)(2,1)} %copy.164), calls=%async_computation.2 | async-start | bytes 131072 | tf_op jit(solution)/shard_map/all_to_all | solution.py:23
  21.8 15.2 %all-to-all-start.1 = ((bf16[32,8,4,128]{3,2,0,1:T(4,128)(2,1)}), bf16[32,8,4,128]{3,2,0,1:T(4,128)(2,1)S(1)}, u32[]{:S(2)}, u32[]{:S(2)}) async-start(bf16[32,8,4,128]{3,2,0,1:T(4,128)(2,1)} %copy.162), calls=%async_computation.1 | async-start | bytes 524288 | tf_op jit(solution)/shard_map/all_to_all | solution.py:21
  28.5 15.0 %collective-permute-start = (bf16[2,256,1,128]{3,1,2,0:T(8,128)(2,1)S(1)}, bf16[2,256,1,128]{3,1,2,0:T(8,128)(2,1)S(1)}, u32[]{:S(2)}, u32[]{:S(2)}) collective-permute-start(bf16[2,256,1,128]{3,1,2,0:T(8,128)(2,1)S(1)} %pad_maximum_fusion.1), channel_id=1, source_target_pairs={{0,8},{8,16},{16,24},{24,32},{32,40},{40,48},{48,56},{56,64},{64,7... | collective-permute-start | bytes 393224 | tf_op jit(solution)/shard_map/ppermute | solution.py:16
  37.0 24.1 %all-to-all-start.4 = ((bf16[32,8,4,128]{3,0,2,1:T(8,128)(2,1)}), bf16[32,8,4,128]{3,0,2,1:T(8,128)(2,1)S(1)}, u32[]{:S(2)}, u32[]{:S(2)}) async-start(bf16[32,8,4,128]{3,0,2,1:T(8,128)(2,1)} %copy.183), calls=%async_computation.4 | async-start | bytes 524288 | tf_op jit(solution)/shard_map/all_to_all | solution.py:24
  43.5 68.9 %copy-start.20 = (bf16[2,256,1,128]{3,1,2,0:T(8,128)(2,1)}, bf16[2,256,1,128]{3,1,2,0:T(8,128)(2,1)S(1)}, u32[]{:S(2)}) copy-start(bf16[2,256,1,128]{3,1,2,0:T(8,128)(2,1)S(1)} %collective-permute-done) | copy-start | bytes 393220
  43.5 7.6 %collective-permute-start.1 = (bf16[2,256,1,128]{3,1,2,0:T(8,128)(2,1)S(1)}, bf16[2,256,1,128]{3,1,2,0:T(8,128)(2,1)S(1)}, u32[]{:S(2)}, u32[]{:S(2)}) collective-permute-start(bf16[2,256,1,128]{3,1,2,0:T(8,128)(2,1)S(1)} %collective-permute-done), channel_id=1, source_target_pairs={{0,8},{8,16},{16,24},{24,32},{32,40},{40,48},{48,56},{56,64},{64,7... | collective-permute-start | bytes 393224 | tf_op jit(solution)/shard_map/ppermute | solution.py:16
  51.1 61.6 %copy-start.22 = (bf16[2,256,1,128]{3,1,2,0:T(8,128)(2,1)}, bf16[2,256,1,128]{3,1,2,0:T(8,128)(2,1)S(1)}, u32[]{:S(2)}) copy-start(bf16[2,256,1,128]{3,1,2,0:T(8,128)(2,1)S(1)} %collective-permute-done.1) | copy-start | bytes 393220
  51.1 11.8 %collective-permute-start.2 = (bf16[2,256,1,128]{3,1,2,0:T(8,128)(2,1)S(1)}, bf16[2,256,1,128]{3,1,2,0:T(8,128)(2,1)S(1)}, u32[]{:S(2)}, u32[]{:S(2)}) collective-permute-start(bf16[2,256,1,128]{3,1,2,0:T(8,128)(2,1)S(1)} %collective-permute-done.1), channel_id=1, source_target_pairs={{0,8},{8,16},{16,24},{24,32},{32,40},{40,48},{48,56},{56,64},{64,7... | collective-permute-start | bytes 393224 | tf_op jit(solution)/shard_map/ppermute | solution.py:16
  62.0 65.7 %copy-start.6 = (f32[1,4,256,256]{2,3,1,0:T(8,128)}, f32[1,4,256,256]{2,3,1,0:T(8,128)S(1)}, u32[]{:S(2)}) copy-start(f32[1,4,256,256]{2,3,1,0:T(8,128)S(1)} %get-tuple-element.45) | copy-start | bytes 3145732
  62.4 65.0 %copy-start.8 = (f32[1,4,256,256]{2,3,1,0:T(8,128)}, f32[1,4,256,256]{2,3,1,0:T(8,128)S(1)}, u32[]{:S(2)}) copy-start(f32[1,4,256,256]{2,3,1,0:T(8,128)S(1)} %get-tuple-element.47) | copy-start | bytes 3145732
  62.9 11.9 %collective-permute-start.3 = (bf16[2,256,1,128]{3,1,2,0:T(8,128)(2,1)S(1)}, bf16[2,256,1,128]{3,1,2,0:T(8,128)(2,1)S(1)}, u32[]{:S(2)}, u32[]{:S(2)}) collective-permute-start(bf16[2,256,1,128]{3,1,2,0:T(8,128)(2,1)S(1)} %collective-permute-done.2), channel_id=1, source_target_pairs={{0,8},{8,16},{16,24},{24,32},{32,40},{40,48},{48,56},{56,64},{64,7... | collective-permute-start | bytes 393224 | tf_op jit(solution)/shard_map/ppermute | solution.py:16
  73.3 54.8 %copy-start.4 = (f32[1,4,256,256]{2,3,1,0:T(8,128)}, f32[1,4,256,256]{2,3,1,0:T(8,128)S(1)}, u32[]{:S(2)}) copy-start(f32[1,4,256,256]{2,3,1,0:T(8,128)S(1)} %get-tuple-element.43) | copy-start | bytes 3145732
  74.8 11.8 %collective-permute-start.4 = (bf16[2,256,1,128]{3,1,2,0:T(8,128)(2,1)S(1)}, bf16[2,256,1,128]{3,1,2,0:T(8,128)(2,1)S(1)}, u32[]{:S(2)}, u32[]{:S(2)}) collective-permute-start(bf16[2,256,1,128]{3,1,2,0:T(8,128)(2,1)S(1)} %collective-permute-done.3), channel_id=1, source_target_pairs={{0,8},{8,16},{16,24},{24,32},{32,40},{40,48},{48,56},{56,64},{64,7... | collective-permute-start | bytes 393224 | tf_op jit(solution)/shard_map/ppermute | solution.py:16
  85.1 43.3 %copy-start.2 = (f32[1,4,256,256]{2,3,1,0:T(8,128)}, f32[1,4,256,256]{2,3,1,0:T(8,128)S(1)}, u32[]{:S(2)}) copy-start(f32[1,4,256,256]{2,3,1,0:T(8,128)S(1)} %get-tuple-element.41) | copy-start | bytes 3145732
  86.7 11.7 %collective-permute-start.5 = (bf16[2,256,1,128]{3,1,2,0:T(8,128)(2,1)S(1)}, bf16[2,256,1,128]{3,1,2,0:T(8,128)(2,1)S(1)}, u32[]{:S(2)}, u32[]{:S(2)}) collective-permute-start(bf16[2,256,1,128]{3,1,2,0:T(8,128)(2,1)S(1)} %collective-permute-done.4), channel_id=1, source_target_pairs={{0,8},{8,16},{16,24},{24,32},{32,40},{40,48},{48,56},{56,64},{64,7... | collective-permute-start | bytes 393224 | tf_op jit(solution)/shard_map/ppermute | solution.py:16
  96.8 31.8 %copy-start = (f32[1,4,256,256]{2,3,1,0:T(8,128)}, f32[1,4,256,256]{2,3,1,0:T(8,128)S(1)}, u32[]{:S(2)}) copy-start(f32[1,4,256,256]{2,3,1,0:T(8,128)S(1)} %get-tuple-element.39) | copy-start | bytes 3145732
  98.4 11.7 %collective-permute-start.6 = (bf16[2,256,1,128]{3,1,2,0:T(8,128)(2,1)S(1)}, bf16[2,256,1,128]{3,1,2,0:T(8,128)(2,1)S(1)}, u32[]{:S(2)}, u32[]{:S(2)}) collective-permute-start(bf16[2,256,1,128]{3,1,2,0:T(8,128)(2,1)S(1)} %collective-permute-done.5), channel_id=1, source_target_pairs={{0,8},{8,16},{16,24},{24,32},{32,40},{40,48},{48,56},{56,64},{64,7... | collective-permute-start | bytes 393224 | tf_op jit(solution)/shard_map/ppermute | solution.py:16
  117.1 23.9 %collective-permute-start.7 = (f32[2,256,1,128]{3,1,2,0:T(8,128)}, f32[2,256,1,128]{3,1,2,0:T(8,128)}, u32[]{:S(2)}, u32[]{:S(2)}) collective-permute-start(f32[2,256,1,128]{3,1,2,0:T(8,128)} %pad_maximum_fusion), channel_id=1, source_target_pairs={{0,8},{8,16},{16,24},{24,32},{32,40},{40,48},{48,56},{56,64},{64,7... | collective-permute-start | bytes 786440 | tf_op jit(solution)/shard_map/ppermute | solution.py:16
  133.1 83.5 %all-to-all-start.5 = ((bf16[256,1,4,128]{3,2,1,0:T(4,128)(2,1)}), bf16[256,1,4,128]{3,2,1,0:T(4,128)(2,1)}, u32[]{:S(2)}, u32[]{:S(2)}) async-start(bf16[256,1,4,128]{3,2,1,0:T(4,128)(2,1)} %copy.208), calls=%async_computation.5 | async-start | bytes 524288 | tf_op jit(solution)/shard_map/all_to_all | solution.py:118
  142.0 5.2 %collective-permute-start.8 = (f32[2,256,1,128]{3,1,2,0:T(8,128)S(1)}, f32[2,256,1,128]{3,1,2,0:T(8,128)S(1)}, u32[]{:S(2)}, u32[]{:S(2)}) collective-permute-start(f32[2,256,1,128]{3,1,2,0:T(8,128)S(1)} %maximum_add_fusion), channel_id=1, source_target_pairs={{0,8},{8,16},{16,24},{24,32},{32,40},{40,48},{48,56},{56,64},{64,7... | collective-permute-start | bytes 786440 | tf_op jit(solution)/shard_map/ppermute | solution.py:16
  147.3 14.6 %collective-permute-start.9 = (f32[2,256,1,128]{3,1,2,0:T(8,128)S(1)}, f32[2,256,1,128]{3,1,2,0:T(8,128)S(1)}, u32[]{:S(2)}, u32[]{:S(2)}) collective-permute-start(f32[2,256,1,128]{3,1,2,0:T(8,128)S(1)} %maximum_add_fusion.1), channel_id=1, source_target_pairs={{0,8},{8,16},{16,24},{24,32},{32,40},{40,48},{48,56},{56,64},{64,7... | collective-permute-start | bytes 786440 | tf_op jit(solution)/shard_map/ppermute | solution.py:16
  158.9 14.4 %copy-start.12 = (bf16[4,256,256]{1,2,0:T(8,128)(2,1)S(1)}, bf16[4,256,256]{1,2,0:T(8,128)(2,1)}, u32[]{:S(2)}) copy-start(bf16[4,256,256]{1,2,0:T(8,128)(2,1)} %copy-done.11) | copy-start | bytes 1572868
  161.9 15.2 %collective-permute-start.10 = (f32[2,256,1,128]{3,1,2,0:T(8,128)S(1)}, f32[2,256,1,128]{3,1,2,0:T(8,128)S(1)}, u32[]{:S(2)}, u32[]{:S(2)}) collective-permute-start(f32[2,256,1,128]{3,1,2,0:T(8,128)S(1)} %maximum_add_fusion.2), channel_id=1, source_target_pairs={{0,8},{8,16},{16,24},{24,32},{32,40},{40,48},{48,56},{56,64},{64,7... | collective-permute-start | bytes 786440 | tf_op jit(solution)/shard_map/ppermute | solution.py:16
  177.1 14.7 %collective-permute-start.11 = (f32[2,256,1,128]{3,1,2,0:T(8,128)S(1)}, f32[2,256,1,128]{3,1,2,0:T(8,128)S(1)}, u32[]{:S(2)}, u32[]{:S(2)}) collective-permute-start(f32[2,256,1,128]{3,1,2,0:T(8,128)S(1)} %maximum_add_fusion.3), channel_id=1, source_target_pairs={{0,8},{8,16},{16,24},{24,32},{32,40},{40,48},{48,56},{56,64},{64,7... | collective-permute-start | bytes 786440 | tf_op jit(solution)/shard_map/ppermute | solution.py:16
  191.8 15.1 %collective-permute-start.12 = (f32[2,256,1,128]{3,1,2,0:T(8,128)S(1)}, f32[2,256,1,128]{3,1,2,0:T(8,128)S(1)}, u32[]{:S(2)}, u32[]{:S(2)}) collective-permute-start(f32[2,256,1,128]{3,1,2,0:T(8,128)S(1)} %maximum_add_fusion.4), channel_id=1, source_target_pairs={{0,8},{8,16},{16,24},{24,32},{32,40},{40,48},{48,56},{56,64},{64,7... | collective-permute-start | bytes 786440 | tf_op jit(solution)/shard_map/ppermute | solution.py:16
  207.0 13.4 %collective-permute-start.13 = (f32[2,256,1,128]{3,1,2,0:T(8,128)S(1)}, f32[2,256,1,128]{3,1,2,0:T(8,128)S(1)}, u32[]{:S(2)}, u32[]{:S(2)}) collective-permute-start(f32[2,256,1,128]{3,1,2,0:T(8,128)S(1)} %maximum_add_fusion.5), channel_id=1, source_target_pairs={{0,8},{8,16},{16,24},{24,32},{32,40},{40,48},{48,56},{56,64},{64,7... | collective-permute-start | bytes 786440 | tf_op jit(solution)/shard_map/ppermute | solution.py:16
  216.6 19.4 %all-to-all-start.3 = ((bf16[256,1,4,128]{3,2,1,0:T(4,128)(2,1)}), bf16[256,1,4,128]{3,2,1,0:T(4,128)(2,1)S(1)}, u32[]{:S(2)}, u32[]{:S(2)}) async-start(bf16[256,1,4,128]{3,2,1,0:T(4,128)(2,1)} %copy.181), calls=%async_computation.3 | async-start | bytes 524288 | tf_op jit(solution)/shard_map/all_to_all | solution.py:117
  220.4 13.7 %collective-permute-start.14 = (bf16[2,256,1,128]{3,1,2,0:T(8,128)(2,1)S(1)}, bf16[2,256,1,128]{3,1,2,0:T(8,128)(2,1)S(1)}, u32[]{:S(2)}, u32[]{:S(2)}) collective-permute-start(bf16[2,256,1,128]{3,1,2,0:T(8,128)(2,1)S(1)} %fusion.85), channel_id=1, source_target_pairs={{0,456},{8,464},{16,472},{24,480},{32,488},{40,496},{48,504},{56,0... | collective-permute-start | bytes 393224 | tf_op jit(solution)/shard_map/ppermute | solution.py:16
  236.0 10.8 %all-to-all-start.6 = ((bf16[8,2,2048]{2,1,0:T(2,128)(2,1)}), bf16[8,2,2048]{2,1,0:T(2,128)(2,1)S(1)}, u32[]{:S(2)}, u32[]{:S(2)}) async-start(bf16[8,2,2048]{2,1,0:T(2,128)(2,1)} %reshape.2131), calls=%async_computation.6 | async-start | bytes 131072 | tf_op jit(solution)/shard_map/all_to_all | solution.py:119
  246.8 8.5 %all-to-all-start.7 = ((bf16[8,2,2048]{2,1,0:T(2,128)(2,1)}), bf16[8,2,2048]{2,1,0:T(2,128)(2,1)S(1)}, u32[]{:S(2)}, u32[]{:S(2)}) async-start(bf16[8,2,2048]{2,1,0:T(2,128)(2,1)} %reshape.2133), calls=%async_computation.7 | async-start | bytes 131072 | tf_op jit(solution)/shard_map/all_to_all | solution.py:120
  (22 other events, 155.0 us)
where the time goes:
time: 258 us; the launch traced here: 256 us
  starting transfers between devices  165 us (64%)
  waiting for transfers between devices  46.4 us (18%)
  matrix products  17.4 us (7%)
  local copies, waits for them, and re-layouts  13.7 us (5%)
  other arithmetic  11.4 us (4%)
    ppermute x15, starting transfers between devices, from_behind(): lax.ppermute(value, axis, [(i, (i + by) % size) for i in range(size)])  130 us
    ppermute x15, waiting for transfers between devices, from_behind(): lax.ppermute(value, axis, [(i, (i + by) % size) for i in range(size)])  35 us
    unnamed x75, local copies, waits for them, and re-layouts  8.78 us
    all_to_all x1, starting transfers between devices, local(): lax.all_to_all(keys, 'head', split_axis=1, concat_axis=0, tiled=True)  5.96 us
    all_to_all x1, starting transfers between devices, local(): lax.all_to_all(grad_keys, 'head', split_axis=0, concat_axis=1, tiled=True)  5.61 us
    all_to_all x1, starting transfers between devices, local(): lax.all_to_all(d_attended, 'head', split_axis=1, concat_axis=0, tiled=True)  5.36 us
  transfers between devices with their start and end apart: 23, of which 16 were waited for; matrix products, arithmetic and copies ran while one was open for 13% of the time, Pallas kernels for 0%

commit v1 on v0

v1 whole, which is shorter than its diff:
```python
import math

import jax
import jax.numpy as jnp
from jax import lax
from jax.experimental import pallas as pl
from jax.experimental.pallas import tpu as pltpu
from jax.sharding import PartitionSpec as P

GROUP = 2048
HEADS = 8
PER = 4
HD = 128
TOK = 256
SUB = 32
ROWS = TOK * PER
COLS = 512
LOG2E = 1.4426950408889634
NEG = -1e30
F32 = jnp.float32
BF16 = jnp.bfloat16
VM = pl.BlockSpec(memory_space=pltpu.VMEM)
SM = pl.BlockSpec(memory_space=pltpu.SMEM)
AXES = ("seq", "head")


def params():
    return pltpu.CompilerParams(vmem_limit_bytes=48 * 1024 * 1024)


def dot(a, b):
    return jnp.dot(a, b, preferred_element_type=F32)


def place_of_head(shift_ref, head):
    place = jnp.zeros(head.shape, jnp.int32)
    plain = jnp.int32(0)
    moved = jnp.int32(HEADS // 2)
    for h in range(HEADS):
        is_moved = (shift_ref[h] > 0).astype(jnp.int32)
        rank = jnp.where(is_moved == 1, moved, plain)
        place = jnp.where(head == h, rank, place)
        moved = moved + is_moved
        plain = plain + 1 - is_moved
    return place


def kv_order(shift_ref, back):
    local = lax.broadcasted_iota(jnp.int32, (TOK, TOK), 0 if back else 1)
    placed = lax.broadcasted_iota(jnp.int32, (TOK, TOK), 1 if back else 0)
    head = lax.broadcasted_iota(jnp.int32, (TOK, 1) if back else (1, TOK), 0 if back else 1) & 7
    place = place_of_head(shift_ref, head)
    hit = ((local >> 3) == (placed & 31)) & (place == (placed >> 5))
    return jnp.where(hit, 1.0, 0.0).astype(BF16)


def q_order(shift_ref, back):
    local = lax.broadcasted_iota(jnp.int32, (TOK, TOK), 0 if back else 1)
    placed = lax.broadcasted_iota(jnp.int32, (TOK, TOK), 1 if back else 0)
    head = lax.broadcasted_iota(jnp.int32, (TOK, 1) if back else (1, TOK), 0 if back else 1)
    place = place_of_head(shift_ref, (head >> 2) & 7)
    same = ((local >> 5) == ((placed & 31) >> 2)) & ((local & 3) == (placed & 3))
    return jnp.where(same & (place == (placed >> 5)), 1.0, 0.0).astype(BF16)


def pack_kv_kernel(shift_ref, k_ref, v_ref, out_ref):
    order = kv_order(shift_ref, False)
    for n, ref in enumerate((k_ref, v_ref)):
        moved = dot(order, ref[...]).astype(BF16)
        for h in range(HEADS):
            out_ref[h, n * SUB : (n + 1) * SUB, :] = moved[h * SUB : (h + 1) * SUB]


def pack_q_kernel(shift_ref, q_ref, d_ref, out_ref):
    order = q_order(shift_ref, False)
    for n, ref in enumerate((q_ref, d_ref)):
        for b in range(4):
            moved = dot(order, ref[b * TOK : (b + 1) * TOK, :]).astype(BF16)
            for h in range(HEADS):
                at = n * 128 + b * 32
                out_ref[h, at : at + 32, :] = moved[h * 32 : (h + 1) * 32]


def unpack_kv_kernel(shift_ref, in_ref, k_ref, v_ref):
    order = kv_order(shift_ref, True)
    for n, ref in enumerate((k_ref, v_ref)):
        held = in_ref[:, n * SUB : (n + 1) * SUB, :].reshape(TOK, HD)
        ref[...] = dot(order, held).astype(BF16)


def unpack_q_kernel(shift_ref, in_ref, o_ref, q_ref):
    order = q_order(shift_ref, True)
    for n, ref in enumerate((o_ref, q_ref)):
        for b in range(4):
            at = n * 128 + b * 32
            held = in_ref[:, at : at + 32, :].reshape(TOK, HD)
            ref[b * TOK : (b + 1) * TOK, :] = dot(order, held).astype(BF16)


def attend_kernel(
    where_ref, qd_ref, a0, a1, a2, a3, b0, b1, b2, b3,
    oq_ref, near_ref, far_ref,
    k_s, v_s, kt_s, vt_s, q_s, d_s, qt_s, dt_s, s_s, m_s, l_s, ot_s, dqt_s, dot_s,
):
    chips = where_ref[0]
    core = where_ref[1]
    scaling = 1.0 / math.sqrt(HD)
    exponent = scaling * LOG2E

    def stage(slot, ref):
        k = ref[:, 0:SUB, :].reshape(TOK, HD)
        v = ref[:, SUB : 2 * SUB, :].reshape(TOK, HD)
        k_s[slot] = k
        v_s[slot] = v
        kt_s[slot] = k.T
        vt_s[slot] = v.T

    q = qd_ref[:, 0:128, :].reshape(ROWS, HD)
    d = qd_ref[:, 128:256, :].reshape(ROWS, HD)
    q_s[...] = q
    d_s[...] = d
    qt_s[...] = q.T
    dt_s[...] = d.T
    for dist, (mine, other) in enumerate(((a0, b0), (a1, b1), (a2, b2), (a3, b3))):
        if dist == 0:
            stage(0, mine)
            stage(1, other)
        else:

            @pl.when(chips >= dist)
            def _():
                stage(2 * dist, mine)
                stage(2 * dist + 1, other)

            @pl.when(chips < dist)
            def _():
                near_ref[dist] = jnp.zeros((2, TOK, HD), BF16)
                far_ref[dist] = jnp.zeros((2, TOK, HD), BF16)

    @pl.when(core == 0)
    def _():
        far_ref[0] = jnp.zeros((2, TOK, HD), BF16)

    first = 2 - core
    last = 2 * (chips + 1)

    def fold(x, op):
        parts = x.reshape(TOK // 8, 8, COLS)
        return op(parts, axis=0)

    for c in range(ROWS // COLS):
        at = slice(c * COLS, (c + 1) * COLS)
        s = dot(k_s[0], qt_s[:, at])
        u = lax.broadcasted_iota(jnp.int32, (TOK, COLS), 0)
        t = (lax.broadcasted_iota(jnp.int32, (TOK, COLS), 1) + c * COLS) >> 2
        s = jnp.where(u <= t, s, NEG)
        s_s[0, :, at] = s
        m_s[:, at] = fold(s, jnp.max)

    def scores(b, _):
        for c in range(ROWS // COLS):
            at = slice(c * COLS, (c + 1) * COLS)
            s = dot(k_s[b], qt_s[:, at])
            s_s[b, :, at] = s
            m_s[:, at] = jnp.maximum(m_s[:, at], fold(s, jnp.max))
        return 0

    lax.fori_loop(first, last, scores, 0)
    m_s[...] = jnp.broadcast_to(jnp.max(m_s[...], axis=0, keepdims=True), (8, ROWS))
    l_s[...] = jnp.zeros((8, ROWS), F32)
    ot_s[...] = jnp.zeros((HD, ROWS), F32)

    def forward(b, _):
        for c in range(ROWS // COLS):
            at = slice(c * COLS, (c + 1) * COLS)
            p = jnp.exp2((s_s[b, :, at] - m_s[0:1, at]) * exponent)
            s_s[b, :, at] = p
            l_s[:, at] += fold(p, jnp.sum)
            ot_s[:, at] += dot(vt_s[b], p.astype(BF16))
        return 0

    forward(0, 0)
    lax.fori_loop(first, last, forward, 0)
    inv = 1.0 / jnp.sum(l_s[...], axis=0, keepdims=True)
    out_t = (ot_s[...] * inv).astype(BF16)
    l_s[...] = jnp.broadcast_to(inv, (8, ROWS))
    row_dot = jnp.sum(dt_s[...].astype(F32) * out_t.astype(F32), axis=0, keepdims=True)
    dot_s[...] = jnp.broadcast_to(row_dot, (8, ROWS))
    oq_ref[:, 0:128, :] = out_t.T.reshape(HEADS, 128, HD)
    dqt_s[...] = jnp.zeros((HD, ROWS), F32)

    def backward(b, _):
        dk = jnp.zeros((TOK, HD), F32)
        dv = jnp.zeros((TOK, HD), F32)
        for c in range(ROWS // COLS):
            at = slice(c * COLS, (c + 1) * COLS)
            p = s_s[b, :, at] * l_s[0:1, at]
            dp = dot(v_s[b], dt_s[:, at])
            ds = (p * (dp - dot_s[0:1, at])).astype(BF16)
            dqt_s[:, at] += dot(kt_s[b], ds)
            dk = dk + dot(ds, q_s[at, :])
            dv = dv + dot(p.astype(BF16), d_s[at, :])
        return (dk * scaling).astype(BF16), dv.astype(BF16)

    near_ref[0, 0], near_ref[0, 1] = backward(0, 0)

    @pl.when(core == 1)
    def _():
        far_ref[0, 0], far_ref[0, 1] = backward(1, 0)

    def pair(dist, _):
        near_ref[dist, 0], near_ref[dist, 1] = backward(2 * dist, 0)
        far_ref[dist, 0], far_ref[dist, 1] = backward(2 * dist + 1, 0)
        return 0

    lax.fori_loop(1, chips + 1, pair, 0)
    oq_ref[:, 128:256, :] = (dqt_s[...] * scaling).astype(BF16).T.reshape(HEADS, 128, HD)


def attend(where, qd, mine, other):
    f = pl.pallas_call(
        attend_kernel,
        out_shape=(
            jax.ShapeDtypeStruct((HEADS, 256, HD), BF16),
            jax.ShapeDtypeStruct((4, 2, TOK, HD), BF16),
            jax.ShapeDtypeStruct((4, 2, TOK, HD), BF16),
        ),
        in_specs=[SM] + [VM] * 9,
        out_specs=(VM, VM, VM),
        scratch_shapes=[
            pltpu.VMEM((8, TOK, HD), BF16),
            pltpu.VMEM((8, TOK, HD), BF16),
            pltpu.VMEM((8, HD, TOK), BF16),
            pltpu.VMEM((8, HD, TOK), BF16),
            pltpu.VMEM((ROWS, HD), BF16),
            pltpu.VMEM((ROWS, HD), BF16),
            pltpu.VMEM((HD, ROWS), BF16),
            pltpu.VMEM((HD, ROWS), BF16),
            pltpu.VMEM((8, TOK, ROWS), F32),
            pltpu.VMEM((8, ROWS), F32),
            pltpu.VMEM((8, ROWS), F32),
            pltpu.VMEM((HD, ROWS), F32),
            pltpu.VMEM((HD, ROWS), F32),
            pltpu.VMEM((8, ROWS), F32),
        ],
        compiler_params=params(),
    )
    return f(where, qd, *mine, *other)


def call(kernel, shapes, n_in):
    return pl.pallas_call(
        kernel,
        out_shape=tuple(jax.ShapeDtypeStruct(s, BF16) for s in shapes),
        in_specs=[SM] + [VM] * n_in,
        out_specs=tuple(VM for _ in shapes),
        compiler_params=params(),
    )


def rows_of_groups():
    rows = []
    for start in range(0, 64, 8):
        for core in range(2):
            for place in range(HEADS):
                moved = GROUP // 2 // TOK if place >= HEADS // 2 else 0
                rows.append([(start + moved + 2 * i + core) % 64 * 8 + place for i in range(4)])
    return rows


def local(queries, keys, values, d_attended, shift_amounts):
    seq_pos = lax.axis_index("seq")
    place = lax.axis_index("head")
    in_group = (seq_pos - jnp.where(place >= HEADS // 2, 4, 0)) & 7
    where = jnp.stack((in_group >> 1, in_group & 1)).astype(jnp.int32)
    rows = rows_of_groups()
    swap = [(s * 8 + h, (s ^ 1) * 8 + h) for s in range(64) for h in range(8)]

    (kv,) = call(pack_kv_kernel, [(HEADS, 2 * SUB, HD)], 2)(
        shift_amounts, keys.reshape(TOK, HD), values.reshape(TOK, HD)
    )
    own = lax.all_to_all(kv, "head", 0, 0, tiled=True)
    (qd,) = call(pack_q_kernel, [(HEADS, 256, HD)], 2)(
        shift_amounts, queries.reshape(ROWS, HD), d_attended.reshape(ROWS, HD)
    )
    mine = [own]
    for dist in (1, 2, 3):
        mine.append(lax.ppermute(own, AXES, [(r[i], r[i + dist]) for r in rows for i in range(4 - dist)]))
    qd_here = lax.all_to_all(qd, "head", 0, 0, tiled=True)
    other = [lax.ppermute(x, AXES, swap) for x in mine]
    oq, near, far = attend(where, qd_here, mine, other)
    got = lax.ppermute(far, AXES, swap)
    total = near[0].astype(F32) + got[0].astype(F32)
    for dist in (1, 2, 3):
        part = (near[dist].astype(F32) + got[dist].astype(F32)).astype(BF16)
        back = lax.ppermute(part, AXES, [(r[i + dist], r[i]) for r in rows for i in range(4 - dist)])
        total = total + back.astype(F32)
    oq_back = lax.all_to_all(oq, "head", 0, 0, tiled=True)
    grads = total.astype(BF16).reshape(2, HEADS, SUB, HD).transpose(1, 0, 2, 3).reshape(HEADS, 2 * SUB, HD)
    grads_back = lax.all_to_all(grads, "head", 0, 0, tiled=True)
    attended, d_queries = call(unpack_q_kernel, [(ROWS, HD)] * 2, 1)(shift_amounts, oq_back)
    d_keys, d_values = call(unpack_kv_kernel, [(TOK, HD)] * 2, 1)(shift_amounts, grads_back)
    return (
        attended.reshape(SUB, HEADS, PER, HD),
        d_queries.reshape(SUB, HEADS, PER, HD),
        d_keys.reshape(SUB, HEADS, HD),
        d_values.reshape(SUB, HEADS, HD),
    )


def solution(mesh):
    wide = P(("seq", "head"), None, None, None)
    flat = P(("seq", "head"), None, None)
    return jax.shard_map(
        local,
        mesh=mesh,
        in_specs=(wide, flat, flat, wide, P()),
        out_specs=(wide, wide, flat, flat),
        check_vma=False,
    )
```

time: 258 us -> 103 us (0.40)
  the two profiles are of different devices: /device:TPU:185 before, /device:TPU:184 now
where the time goes in v1:
time: 103 us; the launch traced here: 102 us
  starting transfers between devices  32.8 us (32%)
  waiting for transfers between devices  26.2 us (25%)
  blocking collectives  21.1 us (20%)
  Pallas kernels  18.9 us (18%)
  local copies, waits for them, and re-layouts  2.34 us (2%)
    all_to_all x1, blocking collectives, local(): grads_back = lax.all_to_all(grads, 'head', 0, 0, tiled=True)  21.1 us
    pallas_call x1, Pallas kernels, attend(): return f(where, qd, *mine, *other)  12.5 us
    ppermute x4, starting transfers between devices, local(): other = [lax.ppermute(x, AXES, swap) for x in mine]  8.14 us
    all_to_all x1, waiting for transfers between devices, local(): oq_back = lax.all_to_all(oq, 'head', 0, 0, tiled=True)  6.97 us
    ppermute x3, waiting for transfers between devices, local(): lax.ppermute(part, AXES, [(r[i + dist], r[i]) for r in rows for i in rang...  6.56 us
    all_to_all x1, starting transfers between devices, local(): own = lax.all_to_all(kv, 'head', 0, 0, tiled=True)  6.11 us
    ppermute x3, waiting for transfers between devices, local(): lax.ppermute(own, AXES, [(r[i], r[i + dist]) for r in rows for i in range...  5.5 us
    all_to_all x1, waiting for transfers between devices, local(): own = lax.all_to_all(kv, 'head', 0, 0, tiled=True)  4.78 us
  transfers between devices with their start and end apart: 14, of which 9 were waited for; matrix products, arithmetic and copies ran while one was open for 0% of the time, Pallas kernels for 3%

profile of v1, /device:TPU:184, one launch (start us, length us, event | category | flops | bytes accessed | tf_op | source)
XLA Modules:
  0.0 102.4 jit_solution(16714639469817287404)
XLA Ops:
  0.6 0.6 copy-done.4
  1.3 0.8 copy-done.2
  2.1 0.8 copy-done.3
  3.0 1.4 %shard_map.85 = bf16[8,64,128]{2,1,0:T(8,128)(2,1)} custom-call(s32[8]{0:T(128)S(1)} %copy-done.4, bf16[256,128]{1,0:T(8,128)(2,1)S(1)} %bitcast.30, bf16[256,128]{1,0:T(8,128)(2,1)S(1)} %bitcast.31), custom_call_target="tpu_custom_call" | custom-call | tf_op jit(solution)/shard_map/pallas_call | solution.py:279
  4.4 6.1 %all-to-all-start.1 = ((bf16[8,64,128]{2,1,0:T(8,128)(2,1)}), bf16[8,64,128]{2,1,0:T(8,128)(2,1)S(1)}, u32[]{:S(2)}, u32[]{:S(2)}) async-start(bf16[8,64,128]{2,1,0:T(8,128)(2,1)} %shard_map.85), calls=%async_computation.1 | async-start | bytes 262144 | tf_op jit(solution)/shard_map/all_to_all | solution.py:282
  10.5 1.8 %shard_map.84 = bf16[8,256,128]{2,1,0:T(8,128)(2,1)} custom-call(s32[8]{0:T(128)S(1)} %copy-done.4, bf16[1024,128]{1,0:T(8,128)(2,1)S(1)} %bitcast.28, bf16[1024,128]{1,0:T(8,128)(2,1)S(1)} %bitcast.29), custom_call_target="tpu_custom_call" | custom-call | tf_op jit(solution)/shard_map/pallas_call | solution.py:283
  12.3 4.8 %all-to-all-done.1.a0 = bf16[8,64,128]{2,1,0:T(8,128)(2,1)S(1)} async-done(((bf16[8,64,128]{2,1,0:T(8,128)(2,1)}), bf16[8,64,128]{2,1,0:T(8,128)(2,1)S(1)}, u32[]{:S(2)}, u32[]{:S(2)}) %all-to-all-start.1) | async-done | bytes 131104 | tf_op jit(solution)/shard_map/all_to_all | solution.py:282
  17.1 3.5 %all-to-all-start = ((bf16[8,256,128]{2,1,0:T(8,128)(2,1)}), bf16[8,256,128]{2,1,0:T(8,128)(2,1)S(1)}, u32[]{:S(2)}, u32[]{:S(2)}) async-start(bf16[8,256,128]{2,1,0:T(8,128)(2,1)} %shard_map.84), calls=%async_computation | async-start | bytes 1048576 | tf_op jit(solution)/shard_map/all_to_all | solution.py:289
  20.6 1.3 %collective-permute-start.2 = (bf16[8,64,128]{2,1,0:T(8,128)(2,1)S(1)}, bf16[8,64,128]{2,1,0:T(8,128)(2,1)S(1)}, u32[]{:S(2)}, u32[]{:S(2)}) collective-permute-start(bf16[8,64,128]{2,1,0:T(8,128)(2,1)S(1)} %all-to-all-done.1.a0), channel_id=1, source_target_pairs={{0,48},{1,49},{2,50},{3,51},{36,84},{37,85},{38,86},{39,87},{8,56}... | collective-permute-start | bytes 393224 | tf_op jit(solution)/shard_map/ppermute | solution.py:288
  21.9 1.3 %collective-permute-start.1 = (bf16[8,64,128]{2,1,0:T(8,128)(2,1)S(1)}, bf16[8,64,128]{2,1,0:T(8,128)(2,1)S(1)}, u32[]{:S(2)}, u32[]{:S(2)}) collective-permute-start(bf16[8,64,128]{2,1,0:T(8,128)(2,1)S(1)} %all-to-all-done.1.a0), channel_id=1, source_target_pairs={{0,32},{16,48},{1,33},{17,49},{2,34},{18,50},{3,35},{19,51},{36,68... | collective-permute-start | bytes 393224 | tf_op jit(solution)/shard_map/ppermute | solution.py:288
  23.2 1.3 %collective-permute-start = (bf16[8,64,128]{2,1,0:T(8,128)(2,1)S(1)}, bf16[8,64,128]{2,1,0:T(8,128)(2,1)S(1)}, u32[]{:S(2)}, u32[]{:S(2)}) collective-permute-start(bf16[8,64,128]{2,1,0:T(8,128)(2,1)S(1)} %all-to-all-done.1.a0), channel_id=1, source_target_pairs={{0,16},{16,32},{32,48},{1,17},{17,33},{33,49},{2,18},{18,34},{34,5... | collective-permute-start | bytes 393224 | tf_op jit(solution)/shard_map/ppermute | solution.py:288
  24.5 1.9 %collective-permute-start.3 = (bf16[8,64,128]{2,1,0:T(8,128)(2,1)S(1)}, bf16[8,64,128]{2,1,0:T(8,128)(2,1)S(1)}, u32[]{:S(2)}, u32[]{:S(2)}) collective-permute-start(bf16[8,64,128]{2,1,0:T(8,128)(2,1)S(1)} %all-to-all-done.1.a0), channel_id=1, source_target_pairs={{0,8},{1,9},{2,10},{3,11},{4,12},{5,13},{6,14},{7,15},{8,0},{9,1},... | collective-permute-start | bytes 393224 | tf_op jit(solution)/shard_map/ppermute | solution.py:290
  26.4 4.0 %collective-permute-done.2.a3 = bf16[8,64,128]{2,1,0:T(8,128)(2,1)S(1)} collective-permute-done((bf16[8,64,128]{2,1,0:T(8,128)(2,1)S(1)}, bf16[8,64,128]{2,1,0:T(8,128)(2,1)S(1)}, u32[]{:S(2)}, u32[]{:S(2)}) %collective-permute-start.2) | collective-permute-done | bytes 131104 | tf_op jit(solution)/shard_map/ppermute | solution.py:288
  30.4 1.9 %collective-permute-start.6 = (bf16[8,64,128]{2,1,0:T(8,128)(2,1)S(1)}, bf16[8,64,128]{2,1,0:T(8,128)(2,1)S(1)}, u32[]{:S(2)}, u32[]{:S(2)}) collective-permute-start(bf16[8,64,128]{2,1,0:T(8,128)(2,1)S(1)} %collective-permute-done.2.a3), channel_id=1, source_target_pairs={{0,8},{1,9},{2,10},{3,11},{4,12},{5,13},{6,14},{7,15},{8,0},{9,1},... | collective-permute-start | bytes 393224 | tf_op jit(solution)/shard_map/ppermute | solution.py:290
  32.3 1.5 %collective-permute-done.1.a2 = bf16[8,64,128]{2,1,0:T(8,128)(2,1)S(1)} collective-permute-done((bf16[8,64,128]{2,1,0:T(8,128)(2,1)S(1)}, bf16[8,64,128]{2,1,0:T(8,128)(2,1)S(1)}, u32[]{:S(2)}, u32[]{:S(2)}) %collective-permute-start.1) | collective-permute-done | bytes 131104 | tf_op jit(solution)/shard_map/ppermute | solution.py:288
  33.8 1.9 %collective-permute-start.5 = (bf16[8,64,128]{2,1,0:T(8,128)(2,1)S(1)}, bf16[8,64,128]{2,1,0:T(8,128)(2,1)S(1)}, u32[]{:S(2)}, u32[]{:S(2)}) collective-permute-start(bf16[8,64,128]{2,1,0:T(8,128)(2,1)S(1)} %collective-permute-done.1.a2), channel_id=1, source_target_pairs={{0,8},{1,9},{2,10},{3,11},{4,12},{5,13},{6,14},{7,15},{8,0},{9,1},... | collective-permute-start | bytes 393224 | tf_op jit(solution)/shard_map/ppermute | solution.py:290
  35.8 2.4 %collective-permute-start.4 = (bf16[8,64,128]{2,1,0:T(8,128)(2,1)S(1)}, bf16[8,64,128]{2,1,0:T(8,128)(2,1)S(1)}, u32[]{:S(2)}, u32[]{:S(2)}) collective-permute-start(bf16[8,64,128]{2,1,0:T(8,128)(2,1)S(1)} %collective-permute-done.a1), channel_id=1, source_target_pairs={{0,8},{1,9},{2,10},{3,11},{4,12},{5,13},{6,14},{7,15},{8,0},{9,1},... | collective-permute-start | bytes 393224 | tf_op jit(solution)/shard_map/ppermute | solution.py:290
  38.3 0.9 collective-permute-done.4.b1
  39.1 12.5 %shard_map.86 = (bf16[8,256,128]{2,1,0:T(8,128)(2,1)}, bf16[4,2,256,128]{3,2,1,0:T(8,128)(2,1)S(1)}, bf16[4,2,256,128]{3,2,1,0:T(8,128)(2,1)S(1)}) custom-call(s32[2]{0:T(128)S(1)} %pad_add_fusion.where_ref, bf16[8,256,128]{2,1,0:T(8,128)(2,1)S(1)} %all-to-all-done.qd_ref, bf16[8,64,128]{2,1,0:T(8,128)(2,1)S(1)} %all-to-all-done.1.a0, ...), custom_call_target="tpu_custom_call" | custom-call | tf_op jit(solution)/shard_map/pallas_call | solution.py:248
  51.7 3.8 %collective-permute-start.7 = (bf16[4,2,256,128]{3,2,1,0:T(8,128)(2,1)S(1)}, bf16[4,2,256,128]{3,2,1,0:T(8,128)(2,1)S(1)}, u32[]{:S(2)}, u32[]{:S(2)}) collective-permute-start(bf16[4,2,256,128]{3,2,1,0:T(8,128)(2,1)S(1)} %get-tuple-element.15), channel_id=1, source_target_pairs={{0,8},{1,9},{2,10},{3,11},{4,12},{5,13},{6,14},{7,15},{8,0},{9,1},... | collective-permute-start | bytes 1572872 | tf_op jit(solution)/shard_map/ppermute | solution.py:292
  55.4 1.5 %collective-permute-done.7 = bf16[4,2,256,128]{3,2,1,0:T(8,128)(2,1)S(1)} collective-permute-done((bf16[4,2,256,128]{3,2,1,0:T(8,128)(2,1)S(1)}, bf16[4,2,256,128]{3,2,1,0:T(8,128)(2,1)S(1)}, u32[]{:S(2)}, u32[]{:S(2)}) %collective-permute-start.7) | collective-permute-done | bytes 524320 | tf_op jit(solution)/shard_map/ppermute | solution.py:292
  57.1 1.3 %collective-permute-start.8 = (bf16[2,256,128]{2,1,0:T(8,128)(2,1)S(1)}, bf16[2,256,128]{2,1,0:T(8,128)(2,1)S(1)}, u32[]{:S(2)}, u32[]{:S(2)}) collective-permute-start(bf16[2,256,128]{2,1,0:T(8,128)(2,1)S(1)} %get-tuple-element.18), channel_id=1, source_target_pairs={{16,0},{32,16},{48,32},{17,1},{33,17},{49,33},{18,2},{34,18},{50,3... | collective-permute-start | bytes 393224 | tf_op jit(solution)/shard_map/ppermute | solution.py:296
  58.4 1.3 %collective-permute-start.10 = (bf16[2,256,128]{2,1,0:T(8,128)(2,1)S(1)}, bf16[2,256,128]{2,1,0:T(8,128)(2,1)S(1)}, u32[]{:S(2)}, u32[]{:S(2)}) collective-permute-start(bf16[2,256,128]{2,1,0:T(8,128)(2,1)S(1)} %get-tuple-element.19), channel_id=1, source_target_pairs={{48,0},{49,1},{50,2},{51,3},{84,36},{85,37},{86,38},{87,39},{56,8}... | collective-permute-start | bytes 393224 | tf_op jit(solution)/shard_map/ppermute | solution.py:296
  59.7 1.3 %collective-permute-start.9 = (bf16[2,256,128]{2,1,0:T(8,128)(2,1)S(1)}, bf16[2,256,128]{2,1,0:T(8,128)(2,1)S(1)}, u32[]{:S(2)}, u32[]{:S(2)}) collective-permute-start(bf16[2,256,128]{2,1,0:T(8,128)(2,1)S(1)} %get-tuple-element.20), channel_id=1, source_target_pairs={{32,0},{48,16},{33,1},{49,17},{34,2},{50,18},{35,3},{51,19},{68,36... | collective-permute-start | bytes 393224 | tf_op jit(solution)/shard_map/ppermute | solution.py:296
  61.0 1.3 %collective-permute-done.8 = bf16[2,256,128]{2,1,0:T(8,128)(2,1)S(1)} collective-permute-done((bf16[2,256,128]{2,1,0:T(8,128)(2,1)S(1)}, bf16[2,256,128]{2,1,0:T(8,128)(2,1)S(1)}, u32[]{:S(2)}, u32[]{:S(2)}) %collective-permute-start.8) | collective-permute-done | bytes 131104 | tf_op jit(solution)/shard_map/ppermute | solution.py:296
  62.2 2.8 %collective-permute-done.10 = bf16[2,256,128]{2,1,0:T(8,128)(2,1)S(1)} collective-permute-done((bf16[2,256,128]{2,1,0:T(8,128)(2,1)S(1)}, bf16[2,256,128]{2,1,0:T(8,128)(2,1)S(1)}, u32[]{:S(2)}, u32[]{:S(2)}) %collective-permute-start.10) | collective-permute-done | bytes 131104 | tf_op jit(solution)/shard_map/ppermute | solution.py:296
  65.0 2.5 %collective-permute-done.9 = bf16[2,256,128]{2,1,0:T(8,128)(2,1)S(1)} collective-permute-done((bf16[2,256,128]{2,1,0:T(8,128)(2,1)S(1)}, bf16[2,256,128]{2,1,0:T(8,128)(2,1)S(1)}, u32[]{:S(2)}, u32[]{:S(2)}) %collective-permute-start.9) | collective-permute-done | bytes 131104 | tf_op jit(solution)/shard_map/ppermute | solution.py:296
  67.6 21.1 %all_to_all.20.in_ref = bf16[8,64,128]{2,1,0:T(8,128)(2,1)S(1)} all-to-all(bf16[8,64,128]{2,1,0:T(8,128)(2,1)S(1)} %bitcast.32), channel_id=1, replica_groups=mesh['seq'=64,'head'=8] {'head'}, dimensions={0} | all-to-all | bytes 262144 | tf_op jit(solution)/shard_map/all_to_all | solution.py:300
  88.7 3.5 %all-to-all-start.2 = ((bf16[8,256,128]{2,1,0:T(8,128)(2,1)}), bf16[8,256,128]{2,1,0:T(8,128)(2,1)S(1)}, u32[]{:S(2)}, u32[]{:S(2)}) async-start(bf16[8,256,128]{2,1,0:T(8,128)(2,1)} %get-tuple-element.11), calls=%async_computation.2 | async-start | bytes 1048576 | tf_op jit(solution)/shard_map/all_to_all | solution.py:298
  92.2 1.5 %shard_map.88 = (bf16[256,128]{1,0:T(8,128)(2,1)}, bf16[256,128]{1,0:T(8,128)(2,1)}) custom-call(s32[8]{0:T(128)S(1)} %copy-done.4, bf16[8,64,128]{2,1,0:T(8,128)(2,1)S(1)} %all_to_all.20.in_ref), custom_call_target="tpu_custom_call" | custom-call | tf_op jit(solution)/shard_map/pallas_call | solution.py:302
  93.7 7.0 %all-to-all-done.2.in_ref = bf16[8,256,128]{2,1,0:T(8,128)(2,1)S(1)} async-done(((bf16[8,256,128]{2,1,0:T(8,128)(2,1)}), bf16[8,256,128]{2,1,0:T(8,128)(2,1)S(1)}, u32[]{:S(2)}, u32[]{:S(2)}) %all-to-all-start.2) | async-done | bytes 524320 | tf_op jit(solution)/shard_map/all_to_all | solution.py:298
  100.7 1.7 %shard_map.87 = (bf16[1024,128]{1,0:T(8,128)(2,1)}, bf16[1024,128]{1,0:T(8,128)(2,1)}) custom-call(s32[8]{0:T(128)S(1)} %copy-done.4, bf16[8,256,128]{2,1,0:T(8,128)(2,1)S(1)} %all-to-all-done.2.in_ref), custom_call_target="tpu_custom_call" | custom-call | tf_op jit(solution)/shard_map/pallas_call | solution.py:301
  (16 shorter events, 0.3 us)
Async XLA Ops:
  0.6 0.7 copy-start.4
  1.3 0.8 copy-start.2
  2.1 0.8 copy-start.3
  3.0 7.5 %copy-start = (bf16[32,8,4,128]{3,2,1,0:T(4,128)(2,1)S(1)}, bf16[32,8,4,128]{3,2,1,0:T(4,128)(2,1)}, u32[]{:S(2)}) copy-start(bf16[32,8,4,128]{3,2,1,0:T(4,128)(2,1)} %param.5) | copy-start | bytes 786436
  3.0 7.5 %copy-start.1 = (bf16[32,8,4,128]{3,2,1,0:T(4,128)(2,1)S(1)}, bf16[32,8,4,128]{3,2,1,0:T(4,128)(2,1)}, u32[]{:S(2)}) copy-start(bf16[32,8,4,128]{3,2,1,0:T(4,128)(2,1)} %param.8) | copy-start | bytes 786436
  4.4 12.7 %all-to-all-start.1 = ((bf16[8,64,128]{2,1,0:T(8,128)(2,1)}), bf16[8,64,128]{2,1,0:T(8,128)(2,1)S(1)}, u32[]{:S(2)}, u32[]{:S(2)}) async-start(bf16[8,64,128]{2,1,0:T(8,128)(2,1)} %shard_map.85), calls=%async_computation.1 | async-start | bytes 262144 | tf_op jit(solution)/shard_map/all_to_all | solution.py:282
  17.1 22.1 %all-to-all-start = ((bf16[8,256,128]{2,1,0:T(8,128)(2,1)}), bf16[8,256,128]{2,1,0:T(8,128)(2,1)S(1)}, u32[]{:S(2)}, u32[]{:S(2)}) async-start(bf16[8,256,128]{2,1,0:T(8,128)(2,1)} %shard_map.84), calls=%async_computation | async-start | bytes 1048576 | tf_op jit(solution)/shard_map/all_to_all | solution.py:289
  20.6 9.8 %collective-permute-start.2 = (bf16[8,64,128]{2,1,0:T(8,128)(2,1)S(1)}, bf16[8,64,128]{2,1,0:T(8,128)(2,1)S(1)}, u32[]{:S(2)}, u32[]{:S(2)}) collective-permute-start(bf16[8,64,128]{2,1,0:T(8,128)(2,1)S(1)} %all-to-all-done.1.a0), channel_id=1, source_target_pairs={{0,48},{1,49},{2,50},{3,51},{36,84},{37,85},{38,86},{39,87},{8,56}... | collective-permute-start | bytes 393224 | tf_op jit(solution)/shard_map/ppermute | solution.py:288
  21.9 11.9 %collective-permute-start.1 = (bf16[8,64,128]{2,1,0:T(8,128)(2,1)S(1)}, bf16[8,64,128]{2,1,0:T(8,128)(2,1)S(1)}, u32[]{:S(2)}, u32[]{:S(2)}) collective-permute-start(bf16[8,64,128]{2,1,0:T(8,128)(2,1)S(1)} %all-to-all-done.1.a0), channel_id=1, source_target_pairs={{0,32},{16,48},{1,33},{17,49},{2,34},{18,50},{3,35},{19,51},{36,68... | collective-permute-start | bytes 393224 | tf_op jit(solution)/shard_map/ppermute | solution.py:288
  23.2 12.6 %collective-permute-start = (bf16[8,64,128]{2,1,0:T(8,128)(2,1)S(1)}, bf16[8,64,128]{2,1,0:T(8,128)(2,1)S(1)}, u32[]{:S(2)}, u32[]{:S(2)}) collective-permute-start(bf16[8,64,128]{2,1,0:T(8,128)(2,1)S(1)} %all-to-all-done.1.a0), channel_id=1, source_target_pairs={{0,16},{16,32},{32,48},{1,17},{17,33},{33,49},{2,18},{18,34},{34,5... | collective-permute-start | bytes 393224 | tf_op jit(solution)/shard_map/ppermute | solution.py:288
  24.5 13.8 %collective-permute-start.3 = (bf16[8,64,128]{2,1,0:T(8,128)(2,1)S(1)}, bf16[8,64,128]{2,1,0:T(8,128)(2,1)S(1)}, u32[]{:S(2)}, u32[]{:S(2)}) collective-permute-start(bf16[8,64,128]{2,1,0:T(8,128)(2,1)S(1)} %all-to-all-done.1.a0), channel_id=1, source_target_pairs={{0,8},{1,9},{2,10},{3,11},{4,12},{5,13},{6,14},{7,15},{8,0},{9,1},... | collective-permute-start | bytes 393224 | tf_op jit(solution)/shard_map/ppermute | solution.py:290
  30.4 7.9 %collective-permute-start.6 = (bf16[8,64,128]{2,1,0:T(8,128)(2,1)S(1)}, bf16[8,64,128]{2,1,0:T(8,128)(2,1)S(1)}, u32[]{:S(2)}, u32[]{:S(2)}) collective-permute-start(bf16[8,64,128]{2,1,0:T(8,128)(2,1)S(1)} %collective-permute-done.2.a3), channel_id=1, source_target_pairs={{0,8},{1,9},{2,10},{3,11},{4,12},{5,13},{6,14},{7,15},{8,0},{9,1},... | collective-permute-start | bytes 393224 | tf_op jit(solution)/shard_map/ppermute | solution.py:290
  33.8 4.4 %collective-permute-start.5 = (bf16[8,64,128]{2,1,0:T(8,128)(2,1)S(1)}, bf16[8,64,128]{2,1,0:T(8,128)(2,1)S(1)}, u32[]{:S(2)}, u32[]{:S(2)}) collective-permute-start(bf16[8,64,128]{2,1,0:T(8,128)(2,1)S(1)} %collective-permute-done.1.a2), channel_id=1, source_target_pairs={{0,8},{1,9},{2,10},{3,11},{4,12},{5,13},{6,14},{7,15},{8,0},{9,1},... | collective-permute-start | bytes 393224 | tf_op jit(solution)/shard_map/ppermute | solution.py:290
  35.8 3.4 %collective-permute-start.4 = (bf16[8,64,128]{2,1,0:T(8,128)(2,1)S(1)}, bf16[8,64,128]{2,1,0:T(8,128)(2,1)S(1)}, u32[]{:S(2)}, u32[]{:S(2)}) collective-permute-start(bf16[8,64,128]{2,1,0:T(8,128)(2,1)S(1)} %collective-permute-done.a1), channel_id=1, source_target_pairs={{0,8},{1,9},{2,10},{3,11},{4,12},{5,13},{6,14},{7,15},{8,0},{9,1},... | collective-permute-start | bytes 393224 | tf_op jit(solution)/shard_map/ppermute | solution.py:290
  51.7 5.3 %collective-permute-start.7 = (bf16[4,2,256,128]{3,2,1,0:T(8,128)(2,1)S(1)}, bf16[4,2,256,128]{3,2,1,0:T(8,128)(2,1)S(1)}, u32[]{:S(2)}, u32[]{:S(2)}) collective-permute-start(bf16[4,2,256,128]{3,2,1,0:T(8,128)(2,1)S(1)} %get-tuple-element.15), channel_id=1, source_target_pairs={{0,8},{1,9},{2,10},{3,11},{4,12},{5,13},{6,14},{7,15},{8,0},{9,1},... | collective-permute-start | bytes 1572872 | tf_op jit(solution)/shard_map/ppermute | solution.py:292
  57.1 5.2 %collective-permute-start.8 = (bf16[2,256,128]{2,1,0:T(8,128)(2,1)S(1)}, bf16[2,256,128]{2,1,0:T(8,128)(2,1)S(1)}, u32[]{:S(2)}, u32[]{:S(2)}) collective-permute-start(bf16[2,256,128]{2,1,0:T(8,128)(2,1)S(1)} %get-tuple-element.18), channel_id=1, source_target_pairs={{16,0},{32,16},{48,32},{17,1},{33,17},{49,33},{18,2},{34,18},{50,3... | collective-permute-start | bytes 393224 | tf_op jit(solution)/shard_map/ppermute | solution.py:296
  58.4 6.7 %collective-permute-start.10 = (bf16[2,256,128]{2,1,0:T(8,128)(2,1)S(1)}, bf16[2,256,128]{2,1,0:T(8,128)(2,1)S(1)}, u32[]{:S(2)}, u32[]{:S(2)}) collective-permute-start(bf16[2,256,128]{2,1,0:T(8,128)(2,1)S(1)} %get-tuple-element.19), channel_id=1, source_target_pairs={{48,0},{49,1},{50,2},{51,3},{84,36},{85,37},{86,38},{87,39},{56,8}... | collective-permute-start | bytes 393224 | tf_op jit(solution)/shard_map/ppermute | solution.py:296
  59.7 7.9 %collective-permute-start.9 = (bf16[2,256,128]{2,1,0:T(8,128)(2,1)S(1)}, bf16[2,256,128]{2,1,0:T(8,128)(2,1)S(1)}, u32[]{:S(2)}, u32[]{:S(2)}) collective-permute-start(bf16[2,256,128]{2,1,0:T(8,128)(2,1)S(1)} %get-tuple-element.20), channel_id=1, source_target_pairs={{32,0},{48,16},{33,1},{49,17},{34,2},{50,18},{35,3},{51,19},{68,36... | collective-permute-start | bytes 393224 | tf_op jit(solution)/shard_map/ppermute | solution.py:296
  88.7 11.9 %all-to-all-start.2 = ((bf16[8,256,128]{2,1,0:T(8,128)(2,1)}), bf16[8,256,128]{2,1,0:T(8,128)(2,1)S(1)}, u32[]{:S(2)}, u32[]{:S(2)}) async-start(bf16[8,256,128]{2,1,0:T(8,128)(2,1)} %get-tuple-element.11), calls=%async_computation.2 | async-start | bytes 1048576 | tf_op jit(solution)/shard_map/all_to_all | solution.py:298

commit v2 on v1

v2 whole, which is shorter than its diff:
```python
import math

import jax
import jax.numpy as jnp
from jax import lax
from jax.experimental import pallas as pl
from jax.experimental.pallas import tpu as pltpu
from jax.sharding import PartitionSpec as P

GROUP = 2048
HEADS = 8
PER = 4
HD = 128
TOK = 256
SUB = 32
ROWS = TOK * PER
COLS = 512
QAT = 64
WIDE = 320
LOG2E = 1.4426950408889634
NEG = -1e30
F32 = jnp.float32
BF16 = jnp.bfloat16
VM = pl.BlockSpec(memory_space=pltpu.VMEM)
SM = pl.BlockSpec(memory_space=pltpu.SMEM)
AXES = ("seq", "head")


LONG = pl.CostEstimate(flops=10_000_000_000, bytes_accessed=1 << 20, transcendentals=0)


def params():
    return pltpu.CompilerParams(vmem_limit_bytes=24 * 1024 * 1024)


def dot(a, b):
    return jnp.dot(a, b, preferred_element_type=F32)


def place_of_head(shift_ref, head):
    place = jnp.zeros(head.shape, jnp.int32)
    plain = jnp.int32(0)
    moved = jnp.int32(HEADS // 2)
    for h in range(HEADS):
        is_moved = (shift_ref[h] > 0).astype(jnp.int32)
        rank = jnp.where(is_moved == 1, moved, plain)
        place = jnp.where(head == h, rank, place)
        moved = moved + is_moved
        plain = plain + 1 - is_moved
    return place


def kv_order(shift_ref, back):
    local = lax.broadcasted_iota(jnp.int32, (TOK, TOK), 0 if back else 1)
    placed = lax.broadcasted_iota(jnp.int32, (TOK, TOK), 1 if back else 0)
    head = lax.broadcasted_iota(jnp.int32, (TOK, 1) if back else (1, TOK), 0 if back else 1) & 7
    place = place_of_head(shift_ref, head)
    hit = ((local >> 3) == (placed & 31)) & (place == (placed >> 5))
    return jnp.where(hit, 1.0, 0.0).astype(BF16)


def q_order(shift_ref, back):
    local = lax.broadcasted_iota(jnp.int32, (TOK, TOK), 0 if back else 1)
    placed = lax.broadcasted_iota(jnp.int32, (TOK, TOK), 1 if back else 0)
    head = lax.broadcasted_iota(jnp.int32, (TOK, 1) if back else (1, TOK), 0 if back else 1)
    place = place_of_head(shift_ref, (head >> 2) & 7)
    same = ((local >> 5) == ((placed & 31) >> 2)) & ((local & 3) == (placed & 3))
    return jnp.where(same & (place == (placed >> 5)), 1.0, 0.0).astype(BF16)


def pack_kernel(shift_hbm, k_hbm, v_hbm, q_hbm, d_hbm, out_ref, shift_ref, k_ref, v_ref, q_ref, d_ref, sems):
    copies = [
        pltpu.make_async_copy(src, dst, sems.at[n])
        for n, (src, dst) in enumerate(
            ((shift_hbm, shift_ref), (k_hbm, k_ref), (v_hbm, v_ref), (q_hbm, q_ref), (d_hbm, d_ref))
        )
    ]
    for copy in copies:
        copy.start()
    copies[0].wait()
    order = kv_order(shift_ref, False)
    wide_order = q_order(shift_ref, False)
    for n, ref in enumerate((k_ref, v_ref)):
        copies[n + 1].wait()
        moved = dot(order, ref[...]).astype(BF16)
        for h in range(HEADS):
            out_ref[h, n * SUB : (n + 1) * SUB, :] = moved[h * SUB : (h + 1) * SUB]
    for n, ref in enumerate((q_ref, d_ref)):
        copies[n + 3].wait()
        for b in range(4):
            moved = dot(wide_order, ref[b * TOK : (b + 1) * TOK, :]).astype(BF16)
            for h in range(HEADS):
                at = QAT + n * 128 + b * 32
                out_ref[h, at : at + 32, :] = moved[h * 32 : (h + 1) * 32]


def unpack_kernel(shift_ref, in_ref, o_ref, q_ref, k_ref, v_ref):
    order = kv_order(shift_ref, True)
    wide_order = q_order(shift_ref, True)
    for n, ref in enumerate((k_ref, v_ref)):
        held = in_ref[:, n * SUB : (n + 1) * SUB, :].reshape(TOK, HD)
        ref[...] = dot(order, held).astype(BF16)
    for n, ref in enumerate((o_ref, q_ref)):
        for b in range(4):
            at = QAT + n * 128 + b * 32
            held = in_ref[:, at : at + 32, :].reshape(TOK, HD)
            ref[b * TOK : (b + 1) * TOK, :] = dot(wide_order, held).astype(BF16)


def attend_kernel(
    where_ref, all_ref, b0, a1, a2, a3, b1, b2, b3,
    near_ref, far_ref, ds_ref, ot_ref,
    k_s, v_s, vt_s, q_s, d_s, qt_s, dt_s, s_s, m_s, l_s, ot_s, dot_s,
):
    chips = where_ref[0]
    core = where_ref[1]
    scaling = 1.0 / math.sqrt(HD)
    exponent = scaling * LOG2E

    def stage(slot, ref):
        k = ref[:, 0:SUB, :].reshape(TOK, HD)
        v = ref[:, SUB : 2 * SUB, :].reshape(TOK, HD)
        k_s[slot] = k
        v_s[slot] = v
        vt_s[slot] = v.T

    q = all_ref[:, QAT : QAT + 128, :].reshape(ROWS, HD)
    d = all_ref[:, QAT + 128 : QAT + 256, :].reshape(ROWS, HD)
    q_s[...] = q
    d_s[...] = d
    qt_s[...] = q.T
    dt_s[...] = d.T
    for dist, (mine, other) in enumerate(((all_ref, b0), (a1, b1), (a2, b2), (a3, b3))):
        if dist == 0:
            stage(0, mine)
            stage(1, other)
        else:

            @pl.when(chips >= dist)
            def _():
                stage(2 * dist, mine)
                stage(2 * dist + 1, other)

            @pl.when(chips < dist)
            def _():
                near_ref[dist] = jnp.zeros((HEADS, 2 * SUB, HD), BF16)
                far_ref[dist] = jnp.zeros((HEADS, 2 * SUB, HD), BF16)

    @pl.when(core == 0)
    def _():
        far_ref[0] = jnp.zeros((HEADS, 2 * SUB, HD), BF16)

    first = 2 - core
    last = 2 * (chips + 1)

    def fold(x, op):
        parts = x.reshape(TOK // 8, 8, COLS)
        return op(parts, axis=0)

    for c in range(ROWS // COLS):
        at = slice(c * COLS, (c + 1) * COLS)
        s = dot(k_s[0], qt_s[:, at])
        u = lax.broadcasted_iota(jnp.int32, (TOK, COLS), 0)
        t = (lax.broadcasted_iota(jnp.int32, (TOK, COLS), 1) + c * COLS) >> 2
        s = jnp.where(u <= t, s, NEG)
        s_s[0, :, at] = s
        m_s[:, at] = fold(s, jnp.max)

    def scores(b, _):
        for c in range(ROWS // COLS):
            at = slice(c * COLS, (c + 1) * COLS)
            s = dot(k_s[b], qt_s[:, at])
            s_s[b, :, at] = s
            m_s[:, at] = jnp.maximum(m_s[:, at], fold(s, jnp.max))
        return 0

    lax.fori_loop(first, last, scores, 0)
    m_s[...] = jnp.broadcast_to(jnp.max(m_s[...], axis=0, keepdims=True), (8, ROWS))
    l_s[...] = jnp.zeros((8, ROWS), F32)
    ot_s[...] = jnp.zeros((HD, ROWS), F32)

    def forward(b, _):
        for c in range(ROWS // COLS):
            at = slice(c * COLS, (c + 1) * COLS)
            p = jnp.exp2((s_s[b, :, at] - m_s[0:1, at]) * exponent)
            s_s[b, :, at] = p
            l_s[:, at] += fold(p, jnp.sum)
            ot_s[:, at] += dot(vt_s[b], p.astype(BF16))
        return 0

    forward(0, 0)
    lax.fori_loop(first, last, forward, 0)
    inv = 1.0 / jnp.sum(l_s[...], axis=0, keepdims=True)
    out_t = (ot_s[...] * inv).astype(BF16)
    l_s[...] = jnp.broadcast_to(inv, (8, ROWS))
    row_dot = jnp.sum(dt_s[...].astype(F32) * out_t.astype(F32), axis=0, keepdims=True)
    dot_s[...] = jnp.broadcast_to(row_dot, (8, ROWS))
    ot_ref[...] = out_t

    def backward(b, out_ref, dist):
        dk = jnp.zeros((TOK, HD), F32)
        dv = jnp.zeros((TOK, HD), F32)
        for c in range(ROWS // COLS):
            at = slice(c * COLS, (c + 1) * COLS)
            p = s_s[b, :, at] * l_s[0:1, at]
            dp = dot(v_s[b], dt_s[:, at])
            ds = (p * (dp - dot_s[0:1, at])).astype(BF16)
            ds_ref[b, :, at] = ds
            dk = dk + dot(ds, q_s[at, :])
            dv = dv + dot(p.astype(BF16), d_s[at, :])
        out_ref[dist, :, 0:SUB, :] = (dk * scaling).astype(BF16).reshape(HEADS, SUB, HD)
        out_ref[dist, :, SUB : 2 * SUB, :] = dv.astype(BF16).reshape(HEADS, SUB, HD)

    backward(0, near_ref, 0)

    @pl.when(core == 1)
    def _():
        backward(1, far_ref, 0)

    def pair(dist, _):
        backward(2 * dist, near_ref, dist)
        backward(2 * dist + 1, far_ref, dist)
        return 0

    lax.fori_loop(1, chips + 1, pair, 0)


def query_kernel(where_ref, ot_ref, ds_ref, all_ref, b0, a1, a2, a3, b1, b2, b3, oq_ref, dqt_s):
    chips = where_ref[0]
    core = where_ref[1]
    oq_ref[:, 0:128, :] = ot_ref[...].T.reshape(HEADS, 128, HD)

    def add(slot, ref, first=False):
        kt = ref[:, 0:SUB, :].reshape(TOK, HD).T
        for c in range(ROWS // COLS):
            at = slice(c * COLS, (c + 1) * COLS)
            part = dot(kt, ds_ref[slot, :, at])
            dqt_s[:, at] = part if first else dqt_s[:, at] + part

    add(0, all_ref, True)

    @pl.when(core == 1)
    def _():
        add(1, b0)

    for dist, mine, other in ((1, a1, b1), (2, a2, b2), (3, a3, b3)):

        @pl.when(chips >= dist)
        def _():
            add(2 * dist, mine)
            add(2 * dist + 1, other)

    grad = (dqt_s[...] * (1.0 / math.sqrt(HD))).astype(BF16)
    oq_ref[:, 128:256, :] = grad.T.reshape(HEADS, 128, HD)


def attend(where, *blocks):
    f = pl.pallas_call(
        attend_kernel,
        out_shape=(
            jax.ShapeDtypeStruct((4, HEADS, 2 * SUB, HD), BF16),
            jax.ShapeDtypeStruct((4, HEADS, 2 * SUB, HD), BF16),
            jax.ShapeDtypeStruct((8, TOK, ROWS), BF16),
            jax.ShapeDtypeStruct((HD, ROWS), BF16),
        ),
        in_specs=[SM] + [VM] * 8,
        out_specs=(VM, VM, VM, VM),
        scratch_shapes=[
            pltpu.VMEM((8, TOK, HD), BF16),
            pltpu.VMEM((8, TOK, HD), BF16),
            pltpu.VMEM((8, HD, TOK), BF16),
            pltpu.VMEM((ROWS, HD), BF16),
            pltpu.VMEM((ROWS, HD), BF16),
            pltpu.VMEM((HD, ROWS), BF16),
            pltpu.VMEM((HD, ROWS), BF16),
            pltpu.VMEM((8, TOK, ROWS), F32),
            pltpu.VMEM((8, ROWS), F32),
            pltpu.VMEM((8, ROWS), F32),
            pltpu.VMEM((HD, ROWS), F32),
            pltpu.VMEM((8, ROWS), F32),
        ],
        compiler_params=params(),
    )
    return f(where, *blocks)


def query_side(where, ot, ds, *blocks):
    f = pl.pallas_call(
        query_kernel,
        out_shape=jax.ShapeDtypeStruct((HEADS, 256, HD), BF16),
        in_specs=[SM] + [VM] * 10,
        out_specs=VM,
        scratch_shapes=[pltpu.VMEM((HD, ROWS), F32)],
        compiler_params=params(),
        cost_estimate=LONG,
    )
    return f(where, ot, ds, *blocks)


def shape(*dims):
    return jax.ShapeDtypeStruct(dims, BF16)


def run(kernel, outs, scratch, *operands, cost=None):
    return pl.pallas_call(
        kernel,
        out_shape=outs,
        in_specs=[SM] + [VM] * (len(operands) - 1),
        out_specs=tuple(VM for _ in outs),
        scratch_shapes=scratch,
        compiler_params=params(),
        cost_estimate=cost,
    )(*operands)


def pack(shift, k, v, q, d):
    return pl.pallas_call(
        pack_kernel,
        out_shape=shape(HEADS, WIDE, HD),
        in_specs=[pl.BlockSpec(memory_space=pl.ANY)] * 5,
        out_specs=VM,
        scratch_shapes=[
            pltpu.SMEM((HEADS,), jnp.int32),
            pltpu.VMEM((TOK, HD), BF16),
            pltpu.VMEM((TOK, HD), BF16),
            pltpu.VMEM((ROWS, HD), BF16),
            pltpu.VMEM((ROWS, HD), BF16),
            pltpu.SemaphoreType.DMA((5,)),
        ],
        compiler_params=pltpu.CompilerParams(vmem_limit_bytes=60 * 1024 * 1024),
    )(shift, k, v, q, d)


def rows_of_groups():
    rows = []
    for start in range(0, 64, 8):
        for core in range(2):
            for place in range(HEADS):
                moved = GROUP // 2 // TOK if place >= HEADS // 2 else 0
                rows.append([(start + moved + 2 * i + core) % 64 * 8 + place for i in range(4)])
    return rows


ALONG = rows_of_groups()
SWAP = [(s * 8 + h, (s ^ 1) * 8 + h) for s in range(64) for h in range(8)]


def ahead(x, dist):
    return lax.ppermute(x, AXES, [(r[i], r[i + dist]) for r in ALONG for i in range(4 - dist)])


def behind(x, dist):
    return lax.ppermute(x, AXES, [(r[i + dist], r[i]) for r in ALONG for i in range(4 - dist)])


def summed(near, far, ot):
    got = lax.ppermute(far, AXES, SWAP)
    parts = [(near[dist].astype(F32) + got[dist].astype(F32)).astype(BF16) for dist in (1, 2, 3)]
    total = near[0].astype(F32) + got[0].astype(F32)
    ot, *parts = lax.optimization_barrier((ot, *parts))
    for dist, part in zip((1, 2, 3), parts):
        total = total + behind(part, dist).astype(F32)
    return total.astype(BF16), ot


def local(queries, keys, values, d_attended, shift_amounts):
    seq_pos = lax.axis_index("seq")
    place = lax.axis_index("head")
    in_group = (seq_pos - jnp.where(place >= HEADS // 2, 4, 0)) & 7
    where = jnp.stack((in_group >> 1, in_group & 1)).astype(jnp.int32)
    packed = pack(
        shift_amounts,
        keys.reshape(TOK, HD),
        values.reshape(TOK, HD),
        queries.reshape(ROWS, HD),
        d_attended.reshape(ROWS, HD),
    )
    everything = lax.all_to_all(packed, "head", 0, 0, tiled=True)
    own = everything[:, 0 : 2 * SUB]
    a = [ahead(own, dist) for dist in (1, 2, 3)]
    blocks = [everything, *a] + [lax.ppermute(x, AXES, SWAP) for x in (own, *a)]
    blocks = [blocks[0], blocks[4], *blocks[1:4], *blocks[5:]]
    near, far, ds, ot = attend(where, *blocks)
    grads, ot = summed(near, far, ot)
    oq = query_side(where, ot, ds, *blocks)
    done = lax.all_to_all(jnp.concatenate((grads, oq), axis=1), "head", 0, 0, tiled=True)
    attended, d_queries, d_keys, d_values = run(
        unpack_kernel,
        (shape(ROWS, HD), shape(ROWS, HD), shape(TOK, HD), shape(TOK, HD)),
        [],
        shift_amounts,
        done,
    )
    return (
        attended.reshape(SUB, HEADS, PER, HD),
        d_queries.reshape(SUB, HEADS, PER, HD),
        d_keys.reshape(SUB, HEADS, HD),
        d_values.reshape(SUB, HEADS, HD),
    )


def solution(mesh):
    wide = P(("seq", "head"), None, None, None)
    flat = P(("seq", "head"), None, None)
    return jax.shard_map(
        local,
        mesh=mesh,
        in_specs=(wide, flat, flat, wide, P()),
        out_specs=(wide, wide, flat, flat),
        check_vma=False,
    )
```

time: 103 us -> 94.2 us (0.915)
  the two profiles are of different devices: /device:TPU:184 before, /device:TPU:176 now
where the time goes in v2:
time: 94.2 us; the launch traced here: 93.7 us
  blocking collectives  44.3 us (47%)
  starting transfers between devices  20.1 us (21%)
  waiting for transfers between devices  14.7 us (16%)
  Pallas kernels  13.4 us (14%)
    all_to_all x1, blocking collectives, local(): lax.all_to_all(jnp.concatenate((grads, oq), axis=1), 'head', 0, 0, tiled=...  26.6 us
    all_to_all x1, blocking collectives, local(): everything = lax.all_to_all(packed, 'head', 0, 0, tiled=True)  17.7 us
    ppermute x3, waiting for transfers between devices, behind(): lax.ppermute(x, AXES, [(r[i + dist], r[i]) for r in ALONG for i in range(...  9.45 us
    ppermute x4, starting transfers between devices, local(): blocks = [everything, *a] + [lax.ppermute(x, AXES, SWAP) for x in (own, *a)]  8.14 us
    pallas_call x1, Pallas kernels, attend(): return f(where, *blocks)  7.24 us
    ppermute x3, starting transfers between devices, ahead(): lax.ppermute(x, AXES, [(r[i], r[i + dist]) for r in ALONG for i in range(...  4.55 us
    ppermute x3, starting transfers between devices, behind(): lax.ppermute(x, AXES, [(r[i + dist], r[i]) for r in ALONG for i in range(...  3.89 us
    ppermute x1, starting transfers between devices, summed(): got = lax.ppermute(far, AXES, SWAP)  3.54 us
  transfers between devices with their start and end apart: 11, of which 5 were waited for; matrix products, arithmetic and copies ran while one was open for 0% of the time, Pallas kernels for 2%

profile of v2, /device:TPU:176, one launch (start us, length us, event | category | flops | bytes accessed | tf_op | source)
XLA Modules:
  0.0 93.7 jit_solution(4326758235409924235)
XLA Ops:
  0.6 2.7 %shard_map.84 = bf16[8,320,128]{2,1,0:T(8,128)(2,1)} custom-call(s32[8]{0:T(128)} %shift_ref.1, bf16[256,128]{1,0:T(8,128)(2,1)} %bitcast.26, bf16[256,128]{1,0:T(8,128)(2,1)} %bitcast.27, bf16[1024,128]{1,0:T(8,128)(2,1)} %bitcast.24, bf16[1024,128]{1,0:T(8,128)(2,1)} %bitcast.25), custom_call_target="tpu_custom_call" | custom-call | tf_op jit(solution)/shard_map/pallas_call | solution.py:317
  3.4 17.7 %all_to_all.10.all_ref = bf16[8,320,128]{2,1,0:T(8,128)(2,1)S(1)} all-to-all(bf16[8,320,128]{2,1,0:T(8,128)(2,1)} %shard_map.84), channel_id=1, replica_groups=mesh['seq'=64,'head'=8] {'head'}, dimensions={0} | all-to-all | bytes 1310720 | tf_op jit(solution)/shard_map/all_to_all | solution.py:378
  21.0 2.6 %collective-permute-start.1 = (bf16[8,64,128]{2,1,0:T(8,128)(2,1)S(1)}, bf16[8,64,128]{2,1,0:T(8,128)(2,1)S(1)}, u32[]{:S(2)}, u32[]{:S(2)}) collective-permute-start(bf16[8,64,128]{2,1,0:T(8,128)(2,1)S(1)} %slice.36), channel_id=1, source_target_pairs={{0,16},{16,32},{32,48},{1,17},{17,33},{33,49},{2,18},{18,34},{34,5... | collective-permute-start | bytes 393224 | tf_op jit(solution)/shard_map/ppermute | solution.py:349
  23.6 1.3 %collective-permute-start.2 = (bf16[8,64,128]{2,1,0:T(8,128)(2,1)S(1)}, bf16[8,64,128]{2,1,0:T(8,128)(2,1)S(1)}, u32[]{:S(2)}, u32[]{:S(2)}) collective-permute-start(bf16[8,64,128]{2,1,0:T(8,128)(2,1)S(1)} %slice.36), channel_id=1, source_target_pairs={{0,32},{16,48},{1,33},{17,49},{2,34},{18,50},{3,35},{19,51},{36,68... | collective-permute-start | bytes 393224 | tf_op jit(solution)/shard_map/ppermute | solution.py:349
  24.9 0.7 collective-permute-start.3
  25.6 1.9 %collective-permute-start = (bf16[8,64,128]{2,1,0:T(8,128)(2,1)S(1)}, bf16[8,64,128]{2,1,0:T(8,128)(2,1)S(1)}, u32[]{:S(2)}, u32[]{:S(2)}) collective-permute-start(bf16[8,64,128]{2,1,0:T(8,128)(2,1)S(1)} %slice.36), channel_id=1, source_target_pairs={{0,8},{1,9},{2,10},{3,11},{4,12},{5,13},{6,14},{7,15},{8,0},{9,1},... | collective-permute-start | bytes 393224 | tf_op jit(solution)/shard_map/ppermute | solution.py:381
  27.5 2.0 %collective-permute-done.1.a1 = bf16[8,64,128]{2,1,0:T(8,128)(2,1)S(1)} collective-permute-done((bf16[8,64,128]{2,1,0:T(8,128)(2,1)S(1)}, bf16[8,64,128]{2,1,0:T(8,128)(2,1)S(1)}, u32[]{:S(2)}, u32[]{:S(2)}) %collective-permute-start.1) | collective-permute-done | bytes 131104 | tf_op jit(solution)/shard_map/ppermute | solution.py:349
  29.5 1.9 %collective-permute-start.4 = (bf16[8,64,128]{2,1,0:T(8,128)(2,1)S(1)}, bf16[8,64,128]{2,1,0:T(8,128)(2,1)S(1)}, u32[]{:S(2)}, u32[]{:S(2)}) collective-permute-start(bf16[8,64,128]{2,1,0:T(8,128)(2,1)S(1)} %collective-permute-done.1.a1), channel_id=1, source_target_pairs={{0,8},{1,9},{2,10},{3,11},{4,12},{5,13},{6,14},{7,15},{8,0},{9,1},... | collective-permute-start | bytes 393224 | tf_op jit(solution)/shard_map/ppermute | solution.py:381
  31.4 0.9 collective-permute-done.2.a2
  32.3 1.9 %collective-permute-start.5 = (bf16[8,64,128]{2,1,0:T(8,128)(2,1)S(1)}, bf16[8,64,128]{2,1,0:T(8,128)(2,1)S(1)}, u32[]{:S(2)}, u32[]{:S(2)}) collective-permute-start(bf16[8,64,128]{2,1,0:T(8,128)(2,1)S(1)} %collective-permute-done.2.a2), channel_id=1, source_target_pairs={{0,8},{1,9},{2,10},{3,11},{4,12},{5,13},{6,14},{7,15},{8,0},{9,1},... | collective-permute-start | bytes 393224 | tf_op jit(solution)/shard_map/ppermute | solution.py:381
  34.2 0.0 collective-permute-done.3.a3
  34.3 2.4 %collective-permute-start.6 = (bf16[8,64,128]{2,1,0:T(8,128)(2,1)S(1)}, bf16[8,64,128]{2,1,0:T(8,128)(2,1)S(1)}, u32[]{:S(2)}, u32[]{:S(2)}) collective-permute-start(bf16[8,64,128]{2,1,0:T(8,128)(2,1)S(1)} %collective-permute-done.3.a3), channel_id=1, source_target_pairs={{0,8},{1,9},{2,10},{3,11},{4,12},{5,13},{6,14},{7,15},{8,0},{9,1},... | collective-permute-start | bytes 393224 | tf_op jit(solution)/shard_map/ppermute | solution.py:381
  36.7 0.1 pad_add_fusion.where_ref
  36.8 0.0 collective-permute-done.b0
  36.8 0.0 collective-permute-done.4.b1
  36.8 0.0 collective-permute-done.5.b2
  36.8 0.9 collective-permute-done.6.b3
  37.6 7.2 %shard_map.85 = (bf16[4,8,64,128]{3,2,1,0:T(8,128)(2,1)S(1)}, bf16[4,8,64,128]{3,2,1,0:T(8,128)(2,1)S(1)}, bf16[8,256,1024]{2,1,0:T(8,128)(2,1)S(1)}, bf16[128,1024]{1,0:T(8,128)(2,1)S(1)}) custom-call(s32[2]{0:T(128)S(1)} %pad_add_fusion.where_ref, bf16[8,320,128]{2,1,0:T(8,128)(2,1)S(1)} %all_to_all.10.all_ref, ...), custom_call_target="tpu_custom_call" | custom-call | tf_op jit(solution)/shard_map/pallas_call | solution.py:284
  44.9 3.5 %collective-permute-start.7 = (bf16[4,8,64,128]{3,2,1,0:T(8,128)(2,1)S(1)}, bf16[4,8,64,128]{3,2,1,0:T(8,128)(2,1)S(1)}, u32[]{:S(2)}, u32[]{:S(2)}) collective-permute-start(bf16[4,8,64,128]{3,2,1,0:T(8,128)(2,1)S(1)} %get-tuple-element.17), channel_id=1, source_target_pairs={{0,8},{1,9},{2,10},{3,11},{4,12},{5,13},{6,14},{7,15},{8,0},{9,1},... | collective-permute-start | bytes 1572872 | tf_op jit(solution)/shard_map/ppermute | solution.py:357
  48.4 1.5 %collective-permute-done.7 = bf16[4,8,64,128]{3,2,1,0:T(8,128)(2,1)S(1)} collective-permute-done((bf16[4,8,64,128]{3,2,1,0:T(8,128)(2,1)S(1)}, bf16[4,8,64,128]{3,2,1,0:T(8,128)(2,1)S(1)}, u32[]{:S(2)}, u32[]{:S(2)}) %collective-permute-start.7) | collective-permute-done | bytes 524320 | tf_op jit(solution)/shard_map/ppermute | solution.py:357
  49.9 0.1 fusion.5
  50.1 0.7 collective-permute-start.10
  50.8 1.9 %collective-permute-start.8 = (bf16[8,64,128]{2,1,0:T(8,128)(2,1)S(1)}, bf16[8,64,128]{2,1,0:T(8,128)(2,1)S(1)}, u32[]{:S(2)}, u32[]{:S(2)}) collective-permute-start(bf16[8,64,128]{2,1,0:T(8,128)(2,1)S(1)} %get-tuple-element.19), channel_id=1, source_target_pairs={{16,0},{32,16},{48,32},{17,1},{33,17},{49,33},{18,2},{34,18},{50,3... | collective-permute-start | bytes 393224 | tf_op jit(solution)/shard_map/ppermute | solution.py:353
  52.7 1.3 %collective-permute-start.9 = (bf16[8,64,128]{2,1,0:T(8,128)(2,1)S(1)}, bf16[8,64,128]{2,1,0:T(8,128)(2,1)S(1)}, u32[]{:S(2)}, u32[]{:S(2)}) collective-permute-start(bf16[8,64,128]{2,1,0:T(8,128)(2,1)S(1)} %get-tuple-element.20), channel_id=1, source_target_pairs={{32,0},{48,16},{33,1},{49,17},{34,2},{50,18},{35,3},{51,19},{68,36... | collective-permute-start | bytes 393224 | tf_op jit(solution)/shard_map/ppermute | solution.py:353
  54.0 1.6 %shard_map.86 = bf16[8,256,128]{2,1,0:T(8,128)(2,1)S(1)} custom-call(s32[2]{0:T(128)S(1)} %pad_add_fusion.where_ref, bf16[128,1024]{1,0:T(8,128)(2,1)S(1)} %get-tuple-element.22.ot_ref, bf16[8,256,1024]{2,1,0:T(8,128)(2,1)S(1)} %get-tuple-element.23.ds_ref, bf16[8,320,128]{2,1,0:T(8,128)(2,1)S(1)} %all_to_all.10.all_ref, ...), custom_call_target="tpu_custom_call" | custom-call | flops 10000000000 | bytes 1048576 | tf_op jit(solution)/shard_map/pallas_call | solution.py:297
  55.6 0.0 collective-permute-done.10
  55.6 9.4 %collective-permute-done.8 = bf16[8,64,128]{2,1,0:T(8,128)(2,1)S(1)} collective-permute-done((bf16[8,64,128]{2,1,0:T(8,128)(2,1)S(1)}, bf16[8,64,128]{2,1,0:T(8,128)(2,1)S(1)}, u32[]{:S(2)}, u32[]{:S(2)}) %collective-permute-start.8) | collective-permute-done | bytes 131104 | tf_op jit(solution)/shard_map/ppermute | solution.py:353
  65.1 0.0 collective-permute-done.9
  65.1 0.1 fusion.2
  65.2 0.0 copy-start
  65.2 26.6 %all_to_all.11.in_ref = bf16[8,320,128]{2,1,0:T(8,128)(2,1)S(1)} all-to-all(bf16[8,320,128]{2,1,0:T(8,128)(2,1)S(1)} %pad_maximum_fusion), channel_id=1, replica_groups=mesh['seq'=64,'head'=8] {'head'}, dimensions={0} | all-to-all | bytes 1310720 | tf_op jit(solution)/shard_map/all_to_all | solution.py:386
  91.8 1.9 %shard_map.87 = (bf16[1024,128]{1,0:T(8,128)(2,1)}, bf16[1024,128]{1,0:T(8,128)(2,1)}, bf16[256,128]{1,0:T(8,128)(2,1)}, bf16[256,128]{1,0:T(8,128)(2,1)}) custom-call(s32[8]{0:T(128)S(1)} %copy-done, bf16[8,320,128]{2,1,0:T(8,128)(2,1)S(1)} %all_to_all.11.in_ref), custom_call_target="tpu_custom_call" | custom-call | tf_op jit(solution)/shard_map/pallas_call | solution.py:305
  (3 shorter events, 0.1 us)
Async XLA Ops:
  21.0 8.5 %collective-permute-start.1 = (bf16[8,64,128]{2,1,0:T(8,128)(2,1)S(1)}, bf16[8,64,128]{2,1,0:T(8,128)(2,1)S(1)}, u32[]{:S(2)}, u32[]{:S(2)}) collective-permute-start(bf16[8,64,128]{2,1,0:T(8,128)(2,1)S(1)} %slice.36), channel_id=1, source_target_pairs={{0,16},{16,32},{32,48},{1,17},{17,33},{33,49},{2,18},{18,34},{34,5... | collective-permute-start | bytes 393224 | tf_op jit(solution)/shard_map/ppermute | solution.py:349
  23.6 8.7 %collective-permute-start.2 = (bf16[8,64,128]{2,1,0:T(8,128)(2,1)S(1)}, bf16[8,64,128]{2,1,0:T(8,128)(2,1)S(1)}, u32[]{:S(2)}, u32[]{:S(2)}) collective-permute-start(bf16[8,64,128]{2,1,0:T(8,128)(2,1)S(1)} %slice.36), channel_id=1, source_target_pairs={{0,32},{16,48},{1,33},{17,49},{2,34},{18,50},{3,35},{19,51},{36,68... | collective-permute-start | bytes 393224 | tf_op jit(solution)/shard_map/ppermute | solution.py:349
  24.9 9.3 %collective-permute-start.3 = (bf16[8,64,128]{2,1,0:T(8,128)(2,1)S(1)}, bf16[8,64,128]{2,1,0:T(8,128)(2,1)S(1)}, u32[]{:S(2)}, u32[]{:S(2)}) collective-permute-start(bf16[8,64,128]{2,1,0:T(8,128)(2,1)S(1)} %slice.36), channel_id=1, source_target_pairs={{0,48},{1,49},{2,50},{3,51},{36,84},{37,85},{38,86},{39,87},{8,56}... | collective-permute-start | bytes 393224 | tf_op jit(solution)/shard_map/ppermute | solution.py:349
  25.6 11.2 %collective-permute-start = (bf16[8,64,128]{2,1,0:T(8,128)(2,1)S(1)}, bf16[8,64,128]{2,1,0:T(8,128)(2,1)S(1)}, u32[]{:S(2)}, u32[]{:S(2)}) collective-permute-start(bf16[8,64,128]{2,1,0:T(8,128)(2,1)S(1)} %slice.36), channel_id=1, source_target_pairs={{0,8},{1,9},{2,10},{3,11},{4,12},{5,13},{6,14},{7,15},{8,0},{9,1},... | collective-permute-start | bytes 393224 | tf_op jit(solution)/shard_map/ppermute | solution.py:381
  29.5 7.2 %collective-permute-start.4 = (bf16[8,64,128]{2,1,0:T(8,128)(2,1)S(1)}, bf16[8,64,128]{2,1,0:T(8,128)(2,1)S(1)}, u32[]{:S(2)}, u32[]{:S(2)}) collective-permute-start(bf16[8,64,128]{2,1,0:T(8,128)(2,1)S(1)} %collective-permute-done.1.a1), channel_id=1, source_target_pairs={{0,8},{1,9},{2,10},{3,11},{4,12},{5,13},{6,14},{7,15},{8,0},{9,1},... | collective-permute-start | bytes 393224 | tf_op jit(solution)/shard_map/ppermute | solution.py:381
  32.3 4.4 %collective-permute-start.5 = (bf16[8,64,128]{2,1,0:T(8,128)(2,1)S(1)}, bf16[8,64,128]{2,1,0:T(8,128)(2,1)S(1)}, u32[]{:S(2)}, u32[]{:S(2)}) collective-permute-start(bf16[8,64,128]{2,1,0:T(8,128)(2,1)S(1)} %collective-permute-done.2.a2), channel_id=1, source_target_pairs={{0,8},{1,9},{2,10},{3,11},{4,12},{5,13},{6,14},{7,15},{8,0},{9,1},... | collective-permute-start | bytes 393224 | tf_op jit(solution)/shard_map/ppermute | solution.py:381
  34.3 3.4 %collective-permute-start.6 = (bf16[8,64,128]{2,1,0:T(8,128)(2,1)S(1)}, bf16[8,64,128]{2,1,0:T(8,128)(2,1)S(1)}, u32[]{:S(2)}, u32[]{:S(2)}) collective-permute-start(bf16[8,64,128]{2,1,0:T(8,128)(2,1)S(1)} %collective-permute-done.3.a3), channel_id=1, source_target_pairs={{0,8},{1,9},{2,10},{3,11},{4,12},{5,13},{6,14},{7,15},{8,0},{9,1},... | collective-permute-start | bytes 393224 | tf_op jit(solution)/shard_map/ppermute | solution.py:381
  44.9 5.1 %collective-permute-start.7 = (bf16[4,8,64,128]{3,2,1,0:T(8,128)(2,1)S(1)}, bf16[4,8,64,128]{3,2,1,0:T(8,128)(2,1)S(1)}, u32[]{:S(2)}, u32[]{:S(2)}) collective-permute-start(bf16[4,8,64,128]{3,2,1,0:T(8,128)(2,1)S(1)} %get-tuple-element.17), channel_id=1, source_target_pairs={{0,8},{1,9},{2,10},{3,11},{4,12},{5,13},{6,14},{7,15},{8,0},{9,1},... | collective-permute-start | bytes 1572872 | tf_op jit(solution)/shard_map/ppermute | solution.py:357
  50.1 5.5 %collective-permute-start.10 = (bf16[8,64,128]{2,1,0:T(8,128)(2,1)S(1)}, bf16[8,64,128]{2,1,0:T(8,128)(2,1)S(1)}, u32[]{:S(2)}, u32[]{:S(2)}) collective-permute-start(bf16[8,64,128]{2,1,0:T(8,128)(2,1)S(1)} %get-tuple-element.21), channel_id=1, source_target_pairs={{48,0},{49,1},{50,2},{51,3},{84,36},{85,37},{86,38},{87,39},{56,8}... | collective-permute-start | bytes 393224 | tf_op jit(solution)/shard_map/ppermute | solution.py:353
  50.8 14.3 %collective-permute-start.8 = (bf16[8,64,128]{2,1,0:T(8,128)(2,1)S(1)}, bf16[8,64,128]{2,1,0:T(8,128)(2,1)S(1)}, u32[]{:S(2)}, u32[]{:S(2)}) collective-permute-start(bf16[8,64,128]{2,1,0:T(8,128)(2,1)S(1)} %get-tuple-element.19), channel_id=1, source_target_pairs={{16,0},{32,16},{48,32},{17,1},{33,17},{49,33},{18,2},{34,18},{50,3... | collective-permute-start | bytes 393224 | tf_op jit(solution)/shard_map/ppermute | solution.py:353
  52.7 12.4 %collective-permute-start.9 = (bf16[8,64,128]{2,1,0:T(8,128)(2,1)S(1)}, bf16[8,64,128]{2,1,0:T(8,128)(2,1)S(1)}, u32[]{:S(2)}, u32[]{:S(2)}) collective-permute-start(bf16[8,64,128]{2,1,0:T(8,128)(2,1)S(1)} %get-tuple-element.20), channel_id=1, source_target_pairs={{32,0},{48,16},{33,1},{49,17},{34,2},{50,18},{35,3},{51,19},{68,36... | collective-permute-start | bytes 393224 | tf_op jit(solution)/shard_map/ppermute | solution.py:353
  65.2 26.7 %copy-start = (s32[8]{0:T(128)S(1)}, s32[8]{0:T(128)}, u32[]{:S(2)}) copy-start(s32[8]{0:T(128)} %shift_ref.1) | copy-start | bytes 100

commit v3 on v2

v3 whole, which is shorter than its diff:
```python
import math

import jax
import jax.numpy as jnp
from jax import lax
from jax.experimental import pallas as pl
from jax.experimental.pallas import tpu as pltpu
from jax.sharding import PartitionSpec as P

GROUP = 2048
HEADS = 8
PER = 4
HD = 128
TOK = 256
SUB = 32
ROWS = TOK * PER
COLS = 256
PAIR = 2 * TOK
STAGE_COST = 10_000_000_000
SUM_COST = 10_000_000_000
LOG2E = 1.4426950408889634
NEG = -1e30
F32 = jnp.float32
BF16 = jnp.bfloat16
VM = pl.BlockSpec(memory_space=pltpu.VMEM)
SM = pl.BlockSpec(memory_space=pltpu.SMEM)
AXES = ("seq", "head")


LONG = pl.CostEstimate(flops=10_000_000_000, bytes_accessed=1 << 20, transcendentals=0)


def params():
    return pltpu.CompilerParams(vmem_limit_bytes=24 * 1024 * 1024)


def dot(a, b):
    return jnp.dot(a, b, preferred_element_type=F32)


def place_of_head(shift_ref, head):
    place = jnp.zeros(head.shape, jnp.int32)
    plain = jnp.int32(0)
    moved = jnp.int32(HEADS // 2)
    for h in range(HEADS):
        is_moved = (shift_ref[h] > 0).astype(jnp.int32)
        rank = jnp.where(is_moved == 1, moved, plain)
        place = jnp.where(head == h, rank, place)
        moved = moved + is_moved
        plain = plain + 1 - is_moved
    return place


def kv_order(shift_ref, back):
    local = lax.broadcasted_iota(jnp.int32, (TOK, TOK), 0 if back else 1)
    placed = lax.broadcasted_iota(jnp.int32, (TOK, TOK), 1 if back else 0)
    head = lax.broadcasted_iota(jnp.int32, (TOK, 1) if back else (1, TOK), 0 if back else 1) & 7
    place = place_of_head(shift_ref, head)
    hit = ((local >> 3) == (placed & 31)) & (place == (placed >> 5))
    return jnp.where(hit, 1.0, 0.0).astype(BF16)


def q_order(shift_ref, back):
    local = lax.broadcasted_iota(jnp.int32, (TOK, TOK), 0 if back else 1)
    placed = lax.broadcasted_iota(jnp.int32, (TOK, TOK), 1 if back else 0)
    head = lax.broadcasted_iota(jnp.int32, (TOK, 1) if back else (1, TOK), 0 if back else 1)
    place = place_of_head(shift_ref, (head >> 2) & 7)
    same = ((local >> 5) == ((placed & 31) >> 2)) & ((local & 3) == (placed & 3))
    return jnp.where(same & (place == (placed >> 5)), 1.0, 0.0).astype(BF16)


def pack_kv_kernel(shift_hbm, k_hbm, v_hbm, out_ref, shift_ref, k_ref, v_ref, sems):
    copies = [
        pltpu.make_async_copy(src, dst, sems.at[n])
        for n, (src, dst) in enumerate(((shift_hbm, shift_ref), (k_hbm, k_ref), (v_hbm, v_ref)))
    ]
    for copy in copies:
        copy.start()
    copies[0].wait()
    order = kv_order(shift_ref, False)
    for n, ref in enumerate((k_ref, v_ref)):
        copies[n + 1].wait()
        moved = dot(order, ref[...]).astype(BF16)
        for h in range(HEADS):
            out_ref[h, n * SUB : (n + 1) * SUB, :] = moved[h * SUB : (h + 1) * SUB]


def pack_q_kernel(shift_ref, q_ref, d_ref, out_ref):
    order = q_order(shift_ref, False)
    for n, ref in enumerate((q_ref, d_ref)):
        for b in range(4):
            moved = dot(order, ref[b * TOK : (b + 1) * TOK, :]).astype(BF16)
            for h in range(HEADS):
                at = n * 128 + b * 32
                out_ref[h, at : at + 32, :] = moved[h * 32 : (h + 1) * 32]


def unpack_kv_kernel(shift_ref, in_ref, k_ref, v_ref):
    order = kv_order(shift_ref, True)
    for n, ref in enumerate((k_ref, v_ref)):
        held = in_ref[:, n * SUB : (n + 1) * SUB, :].reshape(TOK, HD)
        ref[...] = dot(order, held).astype(BF16)


def unpack_q_kernel(shift_ref, in_ref, o_ref, q_ref):
    order = q_order(shift_ref, True)
    for n, ref in enumerate((o_ref, q_ref)):
        for b in range(4):
            at = n * 128 + b * 32
            held = in_ref[:, at : at + 32, :].reshape(TOK, HD)
            ref[b * TOK : (b + 1) * TOK, :] = dot(order, held).astype(BF16)


def attend_kernel(
    where_ref, vt0_ref, qd_ref, a0, b0, a1, a2, a3, b1, b2, b3,
    near_ref, far_ref, ds_ref, ot_ref,
    k_s, v_s, vt_s, q_s, d_s, qt_s, dt_s, s_s, m_s, l_s, ot_s, dot_s,
):
    chips = where_ref[0]
    core = where_ref[1]
    scaling = 1.0 / math.sqrt(HD)
    exponent = scaling * LOG2E
    columns = [slice(c * COLS, (c + 1) * COLS) for c in range(ROWS // COLS)]

    def stage(dist, mine, other):
        for half, ref in enumerate((mine, other)):
            at = slice(half * TOK, (half + 1) * TOK)
            v = ref[:, SUB : 2 * SUB, :].reshape(TOK, HD)
            k_s[dist, at, :] = ref[:, 0:SUB, :].reshape(TOK, HD)
            v_s[dist, at, :] = v
            if dist > 0:
                vt_s[dist, :, at] = v.T

    q = qd_ref[:, 0:128, :].reshape(ROWS, HD)
    d = qd_ref[:, 128:256, :].reshape(ROWS, HD)
    q_s[...] = q
    d_s[...] = d
    qt_s[...] = q.T
    dt_s[...] = d.T
    stage(0, a0, b0)
    vt_s[0] = vt0_ref[...]
    for dist, mine, other in ((1, a1, b1), (2, a2, b2), (3, a3, b3)):

        @pl.when(chips >= dist)
        def _():
            stage(dist, mine, other)

        @pl.when(chips < dist)
        def _():
            near_ref[dist] = jnp.zeros((HEADS, 2 * SUB, HD), BF16)
            far_ref[dist] = jnp.zeros((HEADS, 2 * SUB, HD), BF16)

    def fold(x, op):
        return op(x.reshape(PAIR // 8, 8, COLS), axis=0)

    for c, at in enumerate(columns):
        s = dot(k_s[0], qt_s[:, at])
        u = lax.broadcasted_iota(jnp.int32, (PAIR, COLS), 0)
        t = (lax.broadcasted_iota(jnp.int32, (PAIR, COLS), 1) + c * COLS) >> 2
        limit = jnp.where(u < TOK, t, jnp.where(core == 1, PAIR, 0))
        s = jnp.where(u <= limit, s, NEG)
        s_s[0, :, at] = s
        m_s[:, at] = fold(s, jnp.max)

    def scores(b, _):
        for at in columns:
            s = dot(k_s[b], qt_s[:, at])
            s_s[b, :, at] = s
            m_s[:, at] = jnp.maximum(m_s[:, at], fold(s, jnp.max))
        return 0

    lax.fori_loop(1, chips + 1, scores, 0)
    m_s[...] = jnp.broadcast_to(jnp.max(m_s[...], axis=0, keepdims=True), (8, ROWS))
    l_s[...] = jnp.zeros((8, ROWS), F32)
    ot_s[...] = jnp.zeros((HD, ROWS), F32)

    def forward(b, _):
        for at in columns:
            p = jnp.exp2((s_s[b, :, at] - m_s[0:1, at]) * exponent)
            s_s[b, :, at] = p
            l_s[:, at] += fold(p, jnp.sum)
            ot_s[:, at] += dot(vt_s[b], p.astype(BF16))
        return 0

    lax.fori_loop(0, chips + 1, forward, 0)
    inv = 1.0 / jnp.sum(l_s[...], axis=0, keepdims=True)
    out_t = (ot_s[...] * inv).astype(BF16)
    l_s[...] = jnp.broadcast_to(inv, (8, ROWS))
    row_dot = jnp.sum(dt_s[...].astype(F32) * out_t.astype(F32), axis=0, keepdims=True)
    dot_s[...] = jnp.broadcast_to(row_dot, (8, ROWS))
    ot_ref[...] = out_t

    def backward(b, _):
        dk = jnp.zeros((PAIR, HD), F32)
        dv = jnp.zeros((PAIR, HD), F32)
        for at in columns:
            p = s_s[b, :, at] * l_s[0:1, at]
            dp = dot(v_s[b], dt_s[:, at])
            ds = (p * (dp - dot_s[0:1, at])).astype(BF16)
            ds_ref[b, :, at] = ds
            dk = dk + dot(ds, q_s[at, :])
            dv = dv + dot(p.astype(BF16), d_s[at, :])
        dk = (dk * scaling).astype(BF16)
        dv = dv.astype(BF16)
        for half, ref in enumerate((near_ref, far_ref)):
            at = slice(half * TOK, (half + 1) * TOK)
            ref[b, :, 0:SUB, :] = dk[at].reshape(HEADS, SUB, HD)
            ref[b, :, SUB : 2 * SUB, :] = dv[at].reshape(HEADS, SUB, HD)
        return 0

    lax.fori_loop(0, chips + 1, backward, 0)


def query_kernel(where_ref, ot_ref, ds_ref, a0, b0, a1, a2, a3, b1, b2, b3, oq_ref, dqt_s):
    chips = where_ref[0]
    oq_ref[:, 0:128, :] = ot_ref[...].T.reshape(HEADS, 128, HD)

    def add(dist, mine, other):
        kt = [ref[:, 0:SUB, :].reshape(TOK, HD).T for ref in (mine, other)]
        kt = jnp.concatenate(kt, axis=1)
        for c in range(ROWS // COLS):
            at = slice(c * COLS, (c + 1) * COLS)
            part = dot(kt, ds_ref[dist, :, at])
            dqt_s[:, at] = part if dist == 0 else dqt_s[:, at] + part

    add(0, a0, b0)
    for dist, mine, other in ((1, a1, b1), (2, a2, b2), (3, a3, b3)):

        @pl.when(chips >= dist)
        def _():
            add(dist, mine, other)

    grad = (dqt_s[...] * (1.0 / math.sqrt(HD))).astype(BF16)
    oq_ref[:, 128:256, :] = grad.T.reshape(HEADS, 128, HD)


def stage_kernel(a0, b0, vt_ref):
    for half, ref in enumerate((a0, b0)):
        vt_ref[:, half * TOK : (half + 1) * TOK] = ref[:, SUB : 2 * SUB, :].reshape(TOK, HD).T


def sum_kernel(near_ref, got_ref, c1, c2, c3, out_ref):
    total = near_ref[0].astype(F32) + got_ref[0].astype(F32)
    for ref in (c1, c2, c3):
        total = total + ref[...].astype(F32)
    out_ref[...] = total.astype(BF16)


def attend(where, *blocks):
    f = pl.pallas_call(
        attend_kernel,
        out_shape=(
            jax.ShapeDtypeStruct((4, HEADS, 2 * SUB, HD), BF16),
            jax.ShapeDtypeStruct((4, HEADS, 2 * SUB, HD), BF16),
            jax.ShapeDtypeStruct((4, PAIR, ROWS), BF16),
            jax.ShapeDtypeStruct((HD, ROWS), BF16),
        ),
        in_specs=[SM] + [VM] * 10,
        out_specs=(VM, VM, VM, VM),
        scratch_shapes=[
            pltpu.VMEM((4, PAIR, HD), BF16),
            pltpu.VMEM((4, PAIR, HD), BF16),
            pltpu.VMEM((4, HD, PAIR), BF16),
            pltpu.VMEM((ROWS, HD), BF16),
            pltpu.VMEM((ROWS, HD), BF16),
            pltpu.VMEM((HD, ROWS), BF16),
            pltpu.VMEM((HD, ROWS), BF16),
            pltpu.VMEM((4, PAIR, ROWS), F32),
            pltpu.VMEM((8, ROWS), F32),
            pltpu.VMEM((8, ROWS), F32),
            pltpu.VMEM((HD, ROWS), F32),
            pltpu.VMEM((8, ROWS), F32),
        ],
        compiler_params=params(),
    )
    return f(where, *blocks)


def query_side(where, ot, ds, *blocks):
    f = pl.pallas_call(
        query_kernel,
        out_shape=jax.ShapeDtypeStruct((HEADS, 256, HD), BF16),
        in_specs=[SM] + [VM] * 10,
        out_specs=VM,
        scratch_shapes=[pltpu.VMEM((HD, ROWS), F32)],
        compiler_params=params(),
    )
    return f(where, ot, ds, *blocks)


def shape(*dims):
    return jax.ShapeDtypeStruct(dims, BF16)


def cost_of(flops):
    return pl.CostEstimate(flops=flops, bytes_accessed=1 << 18, transcendentals=0)


def run(kernel, outs, *operands, first=VM, cost=None):
    return pl.pallas_call(
        kernel,
        out_shape=outs,
        in_specs=[first] + [VM] * (len(operands) - 1),
        out_specs=tuple(VM for _ in outs),
        compiler_params=params(),
        cost_estimate=cost,
    )(*operands)


def pack_kv(shift, k, v):
    return pl.pallas_call(
        pack_kv_kernel,
        out_shape=jax.ShapeDtypeStruct((HEADS, 2 * SUB, HD), BF16),
        in_specs=[pl.BlockSpec(memory_space=pl.ANY)] * 3,
        out_specs=VM,
        scratch_shapes=[
            pltpu.SMEM((HEADS,), jnp.int32),
            pltpu.VMEM((TOK, HD), BF16),
            pltpu.VMEM((TOK, HD), BF16),
            pltpu.SemaphoreType.DMA((3,)),
        ],
        compiler_params=pltpu.CompilerParams(vmem_limit_bytes=60 * 1024 * 1024),
    )(shift, k, v)


def rows_of_groups():
    rows = []
    for start in range(0, 64, 8):
        for core in range(2):
            for place in range(HEADS):
                moved = GROUP // 2 // TOK if place >= HEADS // 2 else 0
                rows.append([(start + moved + 2 * i + core) % 64 * 8 + place for i in range(4)])
    return rows


ALONG = rows_of_groups()
SWAP = [(s * 8 + h, (s ^ 1) * 8 + h) for s in range(64) for h in range(8)]


def ahead(x, dist):
    return lax.ppermute(x, AXES, [(r[i], r[i + dist]) for r in ALONG for i in range(4 - dist)])


def behind(x, dist):
    return lax.ppermute(x, AXES, [(r[i + dist], r[i]) for r in ALONG for i in range(4 - dist)])


def local(queries, keys, values, d_attended, shift_amounts):
    seq_pos = lax.axis_index("seq")
    place = lax.axis_index("head")
    in_group = (seq_pos - jnp.where(place >= HEADS // 2, 4, 0)) & 7
    where = jnp.stack((in_group >> 1, in_group & 1)).astype(jnp.int32)
    kv = pack_kv(shift_amounts, keys.reshape(TOK, HD), values.reshape(TOK, HD))
    own = lax.all_to_all(kv, "head", 0, 0, tiled=True)
    (qd,) = run(
        pack_q_kernel,
        (shape(HEADS, 256, HD),),
        shift_amounts, queries.reshape(ROWS, HD), d_attended.reshape(ROWS, HD),
        first=SM,
    )
    a = [ahead(own, dist) for dist in (1, 2, 3)]
    qd_here = lax.all_to_all(qd, "head", 0, 0, tiled=True)
    b = [lax.ppermute(x, AXES, SWAP) for x in (own, *a)]
    (vt0,) = run(stage_kernel, (shape(HD, PAIR),), own, b[0], cost=cost_of(STAGE_COST))
    blocks = [own, b[0], *a, *b[1:]]
    near, far, ds, ot = attend(where, vt0, qd_here, *blocks)

    got = lax.ppermute(far, AXES, SWAP)
    parts = [(near[dist].astype(F32) + got[dist].astype(F32)).astype(BF16) for dist in (1, 2, 3)]
    ot, *parts = lax.optimization_barrier((ot, *parts))
    back = [behind(part, dist) for dist, part in zip((1, 2, 3), parts)]
    oq = query_side(where, ot, ds, *blocks)
    oq_back = lax.all_to_all(oq, "head", 0, 0, tiled=True)
    (grads,) = run(sum_kernel, (shape(HEADS, 2 * SUB, HD),), near, got, *back, cost=cost_of(SUM_COST))
    grads, oq_back = lax.optimization_barrier((grads, oq_back))
    grads_back = lax.all_to_all(grads, "head", 0, 0, tiled=True)
    attended, d_queries = run(
        unpack_q_kernel, (shape(ROWS, HD), shape(ROWS, HD)), shift_amounts, oq_back, first=SM
    )
    d_keys, d_values = run(
        unpack_kv_kernel, (shape(TOK, HD), shape(TOK, HD)), shift_amounts, grads_back, first=SM
    )
    return (
        attended.reshape(SUB, HEADS, PER, HD),
        d_queries.reshape(SUB, HEADS, PER, HD),
        d_keys.reshape(SUB, HEADS, HD),
        d_values.reshape(SUB, HEADS, HD),
    )


def solution(mesh):
    wide = P(("seq", "head"), None, None, None)
    flat = P(("seq", "head"), None, None)
    return jax.shard_map(
        local,
        mesh=mesh,
        in_specs=(wide, flat, flat, wide, P()),
        out_specs=(wide, wide, flat, flat),
        check_vma=False,
    )
```

time: 94.2 us -> 92.2 us (0.979)
  the two profiles are of different devices: /device:TPU:176 before, /device:TPU:8 now
where the time goes in v3:
time: 92.2 us; the launch traced here: 91.4 us
  starting transfers between devices  41.6 us (45%)
  waiting for transfers between devices  18.5 us (20%)
  Pallas kernels  14.9 us (16%)
  blocking collectives  12.7 us (14%)
  local copies, waits for them, and re-layouts  2.55 us (3%)
    all_to_all x1, blocking collectives, local(): own = lax.all_to_all(kv, 'head', 0, 0, tiled=True)  12.7 us
    all_to_all x1, starting transfers between devices, local(): oq_back = lax.all_to_all(oq, 'head', 0, 0, tiled=True)  12.6 us
    all_to_all x1, waiting for transfers between devices, local(): oq_back = lax.all_to_all(oq, 'head', 0, 0, tiled=True)  8.81 us
    ppermute x4, starting transfers between devices, local(): b = [lax.ppermute(x, AXES, SWAP) for x in (own, *a)]  8.64 us
    ppermute x3, starting transfers between devices, ahead(): lax.ppermute(x, AXES, [(r[i], r[i + dist]) for r in ALONG for i in range(...  6.45 us
    pallas_call x5, Pallas kernels, run(): pl.pallas_call(kernel, out_shape=outs, in_specs=[first] + [VM] * (len(ope...  5.8 us
    ppermute x3, starting transfers between devices, behind(): lax.ppermute(x, AXES, [(r[i + dist], r[i]) for r in ALONG for i in range(...  5.15 us
    pallas_call x1, Pallas kernels, attend(): return f(where, *blocks)  5.01 us
  transfers between devices with their start and end apart: 14, of which 5 were waited for; matrix products, arithmetic and copies ran while one was open for 0% of the time, Pallas kernels for 7%

profile of v3, /device:TPU:8, one launch (start us, length us, event | category | flops | bytes accessed | tf_op | source)
XLA Modules:
  0.0 91.4 jit_solution(5239988217929553331)
XLA Ops:
  0.6 1.9 %shard_map.84 = bf16[8,64,128]{2,1,0:T(8,128)(2,1)} custom-call(s32[8]{0:T(128)} %shift_ref.5, bf16[256,128]{1,0:T(8,128)(2,1)} %bitcast.18, bf16[256,128]{1,0:T(8,128)(2,1)} %bitcast.19), custom_call_target="tpu_custom_call" | custom-call | tf_op jit(solution)/shard_map/pallas_call | solution.py:311
  2.6 12.7 %all_to_all.20.a0 = bf16[8,64,128]{2,1,0:T(8,128)(2,1)S(1)} all-to-all(bf16[8,64,128]{2,1,0:T(8,128)(2,1)} %shard_map.84), channel_id=1, replica_groups=mesh['seq'=64,'head'=8] {'head'}, dimensions={0} | all-to-all | bytes 262144 | tf_op jit(solution)/shard_map/all_to_all | solution.py:354
  15.3 3.5 %collective-permute-start.1 = (bf16[8,64,128]{2,1,0:T(8,128)(2,1)S(1)}, bf16[8,64,128]{2,1,0:T(8,128)(2,1)S(1)}, u32[]{:S(2)}, u32[]{:S(2)}) collective-permute-start(bf16[8,64,128]{2,1,0:T(8,128)(2,1)S(1)} %all_to_all.20.a0), channel_id=1, source_target_pairs={{0,16},{16,32},{32,48},{1,17},{17,33},{33,49},{2,18},{18,34},{34,5... | collective-permute-start | bytes 393224 | tf_op jit(solution)/shard_map/ppermute | solution.py:341
  18.7 2.3 %collective-permute-start.2 = (bf16[8,64,128]{2,1,0:T(8,128)(2,1)S(1)}, bf16[8,64,128]{2,1,0:T(8,128)(2,1)S(1)}, u32[]{:S(2)}, u32[]{:S(2)}) collective-permute-start(bf16[8,64,128]{2,1,0:T(8,128)(2,1)S(1)} %all_to_all.20.a0), channel_id=1, source_target_pairs={{0,32},{16,48},{1,33},{17,49},{2,34},{18,50},{3,35},{19,51},{36,68... | collective-permute-start | bytes 393224 | tf_op jit(solution)/shard_map/ppermute | solution.py:341
  21.1 0.7 collective-permute-start.3
  21.7 1.9 %collective-permute-start = (bf16[8,64,128]{2,1,0:T(8,128)(2,1)S(1)}, bf16[8,64,128]{2,1,0:T(8,128)(2,1)S(1)}, u32[]{:S(2)}, u32[]{:S(2)}) collective-permute-start(bf16[8,64,128]{2,1,0:T(8,128)(2,1)S(1)} %all_to_all.20.a0), channel_id=1, source_target_pairs={{0,8},{1,9},{2,10},{3,11},{4,12},{5,13},{6,14},{7,15},{8,0},{9,1},... | collective-permute-start | bytes 393224 | tf_op jit(solution)/shard_map/ppermute | solution.py:363
  23.7 0.9 %copy-done = bf16[32,8,4,128]{3,2,1,0:T(4,128)(2,1)S(1)} copy-done((bf16[32,8,4,128]{3,2,1,0:T(4,128)(2,1)S(1)}, bf16[32,8,4,128]{3,2,1,0:T(4,128)(2,1)}, u32[]{:S(2)}) %copy-start) | copy-done | bytes 262168
  24.6 0.9 %copy-done.1 = bf16[32,8,4,128]{3,2,1,0:T(4,128)(2,1)S(1)} copy-done((bf16[32,8,4,128]{3,2,1,0:T(4,128)(2,1)S(1)}, bf16[32,8,4,128]{3,2,1,0:T(4,128)(2,1)}, u32[]{:S(2)}) %copy-start.1) | copy-done | bytes 262168
  25.6 0.7 copy-done.2
  26.2 1.8 %shard_map.86 = bf16[8,256,128]{2,1,0:T(8,128)(2,1)} custom-call(s32[8]{0:T(128)S(1)} %copy-done.2, bf16[1024,128]{1,0:T(8,128)(2,1)S(1)} %bitcast.16, bf16[1024,128]{1,0:T(8,128)(2,1)S(1)} %bitcast.17), custom_call_target="tpu_custom_call" | custom-call | tf_op jit(solution)/shard_map/pallas_call | solution.py:300
  28.0 3.5 %all-to-all-start.1 = ((bf16[8,256,128]{2,1,0:T(8,128)(2,1)}), bf16[8,256,128]{2,1,0:T(8,128)(2,1)S(1)}, u32[]{:S(2)}, u32[]{:S(2)}) async-start(bf16[8,256,128]{2,1,0:T(8,128)(2,1)} %shard_map.86), calls=%async_computation.1 | async-start | bytes 1048576 | tf_op jit(solution)/shard_map/all_to_all | solution.py:362
  31.6 2.4 %collective-permute-start.4 = (bf16[8,64,128]{2,1,0:T(8,128)(2,1)S(1)}, bf16[8,64,128]{2,1,0:T(8,128)(2,1)S(1)}, u32[]{:S(2)}, u32[]{:S(2)}) collective-permute-start(bf16[8,64,128]{2,1,0:T(8,128)(2,1)S(1)} %collective-permute-done.1.a1), channel_id=1, source_target_pairs={{0,8},{1,9},{2,10},{3,11},{4,12},{5,13},{6,14},{7,15},{8,0},{9,1},... | collective-permute-start | bytes 393224 | tf_op jit(solution)/shard_map/ppermute | solution.py:363
  34.0 1.9 %collective-permute-start.5 = (bf16[8,64,128]{2,1,0:T(8,128)(2,1)S(1)}, bf16[8,64,128]{2,1,0:T(8,128)(2,1)S(1)}, u32[]{:S(2)}, u32[]{:S(2)}) collective-permute-start(bf16[8,64,128]{2,1,0:T(8,128)(2,1)S(1)} %collective-permute-done.2.a2), channel_id=1, source_target_pairs={{0,8},{1,9},{2,10},{3,11},{4,12},{5,13},{6,14},{7,15},{8,0},{9,1},... | collective-permute-start | bytes 393224 | tf_op jit(solution)/shard_map/ppermute | solution.py:363
  36.0 2.4 %collective-permute-start.6 = (bf16[8,64,128]{2,1,0:T(8,128)(2,1)S(1)}, bf16[8,64,128]{2,1,0:T(8,128)(2,1)S(1)}, u32[]{:S(2)}, u32[]{:S(2)}) collective-permute-start(bf16[8,64,128]{2,1,0:T(8,128)(2,1)S(1)} %collective-permute-done.3.a3), channel_id=1, source_target_pairs={{0,8},{1,9},{2,10},{3,11},{4,12},{5,13},{6,14},{7,15},{8,0},{9,1},... | collective-permute-start | bytes 393224 | tf_op jit(solution)/shard_map/ppermute | solution.py:363
  38.4 0.1 shard_map.85.vt0_ref
  38.5 0.8 collective-permute-done.6.b3
  39.3 2.2 %all-to-all-done.1.qd_ref = bf16[8,256,128]{2,1,0:T(8,128)(2,1)S(1)} async-done(((bf16[8,256,128]{2,1,0:T(8,128)(2,1)}), bf16[8,256,128]{2,1,0:T(8,128)(2,1)S(1)}, u32[]{:S(2)}, u32[]{:S(2)}) %all-to-all-start.1) | async-done | bytes 524320 | tf_op jit(solution)/shard_map/all_to_all | solution.py:362
  41.5 5.0 %shard_map.87 = (bf16[4,8,64,128]{3,2,1,0:T(8,128)(2,1)S(1)}, bf16[4,8,64,128]{3,2,1,0:T(8,128)(2,1)S(1)}, bf16[4,512,1024]{2,1,0:T(8,128)(2,1)S(1)}, bf16[128,1024]{1,0:T(8,128)(2,1)S(1)}) custom-call(s32[2]{0:T(128)S(1)} %pad_add_fusion.where_ref, bf16[128,512]{1,0:T(8,128)(2,1)S(1)} %shard_map.85.vt0_ref, bf16[8,256,128]{2,1,0:T(8,128)(2,1)S(1)} %all-to-all-done.1.qd_ref, ...), custom_call_target="tpu_custom_call" | custom-call | tf_op jit(solution)/shard_map/pallas_call | solution.py:276
  46.6 1.9 %collective-permute-start.7 = (bf16[4,8,64,128]{3,2,1,0:T(8,128)(2,1)S(1)}, bf16[4,8,64,128]{3,2,1,0:T(8,128)(2,1)S(1)}, u32[]{:S(2)}, u32[]{:S(2)}) collective-permute-start(bf16[4,8,64,128]{3,2,1,0:T(8,128)(2,1)S(1)} %get-tuple-element.19), channel_id=1, source_target_pairs={{0,8},{1,9},{2,10},{3,11},{4,12},{5,13},{6,14},{7,15},{8,0},{9,1},... | collective-permute-start | bytes 1572872 | tf_op jit(solution)/shard_map/ppermute | solution.py:368
  48.5 1.9 %collective-permute-done.7.got_ref = bf16[4,8,64,128]{3,2,1,0:T(8,128)(2,1)S(1)} collective-permute-done((bf16[4,8,64,128]{3,2,1,0:T(8,128)(2,1)S(1)}, bf16[4,8,64,128]{3,2,1,0:T(8,128)(2,1)S(1)}, u32[]{:S(2)}, u32[]{:S(2)}) %collective-permute-start.7) | collective-permute-done | bytes 524320 | tf_op jit(solution)/shard_map/ppermute | solution.py:368
  50.4 0.1 fusion.2
  50.5 3.2 %collective-permute-start.8 = (bf16[8,64,128]{2,1,0:T(8,128)(2,1)S(1)}, bf16[8,64,128]{2,1,0:T(8,128)(2,1)S(1)}, u32[]{:S(2)}, u32[]{:S(2)}) collective-permute-start(bf16[8,64,128]{2,1,0:T(8,128)(2,1)S(1)} %get-tuple-element.21), channel_id=1, source_target_pairs={{16,0},{32,16},{48,32},{17,1},{33,17},{49,33},{18,2},{34,18},{50,3... | collective-permute-start | bytes 393224 | tf_op jit(solution)/shard_map/ppermute | solution.py:345
  53.7 1.3 %collective-permute-start.9 = (bf16[8,64,128]{2,1,0:T(8,128)(2,1)S(1)}, bf16[8,64,128]{2,1,0:T(8,128)(2,1)S(1)}, u32[]{:S(2)}, u32[]{:S(2)}) collective-permute-start(bf16[8,64,128]{2,1,0:T(8,128)(2,1)S(1)} %get-tuple-element.22), channel_id=1, source_target_pairs={{32,0},{48,16},{33,1},{49,17},{34,2},{50,18},{35,3},{51,19},{68,36... | collective-permute-start | bytes 393224 | tf_op jit(solution)/shard_map/ppermute | solution.py:345
  55.0 0.7 collective-permute-start.10
  55.7 2.1 %shard_map.89 = bf16[8,256,128]{2,1,0:T(8,128)(2,1)} custom-call(s32[2]{0:T(128)S(1)} %pad_add_fusion.where_ref, bf16[128,1024]{1,0:T(8,128)(2,1)S(1)} %get-tuple-element.24.ot_ref, bf16[4,512,1024]{2,1,0:T(8,128)(2,1)S(1)} %get-tuple-element.25.ds_ref, bf16[8,64,128]{2,1,0:T(8,128)(2,1)S(1)} %all_to_all.20.a0, ...), custom_call_target="tpu_custom_call" | custom-call | tf_op jit(solution)/shard_map/pallas_call | solution.py:288
  57.8 12.6 %all-to-all-start.2 = ((bf16[8,256,128]{2,1,0:T(8,128)(2,1)}), bf16[8,256,128]{2,1,0:T(8,128)(2,1)S(1)}, u32[]{:S(2)}, u32[]{:S(2)}) async-start(bf16[8,256,128]{2,1,0:T(8,128)(2,1)} %shard_map.89), calls=%async_computation.2 | async-start | bytes 1048576 | tf_op jit(solution)/shard_map/all_to_all | solution.py:373
  70.5 0.7 shard_map.88
  71.2 8.8 %all-to-all-done.2.in_ref = bf16[8,256,128]{2,1,0:T(8,128)(2,1)S(1)} async-done(((bf16[8,256,128]{2,1,0:T(8,128)(2,1)}), bf16[8,256,128]{2,1,0:T(8,128)(2,1)S(1)}, u32[]{:S(2)}, u32[]{:S(2)}) %all-to-all-start.2) | async-done | bytes 524320 | tf_op jit(solution)/shard_map/all_to_all | solution.py:373
  80.0 3.4 %all-to-all-start.3 = ((bf16[8,64,128]{2,1,0:T(8,128)(2,1)}), bf16[8,64,128]{2,1,0:T(8,128)(2,1)S(1)}, u32[]{:S(2)}, u32[]{:S(2)}) async-start(bf16[8,64,128]{2,1,0:T(8,128)(2,1)} %shard_map.88), calls=%async_computation.3 | async-start | bytes 262144 | tf_op jit(solution)/shard_map/all_to_all | solution.py:376
  83.4 1.7 %shard_map.90 = (bf16[1024,128]{1,0:T(8,128)(2,1)}, bf16[1024,128]{1,0:T(8,128)(2,1)}) custom-call(s32[8]{0:T(128)S(1)} %copy-done.3, bf16[8,256,128]{2,1,0:T(8,128)(2,1)S(1)} %all-to-all-done.2.in_ref), custom_call_target="tpu_custom_call" | custom-call | tf_op jit(solution)/shard_map/pallas_call | solution.py:300
  85.1 4.8 %all-to-all-done.3.in_ref = bf16[8,64,128]{2,1,0:T(8,128)(2,1)S(1)} async-done(((bf16[8,64,128]{2,1,0:T(8,128)(2,1)}), bf16[8,64,128]{2,1,0:T(8,128)(2,1)S(1)}, u32[]{:S(2)}, u32[]{:S(2)}) %all-to-all-start.3) | async-done | bytes 131104 | tf_op jit(solution)/shard_map/all_to_all | solution.py:376
  89.9 1.4 %shard_map.91 = (bf16[256,128]{1,0:T(8,128)(2,1)}, bf16[256,128]{1,0:T(8,128)(2,1)}) custom-call(s32[8]{0:T(128)S(1)} %copy-done.3, bf16[8,64,128]{2,1,0:T(8,128)(2,1)S(1)} %all-to-all-done.3.in_ref), custom_call_target="tpu_custom_call" | custom-call | tf_op jit(solution)/shard_map/pallas_call | solution.py:300
  (15 shorter events, 0.1 us)
Async XLA Ops:
  15.3 16.3 %collective-permute-start.1 = (bf16[8,64,128]{2,1,0:T(8,128)(2,1)S(1)}, bf16[8,64,128]{2,1,0:T(8,128)(2,1)S(1)}, u32[]{:S(2)}, u32[]{:S(2)}) collective-permute-start(bf16[8,64,128]{2,1,0:T(8,128)(2,1)S(1)} %all_to_all.20.a0), channel_id=1, source_target_pairs={{0,16},{16,32},{32,48},{1,17},{17,33},{33,49},{2,18},{18,34},{34,5... | collective-permute-start | bytes 393224 | tf_op jit(solution)/shard_map/ppermute | solution.py:341
  18.7 15.3 %collective-permute-start.2 = (bf16[8,64,128]{2,1,0:T(8,128)(2,1)S(1)}, bf16[8,64,128]{2,1,0:T(8,128)(2,1)S(1)}, u32[]{:S(2)}, u32[]{:S(2)}) collective-permute-start(bf16[8,64,128]{2,1,0:T(8,128)(2,1)S(1)} %all_to_all.20.a0), channel_id=1, source_target_pairs={{0,32},{16,48},{1,33},{17,49},{2,34},{18,50},{3,35},{19,51},{36,68... | collective-permute-start | bytes 393224 | tf_op jit(solution)/shard_map/ppermute | solution.py:341
  21.1 14.9 %collective-permute-start.3 = (bf16[8,64,128]{2,1,0:T(8,128)(2,1)S(1)}, bf16[8,64,128]{2,1,0:T(8,128)(2,1)S(1)}, u32[]{:S(2)}, u32[]{:S(2)}) collective-permute-start(bf16[8,64,128]{2,1,0:T(8,128)(2,1)S(1)} %all_to_all.20.a0), channel_id=1, source_target_pairs={{0,48},{1,49},{2,50},{3,51},{36,84},{37,85},{38,86},{39,87},{8,56}... | collective-permute-start | bytes 393224 | tf_op jit(solution)/shard_map/ppermute | solution.py:341
  21.7 16.6 %collective-permute-start = (bf16[8,64,128]{2,1,0:T(8,128)(2,1)S(1)}, bf16[8,64,128]{2,1,0:T(8,128)(2,1)S(1)}, u32[]{:S(2)}, u32[]{:S(2)}) collective-permute-start(bf16[8,64,128]{2,1,0:T(8,128)(2,1)S(1)} %all_to_all.20.a0), channel_id=1, source_target_pairs={{0,8},{1,9},{2,10},{3,11},{4,12},{5,13},{6,14},{7,15},{8,0},{9,1},... | collective-permute-start | bytes 393224 | tf_op jit(solution)/shard_map/ppermute | solution.py:363
  23.7 1.0 %copy-start = (bf16[32,8,4,128]{3,2,1,0:T(4,128)(2,1)S(1)}, bf16[32,8,4,128]{3,2,1,0:T(4,128)(2,1)}, u32[]{:S(2)}) copy-start(bf16[32,8,4,128]{3,2,1,0:T(4,128)(2,1)} %param.5) | copy-start | bytes 786436
  24.6 0.9 %copy-start.1 = (bf16[32,8,4,128]{3,2,1,0:T(4,128)(2,1)S(1)}, bf16[32,8,4,128]{3,2,1,0:T(4,128)(2,1)}, u32[]{:S(2)}) copy-start(bf16[32,8,4,128]{3,2,1,0:T(4,128)(2,1)} %param.8) | copy-start | bytes 786436
  25.6 0.7 copy-start.2
  28.0 13.5 %all-to-all-start.1 = ((bf16[8,256,128]{2,1,0:T(8,128)(2,1)}), bf16[8,256,128]{2,1,0:T(8,128)(2,1)S(1)}, u32[]{:S(2)}, u32[]{:S(2)}) async-start(bf16[8,256,128]{2,1,0:T(8,128)(2,1)} %shard_map.86), calls=%async_computation.1 | async-start | bytes 1048576 | tf_op jit(solution)/shard_map/all_to_all | solution.py:362
  31.6 6.9 %collective-permute-start.4 = (bf16[8,64,128]{2,1,0:T(8,128)(2,1)S(1)}, bf16[8,64,128]{2,1,0:T(8,128)(2,1)S(1)}, u32[]{:S(2)}, u32[]{:S(2)}) collective-permute-start(bf16[8,64,128]{2,1,0:T(8,128)(2,1)S(1)} %collective-permute-done.1.a1), channel_id=1, source_target_pairs={{0,8},{1,9},{2,10},{3,11},{4,12},{5,13},{6,14},{7,15},{8,0},{9,1},... | collective-permute-start | bytes 393224 | tf_op jit(solution)/shard_map/ppermute | solution.py:363
  34.0 4.5 %collective-permute-start.5 = (bf16[8,64,128]{2,1,0:T(8,128)(2,1)S(1)}, bf16[8,64,128]{2,1,0:T(8,128)(2,1)S(1)}, u32[]{:S(2)}, u32[]{:S(2)}) collective-permute-start(bf16[8,64,128]{2,1,0:T(8,128)(2,1)S(1)} %collective-permute-done.2.a2), channel_id=1, source_target_pairs={{0,8},{1,9},{2,10},{3,11},{4,12},{5,13},{6,14},{7,15},{8,0},{9,1},... | collective-permute-start | bytes 393224 | tf_op jit(solution)/shard_map/ppermute | solution.py:363
  36.0 3.4 %collective-permute-start.6 = (bf16[8,64,128]{2,1,0:T(8,128)(2,1)S(1)}, bf16[8,64,128]{2,1,0:T(8,128)(2,1)S(1)}, u32[]{:S(2)}, u32[]{:S(2)}) collective-permute-start(bf16[8,64,128]{2,1,0:T(8,128)(2,1)S(1)} %collective-permute-done.3.a3), channel_id=1, source_target_pairs={{0,8},{1,9},{2,10},{3,11},{4,12},{5,13},{6,14},{7,15},{8,0},{9,1},... | collective-permute-start | bytes 393224 | tf_op jit(solution)/shard_map/ppermute | solution.py:363
  46.6 3.8 %collective-permute-start.7 = (bf16[4,8,64,128]{3,2,1,0:T(8,128)(2,1)S(1)}, bf16[4,8,64,128]{3,2,1,0:T(8,128)(2,1)S(1)}, u32[]{:S(2)}, u32[]{:S(2)}) collective-permute-start(bf16[4,8,64,128]{3,2,1,0:T(8,128)(2,1)S(1)} %get-tuple-element.19), channel_id=1, source_target_pairs={{0,8},{1,9},{2,10},{3,11},{4,12},{5,13},{6,14},{7,15},{8,0},{9,1},... | collective-permute-start | bytes 1572872 | tf_op jit(solution)/shard_map/ppermute | solution.py:368
  50.5 19.9 %collective-permute-start.8 = (bf16[8,64,128]{2,1,0:T(8,128)(2,1)S(1)}, bf16[8,64,128]{2,1,0:T(8,128)(2,1)S(1)}, u32[]{:S(2)}, u32[]{:S(2)}) collective-permute-start(bf16[8,64,128]{2,1,0:T(8,128)(2,1)S(1)} %get-tuple-element.21), channel_id=1, source_target_pairs={{16,0},{32,16},{48,32},{17,1},{33,17},{49,33},{18,2},{34,18},{50,3... | collective-permute-start | bytes 393224 | tf_op jit(solution)/shard_map/ppermute | solution.py:345
  53.7 16.7 %collective-permute-start.9 = (bf16[8,64,128]{2,1,0:T(8,128)(2,1)S(1)}, bf16[8,64,128]{2,1,0:T(8,128)(2,1)S(1)}, u32[]{:S(2)}, u32[]{:S(2)}) collective-permute-start(bf16[8,64,128]{2,1,0:T(8,128)(2,1)S(1)} %get-tuple-element.22), channel_id=1, source_target_pairs={{32,0},{48,16},{33,1},{49,17},{34,2},{50,18},{35,3},{51,19},{68,36... | collective-permute-start | bytes 393224 | tf_op jit(solution)/shard_map/ppermute | solution.py:345
  55.0 15.5 %collective-permute-start.10 = (bf16[8,64,128]{2,1,0:T(8,128)(2,1)S(1)}, bf16[8,64,128]{2,1,0:T(8,128)(2,1)S(1)}, u32[]{:S(2)}, u32[]{:S(2)}) collective-permute-start(bf16[8,64,128]{2,1,0:T(8,128)(2,1)S(1)} %get-tuple-element.23), channel_id=1, source_target_pairs={{48,0},{49,1},{50,2},{51,3},{84,36},{85,37},{86,38},{87,39},{56,8}... | collective-permute-start | bytes 393224 | tf_op jit(solution)/shard_map/ppermute | solution.py:345
  57.8 22.2 %all-to-all-start.2 = ((bf16[8,256,128]{2,1,0:T(8,128)(2,1)}), bf16[8,256,128]{2,1,0:T(8,128)(2,1)S(1)}, u32[]{:S(2)}, u32[]{:S(2)}) async-start(bf16[8,256,128]{2,1,0:T(8,128)(2,1)} %shard_map.89), calls=%async_computation.2 | async-start | bytes 1048576 | tf_op jit(solution)/shard_map/all_to_all | solution.py:373
  70.4 13.0 %copy-start.3 = (s32[8]{0:T(128)S(1)}, s32[8]{0:T(128)}, u32[]{:S(2)}) copy-start(s32[8]{0:T(128)} %shift_ref.5) | copy-start | bytes 100
  80.0 9.9 %all-to-all-start.3 = ((bf16[8,64,128]{2,1,0:T(8,128)(2,1)}), bf16[8,64,128]{2,1,0:T(8,128)(2,1)S(1)}, u32[]{:S(2)}, u32[]{:S(2)}) async-start(bf16[8,64,128]{2,1,0:T(8,128)(2,1)} %shard_map.88), calls=%async_computation.3 | async-start | bytes 262144 | tf_op jit(solution)/shard_map/all_to_all | solution.py:376

commit v4 on v3

--- a/solution.py
+++ b/solution.py
@@ -16,8 +16,8 @@
 ROWS = TOK * PER
 COLS = 256
 PAIR = 2 * TOK
-STAGE_COST = 10_000_000_000
-SUM_COST = 10_000_000_000
+QAT = 64
+WIDE = 320
 LOG2E = 1.4426950408889634
 NEG = -1e30
 F32 = jnp.float32
@@ -69,50 +69,47 @@
     return jnp.where(same & (place == (placed >> 5)), 1.0, 0.0).astype(BF16)
 
 
-def pack_kv_kernel(shift_hbm, k_hbm, v_hbm, out_ref, shift_ref, k_ref, v_ref, sems):
+def pack_kernel(shift_hbm, k_hbm, v_hbm, q_hbm, d_hbm, out_ref, shift_ref, k_ref, v_ref, q_ref, d_ref, sems):
     copies = [
         pltpu.make_async_copy(src, dst, sems.at[n])
-        for n, (src, dst) in enumerate(((shift_hbm, shift_ref), (k_hbm, k_ref), (v_hbm, v_ref)))
+        for n, (src, dst) in enumerate(
+            ((shift_hbm, shift_ref), (k_hbm, k_ref), (v_hbm, v_ref), (q_hbm, q_ref), (d_hbm, d_ref))
+        )
     ]
     for copy in copies:
         copy.start()
     copies[0].wait()
     order = kv_order(shift_ref, False)
+    wide_order = q_order(shift_ref, False)
     for n, ref in enumerate((k_ref, v_ref)):
         copies[n + 1].wait()
         moved = dot(order, ref[...]).astype(BF16)
         for h in range(HEADS):
             out_ref[h, n * SUB : (n + 1) * SUB, :] = moved[h * SUB : (h + 1) * SUB]
-
-
-def pack_q_kernel(shift_ref, q_ref, d_ref, out_ref):
-    order = q_order(shift_ref, False)
     for n, ref in enumerate((q_ref, d_ref)):
+        copies[n + 3].wait()
         for b in range(4):
-            moved = dot(order, ref[b * TOK : (b + 1) * TOK, :]).astype(BF16)
+            moved = dot(wide_order, ref[b * TOK : (b + 1) * TOK, :]).astype(BF16)
             for h in range(HEADS):
-                at = n * 128 + b * 32
+                at = QAT + n * 128 + b * 32
                 out_ref[h, at : at + 32, :] = moved[h * 32 : (h + 1) * 32]
 
 
-def unpack_kv_kernel(shift_ref, in_ref, k_ref, v_ref):
+def unpack_kernel(shift_ref, in_ref, o_ref, q_ref, k_ref, v_ref):
     order = kv_order(shift_ref, True)
+    wide_order = q_order(shift_ref, True)
     for n, ref in enumerate((k_ref, v_ref)):
         held = in_ref[:, n * SUB : (n + 1) * SUB, :].reshape(TOK, HD)
         ref[...] = dot(order, held).astype(BF16)
-
-
-def unpack_q_kernel(shift_ref, in_ref, o_ref, q_ref):
-    order = q_order(shift_ref, True)
     for n, ref in enumerate((o_ref, q_ref)):
         for b in range(4):
-            at = n * 128 + b * 32
+            at = QAT + n * 128 + b * 32
             held = in_ref[:, at : at + 32, :].reshape(TOK, HD)
-            ref[b * TOK : (b + 1) * TOK, :] = dot(order, held).astype(BF16)
+            ref[b * TOK : (b + 1) * TOK, :] = dot(wide_order, held).astype(BF16)
 
 
 def attend_kernel(
-    where_ref, vt0_ref, qd_ref, a0, b0, a1, a2, a3, b1, b2, b3,
+    where_ref, all_ref, b0, a1, b1, a23, b23,
     near_ref, far_ref, ds_ref, ot_ref,
     k_s, v_s, vt_s, q_s, d_s, qt_s, dt_s, s_s, m_s, l_s, ot_s, dot_s,
 ):
@@ -128,18 +125,16 @@
             v = ref[:, SUB : 2 * SUB, :].reshape(TOK, HD)
             k_s[dist, at, :] = ref[:, 0:SUB, :].reshape(TOK, HD)
             v_s[dist, at, :] = v
-            if dist > 0:
-                vt_s[dist, :, at] = v.T
-
-    q = qd_ref[:, 0:128, :].reshape(ROWS, HD)
-    d = qd_ref[:, 128:256, :].reshape(ROWS, HD)
+            vt_s[dist, :, at] = v.T
+
+    q = all_ref[:, QAT : QAT + 128, :].reshape(ROWS, HD)
+    d = all_ref[:, QAT + 128 : QAT + 256, :].reshape(ROWS, HD)
     q_s[...] = q
     d_s[...] = d
     qt_s[...] = q.T
     dt_s[...] = d.T
-    stage(0, a0, b0)
-    vt_s[0] = vt0_ref[...]
-    for dist, mine, other in ((1, a1, b1), (2, a2, b2), (3, a3, b3)):
+    stage(0, all_ref, b0)
+    for dist, mine, other in ((1, a1, b1), (2, a23.at[0], b23.at[0]), (3, a23.at[1], b23.at[1])):
 
         @pl.when(chips >= dist)
         def _():
@@ -211,7 +206,7 @@
     lax.fori_loop(0, chips + 1, backward, 0)
 
 
-def query_kernel(where_ref, ot_ref, ds_ref, a0, b0, a1, a2, a3, b1, b2, b3, oq_ref, dqt_s):
+def query_kernel(where_ref, ot_ref, ds_ref, all_ref, b0, a1, b1, a23, b23, oq_ref, dqt_s):
     chips = where_ref[0]
     oq_ref[:, 0:128, :] = ot_ref[...].T.reshape(HEADS, 128, HD)
 
@@ -223,8 +218,8 @@
             part = dot(kt, ds_ref[dist, :, at])
             dqt_s[:, at] = part if dist == 0 else dqt_s[:, at] + part
 
-    add(0, a0, b0)
-    for dist, mine, other in ((1, a1, b1), (2, a2, b2), (3, a3, b3)):
+    add(0, all_ref, b0)
+    for dist, mine, other in ((1, a1, b1), (2, a23.at[0], b23.at[0]), (3, a23.at[1], b23.at[1])):
 
         @pl.when(chips >= dist)
         def _():
@@ -232,18 +227,6 @@
 
     grad = (dqt_s[...] * (1.0 / math.sqrt(HD))).astype(BF16)
     oq_ref[:, 128:256, :] = grad.T.reshape(HEADS, 128, HD)
-
-
-def stage_kernel(a0, b0, vt_ref):
-    for half, ref in enumerate((a0, b0)):
-        vt_ref[:, half * TOK : (half + 1) * TOK] = ref[:, SUB : 2 * SUB, :].reshape(TOK, HD).T
-
-
-def sum_kernel(near_ref, got_ref, c1, c2, c3, out_ref):
-    total = near_ref[0].astype(F32) + got_ref[0].astype(F32)
-    for ref in (c1, c2, c3):
-        total = total + ref[...].astype(F32)
-    out_ref[...] = total.astype(BF16)
 
 
 def attend(where, *blocks):
@@ -255,7 +238,7 @@
             jax.ShapeDtypeStruct((4, PAIR, ROWS), BF16),
             jax.ShapeDtypeStruct((HD, ROWS), BF16),
         ),
-        in_specs=[SM] + [VM] * 10,
+        in_specs=[SM] + [VM] * 6,
         out_specs=(VM, VM, VM, VM),
         scratch_shapes=[
             pltpu.VMEM((4, PAIR, HD), BF16),
@@ -280,10 +263,11 @@
     f = pl.pallas_call(
         query_kernel,
         out_shape=jax.ShapeDtypeStruct((HEADS, 256, HD), BF16),
-        in_specs=[SM] + [VM] * 10,
+        in_specs=[SM] + [VM] * 8,
         out_specs=VM,
         scratch_shapes=[pltpu.VMEM((HD, ROWS), F32)],
         compiler_params=params(),
+        cost_estimate=LONG,
     )
     return f(where, ot, ds, *blocks)
 
@@ -292,35 +276,34 @@
     return jax.ShapeDtypeStruct(dims, BF16)
 
 
-def cost_of(flops):
-    return pl.CostEstimate(flops=flops, bytes_accessed=1 << 18, transcendentals=0)
-
-
-def run(kernel, outs, *operands, first=VM, cost=None):
+def run(kernel, outs, scratch, *operands, cost=None):
     return pl.pallas_call(
         kernel,
         out_shape=outs,
-        in_specs=[first] + [VM] * (len(operands) - 1),
+        in_specs=[SM] + [VM] * (len(operands) - 1),
         out_specs=tuple(VM for _ in outs),
+        scratch_shapes=scratch,
         compiler_params=params(),
         cost_estimate=cost,
     )(*operands)
 
 
-def pack_kv(shift, k, v):
+def pack(shift, k, v, q, d):
     return pl.pallas_call(
-        pack_kv_kernel,
-        out_shape=jax.ShapeDtypeStruct((HEADS, 2 * SUB, HD), BF16),
-        in_specs=[pl.BlockSpec(memory_space=pl.ANY)] * 3,
+        pack_kernel,
+        out_shape=shape(HEADS, WIDE, HD),
+        in_specs=[pl.BlockSpec(memory_space=pl.ANY)] * 5,
         out_specs=VM,
         scratch_shapes=[
             pltpu.SMEM((HEADS,), jnp.int32),
             pltpu.VMEM((TOK, HD), BF16),
             pltpu.VMEM((TOK, HD), BF16),
-            pltpu.SemaphoreType.DMA((3,)),
+            pltpu.VMEM((ROWS, HD), BF16),
+            pltpu.VMEM((ROWS, HD), BF16),
+            pltpu.SemaphoreType.DMA((5,)),
         ],
         compiler_params=pltpu.CompilerParams(vmem_limit_bytes=60 * 1024 * 1024),
-    )(shift, k, v)
+    )(shift, k, v, q, d)
 
 
 def rows_of_groups():
@@ -345,40 +328,44 @@
     return lax.ppermute(x, AXES, [(r[i + dist], r[i]) for r in ALONG for i in range(4 - dist)])
 
 
+def summed(near, far, ot):
+    got = lax.ppermute(far, AXES, SWAP)
+    parts = [(near[dist].astype(F32) + got[dist].astype(F32)).astype(BF16) for dist in (1, 2, 3)]
+    total = near[0].astype(F32) + got[0].astype(F32)
+    ot, *parts = lax.optimization_barrier((ot, *parts))
+    for dist, part in zip((1, 2, 3), parts):
+        total = total + behind(part, dist).astype(F32)
+    return total.astype(BF16), ot
+
+
 def local(queries, keys, values, d_attended, shift_amounts):
     seq_pos = lax.axis_index("seq")
     place = lax.axis_index("head")
     in_group = (seq_pos - jnp.where(place >= HEADS // 2, 4, 0)) & 7
     where = jnp.stack((in_group >> 1, in_group & 1)).astype(jnp.int32)
-    kv = pack_kv(shift_amounts, keys.reshape(TOK, HD), values.reshape(TOK, HD))
-    own = lax.all_to_all(kv, "head", 0, 0, tiled=True)
-    (qd,) = run(
-        pack_q_kernel,
-        (shape(HEADS, 256, HD),),
-        shift_amounts, queries.reshape(ROWS, HD), d_attended.reshape(ROWS, HD),
-        first=SM,
-    )
-    a = [ahead(own, dist) for dist in (1, 2, 3)]
-    qd_here = lax.all_to_all(qd, "head", 0, 0, tiled=True)
-    b = [lax.ppermute(x, AXES, SWAP) for x in (own, *a)]
-    (vt0,) = run(stage_kernel, (shape(HD, PAIR),), own, b[0], cost=cost_of(STAGE_COST))
-    blocks = [own, b[0], *a, *b[1:]]
-    near, far, ds, ot = attend(where, vt0, qd_here, *blocks)
-
-    got = lax.ppermute(far, AXES, SWAP)
-    parts = [(near[dist].astype(F32) + got[dist].astype(F32)).astype(BF16) for dist in (1, 2, 3)]
-    ot, *parts = lax.optimization_barrier((ot, *parts))
-    back = [behind(part, dist) for dist, part in zip((1, 2, 3), parts)]
+    packed = pack(
+        shift_amounts,
+        keys.reshape(TOK, HD),
+        values.reshape(TOK, HD),
+        queries.reshape(ROWS, HD),
+        d_attended.reshape(ROWS, HD),
+    )
+    everything = lax.all_to_all(packed, "head", 0, 0, tiled=True)
+    own = everything[:, 0 : 2 * SUB]
+    a1, a2, a3 = (ahead(own, dist) for dist in (1, 2, 3))
+    a23 = jnp.stack((a2, a3))
+    b0, b1, b23 = (lax.ppermute(x, AXES, SWAP) for x in (own, a1, a23))
+    blocks = (everything, b0, a1, b1, a23, b23)
+    near, far, ds, ot = attend(where, *blocks)
+    grads, ot = summed(near, far, ot)
     oq = query_side(where, ot, ds, *blocks)
-    oq_back = lax.all_to_all(oq, "head", 0, 0, tiled=True)
-    (grads,) = run(sum_kernel, (shape(HEADS, 2 * SUB, HD),), near, got, *back, cost=cost_of(SUM_COST))
-    grads, oq_back = lax.optimization_barrier((grads, oq_back))
-    grads_back = lax.all_to_all(grads, "head", 0, 0, tiled=True)
-    attended, d_queries = run(
-        unpack_q_kernel, (shape(ROWS, HD), shape(ROWS, HD)), shift_amounts, oq_back, first=SM
-    )
-    d_keys, d_values = run(
-        unpack_kv_kernel, (shape(TOK, HD), shape(TOK, HD)), shift_amounts, grads_back, first=SM
+    done = lax.all_to_all(jnp.concatenate((grads, oq), axis=1), "head", 0, 0, tiled=True)
+    attended, d_queries, d_keys, d_values = run(
+        unpack_kernel,
+        (shape(ROWS, HD), shape(ROWS, HD), shape(TOK, HD), shape(TOK, HD)),
+        [],
+        shift_amounts,
+        done,
     )
     return (
         attended.reshape(SUB, HEADS, PER, HD),

time: 92.2 us -> 91 us (0.987)
  the two profiles are of different devices: /device:TPU:8 before, /device:TPU:176 now
where the time goes in v4:
time: 91 us; the launch traced here: 90.6 us
  blocking collectives  45.5 us (50%)
  starting transfers between devices  17.4 us (19%)
  Pallas kernels  13.3 us (15%)
  waiting for transfers between devices  13.2 us (15%)
    all_to_all x1, blocking collectives, local(): lax.all_to_all(jnp.concatenate((grads, oq), axis=1), 'head', 0, 0, tiled=...  27.8 us
    all_to_all x1, blocking collectives, local(): everything = lax.all_to_all(packed, 'head', 0, 0, tiled=True)  17.7 us
    pallas_call x1, Pallas kernels, attend(): return f(where, *blocks)  7.05 us
    ppermute x3, starting transfers between devices, local(): b0, b1, b23 = (lax.ppermute(x, AXES, SWAP) for x in (own, a1, a23))  6.24 us
    ppermute x3, waiting for transfers between devices, behind(): lax.ppermute(x, AXES, [(r[i + dist], r[i]) for r in ALONG for i in range(...  5.92 us
    ppermute x3, starting transfers between devices, ahead(): lax.ppermute(x, AXES, [(r[i], r[i + dist]) for r in ALONG for i in range(...  5.17 us
    ppermute x3, waiting for transfers between devices, ahead(): lax.ppermute(x, AXES, [(r[i], r[i + dist]) for r in ALONG for i in range(...  4.31 us
    ppermute x3, starting transfers between devices, behind(): lax.ppermute(x, AXES, [(r[i + dist], r[i]) for r in ALONG for i in range(...  3.95 us
  transfers between devices with their start and end apart: 10, of which 5 were waited for; matrix products, arithmetic and copies ran while one was open for 0% of the time, Pallas kernels for 2%

profile of v4, /device:TPU:176, one launch (start us, length us, event | category | flops | bytes accessed | tf_op | source)
XLA Modules:
  0.0 90.6 jit_solution(34876953877888859)
XLA Ops:
  0.6 2.7 %shard_map.84 = bf16[8,320,128]{2,1,0:T(8,128)(2,1)} custom-call(s32[8]{0:T(128)} %shift_ref.1, bf16[256,128]{1,0:T(8,128)(2,1)} %bitcast.30, bf16[256,128]{1,0:T(8,128)(2,1)} %bitcast.31, bf16[1024,128]{1,0:T(8,128)(2,1)} %bitcast.26, bf16[1024,128]{1,0:T(8,128)(2,1)} %bitcast.27), custom_call_target="tpu_custom_call" | custom-call | tf_op jit(solution)/shard_map/pallas_call | solution.py:292
  3.4 17.7 %all_to_all.10.all_ref = bf16[8,320,128]{2,1,0:T(8,128)(2,1)S(1)} all-to-all(bf16[8,320,128]{2,1,0:T(8,128)(2,1)} %shard_map.84), channel_id=1, replica_groups=mesh['seq'=64,'head'=8] {'head'}, dimensions={0} | all-to-all | bytes 1310720 | tf_op jit(solution)/shard_map/all_to_all | solution.py:353
  21.0 1.3 %collective-permute-start.3 = (bf16[8,64,128]{2,1,0:T(8,128)(2,1)S(1)}, bf16[8,64,128]{2,1,0:T(8,128)(2,1)S(1)}, u32[]{:S(2)}, u32[]{:S(2)}) collective-permute-start(bf16[8,64,128]{2,1,0:T(8,128)(2,1)S(1)} %slice.36), channel_id=1, source_target_pairs={{0,32},{16,48},{1,33},{17,49},{2,34},{18,50},{3,35},{19,51},{36,68... | collective-permute-start | bytes 393224 | tf_op jit(solution)/shard_map/ppermute | solution.py:324
  22.3 0.7 collective-permute-start.4
  23.0 3.2 %collective-permute-start.1 = (bf16[8,64,128]{2,1,0:T(8,128)(2,1)S(1)}, bf16[8,64,128]{2,1,0:T(8,128)(2,1)S(1)}, u32[]{:S(2)}, u32[]{:S(2)}) collective-permute-start(bf16[8,64,128]{2,1,0:T(8,128)(2,1)S(1)} %slice.36), channel_id=1, source_target_pairs={{0,16},{16,32},{32,48},{1,17},{17,33},{33,49},{2,18},{18,34},{34,5... | collective-permute-start | bytes 393224 | tf_op jit(solution)/shard_map/ppermute | solution.py:324
  26.2 3.9 %collective-permute-done.3 = bf16[8,64,128]{2,1,0:T(8,128)(2,1)S(1)} collective-permute-done((bf16[8,64,128]{2,1,0:T(8,128)(2,1)S(1)}, bf16[8,64,128]{2,1,0:T(8,128)(2,1)S(1)}, u32[]{:S(2)}, u32[]{:S(2)}) %collective-permute-start.3) | collective-permute-done | bytes 131104 | tf_op jit(solution)/shard_map/ppermute | solution.py:324
  30.2 0.0 collective-permute-done.4
  30.2 1.9 %collective-permute-start.5 = (bf16[2,8,64,128]{3,2,1,0:T(8,128)(2,1)S(1)}, bf16[2,8,64,128]{3,2,1,0:T(8,128)(2,1)S(1)}, u32[]{:S(2)}, u32[]{:S(2)}) collective-permute-start(bf16[2,8,64,128]{3,2,1,0:T(8,128)(2,1)S(1)} %pad_maximum_fusion.1.a23), channel_id=1, source_target_pairs={{0,8},{1,9},{2,10},{3,11},{4,12},{5,13},{6,14},{7,15},{8,0},{9,1},... | collective-permute-start | bytes 786440 | tf_op jit(solution)/shard_map/ppermute | solution.py:357
  32.1 2.4 %collective-permute-start = (bf16[8,64,128]{2,1,0:T(8,128)(2,1)S(1)}, bf16[8,64,128]{2,1,0:T(8,128)(2,1)S(1)}, u32[]{:S(2)}, u32[]{:S(2)}) collective-permute-start(bf16[8,64,128]{2,1,0:T(8,128)(2,1)S(1)} %slice.36), channel_id=1, source_target_pairs={{0,8},{1,9},{2,10},{3,11},{4,12},{5,13},{6,14},{7,15},{8,0},{9,1},... | collective-permute-start | bytes 393224 | tf_op jit(solution)/shard_map/ppermute | solution.py:357
  34.5 0.4 collective-permute-done.1.a1
  34.9 1.9 %collective-permute-start.2 = (bf16[8,64,128]{2,1,0:T(8,128)(2,1)S(1)}, bf16[8,64,128]{2,1,0:T(8,128)(2,1)S(1)}, u32[]{:S(2)}, u32[]{:S(2)}) collective-permute-start(bf16[8,64,128]{2,1,0:T(8,128)(2,1)S(1)} %collective-permute-done.1.a1), channel_id=1, source_target_pairs={{0,8},{1,9},{2,10},{3,11},{4,12},{5,13},{6,14},{7,15},{8,0},{9,1},... | collective-permute-start | bytes 393224 | tf_op jit(solution)/shard_map/ppermute | solution.py:357
  36.8 0.1 pad_add_fusion.where_ref
  36.9 0.0 collective-permute-done.b0
  36.9 1.2 %collective-permute-done.2.b1 = bf16[8,64,128]{2,1,0:T(8,128)(2,1)S(1)} collective-permute-done((bf16[8,64,128]{2,1,0:T(8,128)(2,1)S(1)}, bf16[8,64,128]{2,1,0:T(8,128)(2,1)S(1)}, u32[]{:S(2)}, u32[]{:S(2)}) %collective-permute-start.2) | collective-permute-done | bytes 131104 | tf_op jit(solution)/shard_map/ppermute | solution.py:357
  38.1 0.0 collective-permute-done.5.b23
  38.1 7.0 %shard_map.85 = (bf16[4,8,64,128]{3,2,1,0:T(8,128)(2,1)S(1)}, bf16[4,8,64,128]{3,2,1,0:T(8,128)(2,1)S(1)}, bf16[4,512,1024]{2,1,0:T(8,128)(2,1)S(1)}, bf16[128,1024]{1,0:T(8,128)(2,1)S(1)}) custom-call(s32[2]{0:T(128)S(1)} %pad_add_fusion.where_ref, bf16[8,320,128]{2,1,0:T(8,128)(2,1)S(1)} %all_to_all.10.all_ref, ...), custom_call_target="tpu_custom_call" | custom-call | tf_op jit(solution)/shard_map/pallas_call | solution.py:259
  45.2 2.1 %collective-permute-start.6 = (bf16[4,8,64,128]{3,2,1,0:T(8,128)(2,1)S(1)}, bf16[4,8,64,128]{3,2,1,0:T(8,128)(2,1)S(1)}, u32[]{:S(2)}, u32[]{:S(2)}) collective-permute-start(bf16[4,8,64,128]{3,2,1,0:T(8,128)(2,1)S(1)} %get-tuple-element.17), channel_id=1, source_target_pairs={{0,8},{1,9},{2,10},{3,11},{4,12},{5,13},{6,14},{7,15},{8,0},{9,1},... | collective-permute-start | bytes 1572872 | tf_op jit(solution)/shard_map/ppermute | solution.py:332
  47.3 1.7 %collective-permute-done.6 = bf16[4,8,64,128]{3,2,1,0:T(8,128)(2,1)S(1)} collective-permute-done((bf16[4,8,64,128]{3,2,1,0:T(8,128)(2,1)S(1)}, bf16[4,8,64,128]{3,2,1,0:T(8,128)(2,1)S(1)}, u32[]{:S(2)}, u32[]{:S(2)}) %collective-permute-start.6) | collective-permute-done | bytes 524320 | tf_op jit(solution)/shard_map/ppermute | solution.py:332
  49.0 0.1 fusion.5
  49.1 2.0 %collective-permute-start.7 = (bf16[8,64,128]{2,1,0:T(8,128)(2,1)S(1)}, bf16[8,64,128]{2,1,0:T(8,128)(2,1)S(1)}, u32[]{:S(2)}, u32[]{:S(2)}) collective-permute-start(bf16[8,64,128]{2,1,0:T(8,128)(2,1)S(1)} %get-tuple-element.19), channel_id=1, source_target_pairs={{16,0},{32,16},{48,32},{17,1},{33,17},{49,33},{18,2},{34,18},{50,3... | collective-permute-start | bytes 393224 | tf_op jit(solution)/shard_map/ppermute | solution.py:328
  51.1 1.3 %collective-permute-start.8 = (bf16[8,64,128]{2,1,0:T(8,128)(2,1)S(1)}, bf16[8,64,128]{2,1,0:T(8,128)(2,1)S(1)}, u32[]{:S(2)}, u32[]{:S(2)}) collective-permute-start(bf16[8,64,128]{2,1,0:T(8,128)(2,1)S(1)} %get-tuple-element.20), channel_id=1, source_target_pairs={{32,0},{48,16},{33,1},{49,17},{34,2},{50,18},{35,3},{51,19},{68,36... | collective-permute-start | bytes 393224 | tf_op jit(solution)/shard_map/ppermute | solution.py:328
  52.4 0.7 collective-permute-start.9
  53.1 1.6 %shard_map.86 = bf16[8,256,128]{2,1,0:T(8,128)(2,1)S(1)} custom-call(s32[2]{0:T(128)S(1)} %pad_add_fusion.where_ref, bf16[128,1024]{1,0:T(8,128)(2,1)S(1)} %get-tuple-element.22.ot_ref, bf16[4,512,1024]{2,1,0:T(8,128)(2,1)S(1)} %get-tuple-element.23.ds_ref, bf16[8,320,128]{2,1,0:T(8,128)(2,1)S(1)} %all_to_all.10.all_ref, ...), custom_call_target="tpu_custom_call" | custom-call | flops 10000000000 | bytes 1048576 | tf_op jit(solution)/shard_map/pallas_call | solution.py:272
  54.7 5.9 %collective-permute-done.7 = bf16[8,64,128]{2,1,0:T(8,128)(2,1)S(1)} collective-permute-done((bf16[8,64,128]{2,1,0:T(8,128)(2,1)S(1)}, bf16[8,64,128]{2,1,0:T(8,128)(2,1)S(1)}, u32[]{:S(2)}, u32[]{:S(2)}) %collective-permute-start.7) | collective-permute-done | bytes 131104 | tf_op jit(solution)/shard_map/ppermute | solution.py:328
  60.7 0.0 collective-permute-done.8
  60.7 0.0 collective-permute-done.9
  60.7 0.1 fusion.2
  60.8 0.0 copy-start
  60.8 27.8 %all_to_all.11.in_ref = bf16[8,320,128]{2,1,0:T(8,128)(2,1)S(1)} all-to-all(bf16[8,320,128]{2,1,0:T(8,128)(2,1)S(1)} %pad_maximum_fusion), channel_id=1, replica_groups=mesh['seq'=64,'head'=8] {'head'}, dimensions={0} | all-to-all | bytes 1310720 | tf_op jit(solution)/shard_map/all_to_all | solution.py:362
  88.7 0.0 copy-done
  88.7 1.9 %shard_map.87 = (bf16[1024,128]{1,0:T(8,128)(2,1)}, bf16[1024,128]{1,0:T(8,128)(2,1)}, bf16[256,128]{1,0:T(8,128)(2,1)}, bf16[256,128]{1,0:T(8,128)(2,1)}) custom-call(s32[8]{0:T(128)S(1)} %copy-done, bf16[8,320,128]{2,1,0:T(8,128)(2,1)S(1)} %all_to_all.11.in_ref), custom_call_target="tpu_custom_call" | custom-call | tf_op jit(solution)/shard_map/pallas_call | solution.py:280
  (3 shorter events, 0.1 us)
Async XLA Ops:
  21.0 9.1 %collective-permute-start.3 = (bf16[8,64,128]{2,1,0:T(8,128)(2,1)S(1)}, bf16[8,64,128]{2,1,0:T(8,128)(2,1)S(1)}, u32[]{:S(2)}, u32[]{:S(2)}) collective-permute-start(bf16[8,64,128]{2,1,0:T(8,128)(2,1)S(1)} %slice.36), channel_id=1, source_target_pairs={{0,32},{16,48},{1,33},{17,49},{2,34},{18,50},{3,35},{19,51},{36,68... | collective-permute-start | bytes 393224 | tf_op jit(solution)/shard_map/ppermute | solution.py:324
  22.3 7.8 %collective-permute-start.4 = (bf16[8,64,128]{2,1,0:T(8,128)(2,1)S(1)}, bf16[8,64,128]{2,1,0:T(8,128)(2,1)S(1)}, u32[]{:S(2)}, u32[]{:S(2)}) collective-permute-start(bf16[8,64,128]{2,1,0:T(8,128)(2,1)S(1)} %slice.36), channel_id=1, source_target_pairs={{0,48},{1,49},{2,50},{3,51},{36,84},{37,85},{38,86},{39,87},{8,56}... | collective-permute-start | bytes 393224 | tf_op jit(solution)/shard_map/ppermute | solution.py:324
  23.0 11.9 %collective-permute-start.1 = (bf16[8,64,128]{2,1,0:T(8,128)(2,1)S(1)}, bf16[8,64,128]{2,1,0:T(8,128)(2,1)S(1)}, u32[]{:S(2)}, u32[]{:S(2)}) collective-permute-start(bf16[8,64,128]{2,1,0:T(8,128)(2,1)S(1)} %slice.36), channel_id=1, source_target_pairs={{0,16},{16,32},{32,48},{1,17},{17,33},{33,49},{2,18},{18,34},{34,5... | collective-permute-start | bytes 393224 | tf_op jit(solution)/shard_map/ppermute | solution.py:324
  30.2 7.9 %collective-permute-start.5 = (bf16[2,8,64,128]{3,2,1,0:T(8,128)(2,1)S(1)}, bf16[2,8,64,128]{3,2,1,0:T(8,128)(2,1)S(1)}, u32[]{:S(2)}, u32[]{:S(2)}) collective-permute-start(bf16[2,8,64,128]{3,2,1,0:T(8,128)(2,1)S(1)} %pad_maximum_fusion.1.a23), channel_id=1, source_target_pairs={{0,8},{1,9},{2,10},{3,11},{4,12},{5,13},{6,14},{7,15},{8,0},{9,1},... | collective-permute-start | bytes 786440 | tf_op jit(solution)/shard_map/ppermute | solution.py:357
  32.1 4.8 %collective-permute-start = (bf16[8,64,128]{2,1,0:T(8,128)(2,1)S(1)}, bf16[8,64,128]{2,1,0:T(8,128)(2,1)S(1)}, u32[]{:S(2)}, u32[]{:S(2)}) collective-permute-start(bf16[8,64,128]{2,1,0:T(8,128)(2,1)S(1)} %slice.36), channel_id=1, source_target_pairs={{0,8},{1,9},{2,10},{3,11},{4,12},{5,13},{6,14},{7,15},{8,0},{9,1},... | collective-permute-start | bytes 393224 | tf_op jit(solution)/shard_map/ppermute | solution.py:357
  34.9 3.2 %collective-permute-start.2 = (bf16[8,64,128]{2,1,0:T(8,128)(2,1)S(1)}, bf16[8,64,128]{2,1,0:T(8,128)(2,1)S(1)}, u32[]{:S(2)}, u32[]{:S(2)}) collective-permute-start(bf16[8,64,128]{2,1,0:T(8,128)(2,1)S(1)} %collective-permute-done.1.a1), channel_id=1, source_target_pairs={{0,8},{1,9},{2,10},{3,11},{4,12},{5,13},{6,14},{7,15},{8,0},{9,1},... | collective-permute-start | bytes 393224 | tf_op jit(solution)/shard_map/ppermute | solution.py:357
  45.2 3.8 %collective-permute-start.6 = (bf16[4,8,64,128]{3,2,1,0:T(8,128)(2,1)S(1)}, bf16[4,8,64,128]{3,2,1,0:T(8,128)(2,1)S(1)}, u32[]{:S(2)}, u32[]{:S(2)}) collective-permute-start(bf16[4,8,64,128]{3,2,1,0:T(8,128)(2,1)S(1)} %get-tuple-element.17), channel_id=1, source_target_pairs={{0,8},{1,9},{2,10},{3,11},{4,12},{5,13},{6,14},{7,15},{8,0},{9,1},... | collective-permute-start | bytes 1572872 | tf_op jit(solution)/shard_map/ppermute | solution.py:332
  49.1 11.5 %collective-permute-start.7 = (bf16[8,64,128]{2,1,0:T(8,128)(2,1)S(1)}, bf16[8,64,128]{2,1,0:T(8,128)(2,1)S(1)}, u32[]{:S(2)}, u32[]{:S(2)}) collective-permute-start(bf16[8,64,128]{2,1,0:T(8,128)(2,1)S(1)} %get-tuple-element.19), channel_id=1, source_target_pairs={{16,0},{32,16},{48,32},{17,1},{33,17},{49,33},{18,2},{34,18},{50,3... | collective-permute-start | bytes 393224 | tf_op jit(solution)/shard_map/ppermute | solution.py:328
  51.1 9.6 %collective-permute-start.8 = (bf16[8,64,128]{2,1,0:T(8,128)(2,1)S(1)}, bf16[8,64,128]{2,1,0:T(8,128)(2,1)S(1)}, u32[]{:S(2)}, u32[]{:S(2)}) collective-permute-start(bf16[8,64,128]{2,1,0:T(8,128)(2,1)S(1)} %get-tuple-element.20), channel_id=1, source_target_pairs={{32,0},{48,16},{33,1},{49,17},{34,2},{50,18},{35,3},{51,19},{68,36... | collective-permute-start | bytes 393224 | tf_op jit(solution)/shard_map/ppermute | solution.py:328
  52.4 8.3 %collective-permute-start.9 = (bf16[8,64,128]{2,1,0:T(8,128)(2,1)S(1)}, bf16[8,64,128]{2,1,0:T(8,128)(2,1)S(1)}, u32[]{:S(2)}, u32[]{:S(2)}) collective-permute-start(bf16[8,64,128]{2,1,0:T(8,128)(2,1)S(1)} %get-tuple-element.21), channel_id=1, source_target_pairs={{48,0},{49,1},{50,2},{51,3},{84,36},{85,37},{86,38},{87,39},{56,8}... | collective-permute-start | bytes 393224 | tf_op jit(solution)/shard_map/ppermute | solution.py:328
  60.8 27.9 %copy-start = (s32[8]{0:T(128)S(1)}, s32[8]{0:T(128)}, u32[]{:S(2)}) copy-start(s32[8]{0:T(128)} %shift_ref.1) | copy-start | bytes 100

commit v5 on v4

v5 whole, which is shorter than its diff:
```python
import math

import jax
import jax.numpy as jnp
from jax import lax
from jax.experimental import pallas as pl
from jax.experimental.pallas import tpu as pltpu
from jax.sharding import PartitionSpec as P

GROUP = 2048
HEADS = 8
PER = 4
HD = 128
TOK = 256
SUB = 32
ROWS = TOK * PER
COLS = 512
BOTH = 2 * ROWS
QAT = 64
WIDE = 320
LOG2E = 1.4426950408889634
NEG = -1e30
SCALING = 1.0 / math.sqrt(HD)
EXPONENT = SCALING * LOG2E
F32 = jnp.float32
BF16 = jnp.bfloat16
VM = pl.BlockSpec(memory_space=pltpu.VMEM)
SM = pl.BlockSpec(memory_space=pltpu.SMEM)
AXES = ("seq", "head")


LONG = pl.CostEstimate(flops=10_000_000_000, bytes_accessed=1 << 20, transcendentals=0)


def params():
    return pltpu.CompilerParams(vmem_limit_bytes=24 * 1024 * 1024)


def dot(a, b):
    return jnp.dot(a, b, preferred_element_type=F32)


def place_of_head(shift_ref, head):
    place = jnp.zeros(head.shape, jnp.int32)
    plain = jnp.int32(0)
    moved = jnp.int32(HEADS // 2)
    for h in range(HEADS):
        is_moved = (shift_ref[h] > 0).astype(jnp.int32)
        rank = jnp.where(is_moved == 1, moved, plain)
        place = jnp.where(head == h, rank, place)
        moved = moved + is_moved
        plain = plain + 1 - is_moved
    return place


def kv_order(shift_ref, back):
    local = lax.broadcasted_iota(jnp.int32, (TOK, TOK), 0 if back else 1)
    placed = lax.broadcasted_iota(jnp.int32, (TOK, TOK), 1 if back else 0)
    head = lax.broadcasted_iota(jnp.int32, (TOK, 1) if back else (1, TOK), 0 if back else 1) & 7
    place = place_of_head(shift_ref, head)
    hit = ((local >> 3) == (placed & 31)) & (place == (placed >> 5))
    return jnp.where(hit, 1.0, 0.0).astype(BF16)


def q_order(shift_ref, back):
    local = lax.broadcasted_iota(jnp.int32, (TOK, TOK), 0 if back else 1)
    placed = lax.broadcasted_iota(jnp.int32, (TOK, TOK), 1 if back else 0)
    head = lax.broadcasted_iota(jnp.int32, (TOK, 1) if back else (1, TOK), 0 if back else 1)
    place = place_of_head(shift_ref, (head >> 2) & 7)
    same = ((local >> 5) == ((placed & 31) >> 2)) & ((local & 3) == (placed & 3))
    return jnp.where(same & (place == (placed >> 5)), 1.0, 0.0).astype(BF16)


def pack_kernel(shift_hbm, k_hbm, v_hbm, q_hbm, d_hbm, out_ref, shift_ref, k_ref, v_ref, q_ref, d_ref, sems):
    copies = [
        pltpu.make_async_copy(src, dst, sems.at[n])
        for n, (src, dst) in enumerate(
            ((shift_hbm, shift_ref), (k_hbm, k_ref), (v_hbm, v_ref), (q_hbm, q_ref), (d_hbm, d_ref))
        )
    ]
    for copy in copies:
        copy.start()
    copies[0].wait()
    order = kv_order(shift_ref, False)
    wide_order = q_order(shift_ref, False)
    for n, ref in enumerate((k_ref, v_ref)):
        copies[n + 1].wait()
        moved = dot(order, ref[...]).astype(BF16)
        for h in range(HEADS):
            out_ref[h, n * SUB : (n + 1) * SUB, :] = moved[h * SUB : (h + 1) * SUB]
    for n, ref in enumerate((q_ref, d_ref)):
        copies[n + 3].wait()
        for b in range(4):
            moved = dot(wide_order, ref[b * TOK : (b + 1) * TOK, :]).astype(BF16)
            for h in range(HEADS):
                at = QAT + n * 128 + b * 32
                out_ref[h, at : at + 32, :] = moved[h * 32 : (h + 1) * 32]


def unpack_kernel(shift_ref, in_ref, o_ref, q_ref, k_ref, v_ref):
    order = kv_order(shift_ref, True)
    wide_order = q_order(shift_ref, True)
    for n, ref in enumerate((k_ref, v_ref)):
        held = in_ref[:, n * SUB : (n + 1) * SUB, :].reshape(TOK, HD)
        ref[...] = dot(order, held).astype(BF16)
    for n, ref in enumerate((o_ref, q_ref)):
        for b in range(4):
            at = QAT + n * 128 + b * 32
            held = in_ref[:, at : at + 32, :].reshape(TOK, HD)
            ref[b * TOK : (b + 1) * TOK, :] = dot(wide_order, held).astype(BF16)


def columns():
    return [slice(c * COLS, (c + 1) * COLS) for c in range(BOTH // COLS)]


def fold(x, op):
    return op(x.reshape(TOK // 8, 8, COLS), axis=0)


def rows_of(all_ref, swapped_ref, at):
    mine = all_ref[:, QAT + at : QAT + at + 128, :].reshape(ROWS, HD)
    return mine, swapped_ref[:, at : at + 128, :].reshape(ROWS, HD)


def first_kernel(where_ref, all_ref, swapped_ref, qt_ref, dt_ref, s_ref, dp_ref, m_ref):
    core = where_ref[1]
    for ref, at in ((qt_ref, 0), (dt_ref, 128)):
        mine, other = rows_of(all_ref, swapped_ref, at)
        ref[:, 0:ROWS] = mine.T
        ref[:, ROWS:BOTH] = other.T
    keys = all_ref[:, 0:SUB, :].reshape(TOK, HD)
    vals = all_ref[:, SUB : 2 * SUB, :].reshape(TOK, HD)
    for c, at in enumerate(columns()):
        s = dot(keys, qt_ref[:, at])
        u = lax.broadcasted_iota(jnp.int32, (TOK, COLS), 0)
        if c * COLS < ROWS:
            limit = (lax.broadcasted_iota(jnp.int32, (TOK, COLS), 1) + c * COLS) >> 2
        else:
            limit = jnp.where(core == 0, TOK, -1)
        s = jnp.where(u <= limit, s, NEG)
        s_ref[:, at] = s
        m_ref[:, at] = fold(s, jnp.max)
        dp_ref[:, at] = dot(vals, dt_ref[:, at])


def probs_kernel(where_ref, qt_ref, dt_ref, s0_ref, dp0_ref, m0_ref, a1, a2, a3, p_ref, dp_ref, stats_ref, k_s, v_s, m_s, l_s, r_s):
    chips = where_ref[0]
    for n, ref in enumerate((a1, a2, a3)):
        k_s[n] = ref[:, 0:SUB, :].reshape(TOK, HD)
        v_s[n] = ref[:, SUB : 2 * SUB, :].reshape(TOK, HD)
    m_s[...] = m0_ref[...]

    def scores(b, _):
        for at in columns():
            s = dot(k_s[b - 1], qt_ref[:, at])
            p_ref[b, :, at] = s
            m_s[:, at] = jnp.maximum(m_s[:, at], fold(s, jnp.max))
        return 0

    lax.fori_loop(1, chips + 1, scores, 0)
    top = jnp.max(m_s[...], axis=0, keepdims=True)
    m_s[...] = jnp.broadcast_to(top, (8, BOTH))

    for at in columns():
        p = jnp.exp2((s0_ref[:, at] - m_s[0:1, at]) * EXPONENT)
        p_ref[0, :, at] = p
        l_s[:, at] = fold(p, jnp.sum)
        r_s[:, at] = fold(p * dp0_ref[:, at], jnp.sum)

    def forward(b, _):
        for at in columns():
            p = jnp.exp2((p_ref[b, :, at] - m_s[0:1, at]) * EXPONENT)
            dp = dot(v_s[b - 1], dt_ref[:, at])
            p_ref[b, :, at] = p
            dp_ref[b - 1, :, at] = dp
            l_s[:, at] += fold(p, jnp.sum)
            r_s[:, at] += fold(p * dp, jnp.sum)
        return 0

    lax.fori_loop(1, chips + 1, forward, 0)
    stats_ref[0:1, :] = top
    stats_ref[1:2, :] = jnp.sum(l_s[...], axis=0, keepdims=True)
    stats_ref[2:3, :] = jnp.sum(r_s[...], axis=0, keepdims=True)
    stats_ref[3:8, :] = jnp.zeros((5, BOTH), F32)


def attended_kernel(where_ref, all_ref, a1, a2, a3, p_ref, o_ref, vt_s):
    chips = where_ref[0]
    for n, ref in enumerate((all_ref, a1, a2, a3)):
        vt_s[n] = ref[:, SUB : 2 * SUB, :].reshape(TOK, HD).T
    for at in columns():
        o_ref[:, at] = dot(vt_s[0], p_ref[0, :, at].astype(BF16))

    def add(b, _):
        for at in columns():
            o_ref[:, at] += dot(vt_s[b], p_ref[b, :, at].astype(BF16))
        return 0

    lax.fori_loop(1, chips + 1, add, 0)


def grads_kernel(
    where_ref, stats_ref, swapped_stats_ref, all_ref, swapped_ref, p_ref, dp0_ref, dp_ref,
    own_ref, c1, c2, c3, ds_ref, f_ref, q_s, d_s, g_s, r_s,
):
    chips = where_ref[0]
    q_s[0:ROWS, :], q_s[ROWS:BOTH, :] = rows_of(all_ref, swapped_ref, 0)
    d_s[0:ROWS, :], d_s[ROWS:BOTH, :] = rows_of(all_ref, swapped_ref, 128)
    for half in range(2):
        at = slice(half * ROWS, (half + 1) * ROWS)
        there = slice((1 - half) * ROWS, (2 - half) * ROWS)
        top = stats_ref[0:1, at]
        other_top = swapped_stats_ref[0:1, there]
        highest = jnp.maximum(top, other_top)
        f = jnp.exp2((top - highest) * EXPONENT)
        g = jnp.exp2((other_top - highest) * EXPONENT)
        inv = 1.0 / (stats_ref[1:2, at] * f + swapped_stats_ref[1:2, there] * g)
        row_dot = (stats_ref[2:3, at] * f + swapped_stats_ref[2:3, there] * g) * inv
        f_ref[:, at] = jnp.broadcast_to(f * inv, (8, ROWS))
        r_s[:, at] = jnp.broadcast_to(row_dot, (8, ROWS))

    def grads(b, dp):
        dk = jnp.zeros((TOK, HD), F32)
        dv = jnp.zeros((TOK, HD), F32)
        for at in columns():
            p = p_ref[b, :, at] * f_ref[0:1, at]
            ds = (p * (dp[:, at] - r_s[0:1, at])).astype(BF16)
            ds_ref[b, :, at] = ds
            dk = dk + dot(ds, q_s[at, :])
            dv = dv + dot(p.astype(BF16), d_s[at, :])
        return dk * SCALING, dv

    dk, dv = grads(0, dp0_ref)
    own_ref[:, 0:SUB, :] = dk.reshape(HEADS, SUB, HD)
    own_ref[:, SUB : 2 * SUB, :] = dv.reshape(HEADS, SUB, HD)

    def far(b, _):
        dk, dv = grads(b, dp_ref.at[b - 1])
        g_s[b - 1, :, 0:SUB, :] = dk.astype(BF16).reshape(HEADS, SUB, HD)
        g_s[b - 1, :, SUB : 2 * SUB, :] = dv.astype(BF16).reshape(HEADS, SUB, HD)
        return 0

    lax.fori_loop(1, chips + 1, far, 0)
    for dist, ref in ((1, c1), (2, c2), (3, c3)):

        @pl.when(chips >= dist)
        def _():
            ref[...] = g_s[dist - 1]

        @pl.when(chips < dist)
        def _():
            ref[...] = jnp.zeros((HEADS, 2 * SUB, HD), BF16)


def query_kernel(where_ref, all_ref, a1, a2, a3, ds_ref, o_ref, f_ref, mine_ref, other_ref, kt_s, g_s):
    chips = where_ref[0]
    for n, ref in enumerate((all_ref, a1, a2, a3)):
        kt_s[n] = ref[:, 0:SUB, :].reshape(TOK, HD).T
    for at in columns():
        g_s[:, at] = dot(kt_s[0], ds_ref[0, :, at])

    def add(b, _):
        for at in columns():
            g_s[:, at] += dot(kt_s[b], ds_ref[b, :, at])
        return 0

    lax.fori_loop(1, chips + 1, add, 0)
    for n, ref in enumerate((mine_ref, other_ref)):
        at = slice(n * ROWS, (n + 1) * ROWS)
        o = (o_ref[:, at] * f_ref[0:1, at]).T
        g = (g_s[:, at] * SCALING).T
        ref[:, 0:128, :] = o.reshape(HEADS, 128, HD).astype(ref.dtype)
        ref[:, 128:256, :] = g.reshape(HEADS, 128, HD).astype(ref.dtype)


def sum_kernel(own_ref, c1, c2, c3, out_ref):
    total = own_ref[...]
    for ref in (c1, c2, c3):
        total = total + ref[...].astype(F32)
    out_ref[...] = total.astype(BF16)


def shape(*dims, dtype=BF16):
    return jax.ShapeDtypeStruct(dims, dtype)


def run(kernel, outs, scratch, *operands, first=SM, cost=None):
    return pl.pallas_call(
        kernel,
        out_shape=outs,
        in_specs=[first] + [VM] * (len(operands) - 1),
        out_specs=tuple(VM for _ in outs),
        scratch_shapes=scratch,
        compiler_params=params(),
        cost_estimate=cost,
    )(*operands)


def pack(shift, k, v, q, d):
    return pl.pallas_call(
        pack_kernel,
        out_shape=shape(HEADS, WIDE, HD),
        in_specs=[pl.BlockSpec(memory_space=pl.ANY)] * 5,
        out_specs=VM,
        scratch_shapes=[
            pltpu.SMEM((HEADS,), jnp.int32),
            pltpu.VMEM((TOK, HD), BF16),
            pltpu.VMEM((TOK, HD), BF16),
            pltpu.VMEM((ROWS, HD), BF16),
            pltpu.VMEM((ROWS, HD), BF16),
            pltpu.SemaphoreType.DMA((5,)),
        ],
        compiler_params=pltpu.CompilerParams(vmem_limit_bytes=60 * 1024 * 1024),
    )(shift, k, v, q, d)


def rows_of_groups():
    rows = []
    for start in range(0, 64, 8):
        for core in range(2):
            for place in range(HEADS):
                moved = GROUP // 2 // TOK if place >= HEADS // 2 else 0
                rows.append([(start + moved + 2 * i + core) % 64 * 8 + place for i in range(4)])
    return rows


ALONG = rows_of_groups()
SWAP = [(s * 8 + h, (s ^ 1) * 8 + h) for s in range(64) for h in range(8)]


def ahead(x, dist):
    return lax.ppermute(x, AXES, [(r[i], r[i + dist]) for r in ALONG for i in range(4 - dist)])


def behind(x, dist):
    return lax.ppermute(x, AXES, [(r[i + dist], r[i]) for r in ALONG for i in range(4 - dist)])


def local(queries, keys, values, d_attended, shift_amounts):
    seq_pos = lax.axis_index("seq")
    place = lax.axis_index("head")
    in_group = (seq_pos - jnp.where(place >= HEADS // 2, 4, 0)) & 7
    where = jnp.stack((in_group >> 1, in_group & 1)).astype(jnp.int32)
    packed = pack(
        shift_amounts,
        keys.reshape(TOK, HD),
        values.reshape(TOK, HD),
        queries.reshape(ROWS, HD),
        d_attended.reshape(ROWS, HD),
    )
    everything = lax.all_to_all(packed, "head", 0, 0, tiled=True)
    own = everything[:, 0 : 2 * SUB]
    a = [ahead(own, dist) for dist in (1, 2, 3)]
    swapped = lax.ppermute(everything[:, QAT:WIDE], AXES, SWAP)
    rows = pltpu.VMEM((8, BOTH), F32)
    qt, dt, s0, dp0, m0 = run(
        first_kernel,
        (shape(HD, BOTH), shape(HD, BOTH), shape(TOK, BOTH, dtype=F32), shape(TOK, BOTH, dtype=F32), shape(8, BOTH, dtype=F32)),
        [],
        where, everything, swapped,
        cost=LONG,
    )
    probs, dp, stats = run(
        probs_kernel,
        (shape(4, TOK, BOTH, dtype=F32), shape(3, TOK, BOTH, dtype=F32), shape(8, BOTH, dtype=F32)),
        [pltpu.VMEM((3, TOK, HD), BF16), pltpu.VMEM((3, TOK, HD), BF16), rows, rows, rows],
        where, qt, dt, s0, dp0, m0, *a,
    )
    swapped_stats = lax.ppermute(stats, AXES, SWAP)
    (o,) = run(
        attended_kernel,
        (shape(HD, BOTH, dtype=F32),),
        [pltpu.VMEM((4, HD, TOK), BF16)],
        where, everything, *a, probs,
        cost=LONG,
    )
    block = shape(HEADS, 2 * SUB, HD)
    grads, c1, c2, c3, ds, f = run(
        grads_kernel,
        (shape(HEADS, 2 * SUB, HD, dtype=F32), block, block, block, shape(4, TOK, BOTH), shape(8, BOTH, dtype=F32)),
        [pltpu.VMEM((BOTH, HD), BF16), pltpu.VMEM((BOTH, HD), BF16), pltpu.VMEM((3, HEADS, 2 * SUB, HD), BF16), rows],
        where, stats, swapped_stats, everything, swapped, probs, dp0, dp,
    )
    back = [behind(part, dist) for dist, part in zip((1, 2, 3), (c1, c2, c3))]
    mine, other = run(
        query_kernel,
        (shape(HEADS, 256, HD, dtype=F32), shape(HEADS, 256, HD)),
        [pltpu.VMEM((4, HD, TOK), BF16), pltpu.VMEM((HD, BOTH), F32)],
        where, everything, *a, ds, o, f,
        cost=LONG,
    )
    oq = (mine + lax.ppermute(other, AXES, SWAP).astype(F32)).astype(BF16)
    (grads,) = run(sum_kernel, (block,), [], *(grads, *back), first=VM, cost=LONG)
    done = lax.all_to_all(jnp.concatenate((grads, oq), axis=1), "head", 0, 0, tiled=True)
    attended, d_queries, d_keys, d_values = run(
        unpack_kernel,
        (shape(ROWS, HD), shape(ROWS, HD), shape(TOK, HD), shape(TOK, HD)),
        [],
        shift_amounts,
        done,
    )
    return (
        attended.reshape(SUB, HEADS, PER, HD),
        d_queries.reshape(SUB, HEADS, PER, HD),
        d_keys.reshape(SUB, HEADS, HD),
        d_values.reshape(SUB, HEADS, HD),
    )


def solution(mesh):
    wide = P(("seq", "head"), None, None, None)
    flat = P(("seq", "head"), None, None)
    return jax.shard_map(
        local,
        mesh=mesh,
        in_specs=(wide, flat, flat, wide, P()),
        out_specs=(wide, wide, flat, flat),
        check_vma=False,
    )
```

time: 91 us -> 90.1 us (level)
  blocking collectives: 45.5 us -> 41 us
  waiting for transfers between devices: 13.2 us -> 16.5 us
  Pallas kernels: 13.3 us -> 15.8 us
  starting transfers between devices: 17.4 us -> 15.3 us
    ppermute x3, waiting for transfers between devices: 4.31 us -> 10.7 us  [ahead(): lax.ppermute(x, AXES, [(r[i], r[i + dist]) for r in ALONG for i in range(...]
    all_to_all x1, blocking collectives: 27.8 us -> 23.4 us  [local(): lax.all_to_all(jnp.concatenate((grads, oq), axis=1), 'head', 0, 0, tiled=...]
    ppermute x4 -> x3, waiting for transfers between devices: 2.97 us -> 0.01 us  [the longest x1 0.01 us: local(): swapped = lax.ppermute(everything[:, QAT:WIDE], AXES, SWAP)]
    pallas_call x3 -> x7, Pallas kernels: 10.6 us -> 13.1 us  [run(): pl.pallas_call(kernel, out_shape=outs, in_specs=[first] + [VM] * (len(ope...]
    ppermute x4 -> x3, starting transfers between devices: 8.29 us -> 6.25 us  [the longest x1 2.32 us: local(): oq = (mine + lax.ppermute(other, AXES, SWAP).astype(F32)).astype(BF16)]
  transfers between devices with their start and end apart: 10 -> 9, of which waited for: 5 -> 3; matrix products, arithmetic and copies ran while one was open for 0% -> 0% of each run, Pallas kernels for 2% -> 5%
where the time goes in v5:
time: 90.1 us; the launch traced here: 89.7 us
  blocking collectives  41 us (46%)
  waiting for transfers between devices  16.5 us (18%)
  Pallas kernels  15.8 us (18%)
  starting transfers between devices  15.3 us (17%)
    all_to_all x1, blocking collectives, local(): lax.all_to_all(jnp.concatenate((grads, oq), axis=1), 'head', 0, 0, tiled=...  23.4 us
    all_to_all x1, blocking collectives, local(): everything = lax.all_to_all(packed, 'head', 0, 0, tiled=True)  17.7 us
    pallas_call x7, Pallas kernels, run(): pl.pallas_call(kernel, out_shape=outs, in_specs=[first] + [VM] * (len(ope...  13.1 us
    ppermute x3, waiting for transfers between devices, ahead(): lax.ppermute(x, AXES, [(r[i], r[i + dist]) for r in ALONG for i in range(...  10.7 us
    ppermute x3, waiting for transfers between devices, behind(): lax.ppermute(x, AXES, [(r[i + dist], r[i]) for r in ALONG for i in range(...  5.71 us
    ppermute x3, starting transfers between devices, ahead(): lax.ppermute(x, AXES, [(r[i], r[i + dist]) for r in ALONG for i in range(...  5.17 us
    ppermute x3, starting transfers between devices, behind(): lax.ppermute(x, AXES, [(r[i + dist], r[i]) for r in ALONG for i in range(...  3.89 us
    pallas_call x1, Pallas kernels, pack(): pl.pallas_call(pack_kernel, out_shape=shape(HEADS, WIDE, HD), in_specs=[p...  2.71 us
  transfers between devices with their start and end apart: 9, of which 3 were waited for; matrix products, arithmetic and copies ran while one was open for 0% of the time, Pallas kernels for 5%

profile of v5, /device:TPU:176, one launch (start us, length us, event | category | flops | bytes accessed | tf_op | source)
XLA Modules:
  0.0 89.7 jit_solution(17177461034031868632)
XLA Ops:
  0.6 2.7 %shard_map.84 = bf16[8,320,128]{2,1,0:T(8,128)(2,1)} custom-call(s32[8]{0:T(128)} %shift_ref.1, bf16[256,128]{1,0:T(8,128)(2,1)} %bitcast.12, bf16[256,128]{1,0:T(8,128)(2,1)} %bitcast.13, bf16[1024,128]{1,0:T(8,128)(2,1)} %bitcast.10, bf16[1024,128]{1,0:T(8,128)(2,1)} %bitcast.11), custom_call_target="tpu_custom_call" | custom-call | tf_op jit(solution)/shard_map/pallas_call | solution.py:301
  3.4 17.7 %all_to_all.10.all_ref = bf16[8,320,128]{2,1,0:T(8,128)(2,1)S(1)} all-to-all(bf16[8,320,128]{2,1,0:T(8,128)(2,1)} %shard_map.84), channel_id=1, replica_groups=mesh['seq'=64,'head'=8] {'head'}, dimensions={0} | all-to-all | bytes 1310720 | tf_op jit(solution)/shard_map/all_to_all | solution.py:352
  21.0 1.9 %collective-permute-start = (bf16[8,256,128]{2,1,0:T(8,128)(2,1)S(1)}, bf16[8,256,128]{2,1,0:T(8,128)(2,1)S(1)}, u32[]{:S(2)}, u32[]{:S(2)}) collective-permute-start(bf16[8,256,128]{2,1,0:T(8,128)(2,1)S(1)} %slice.8), channel_id=1, source_target_pairs={{0,8},{1,9},{2,10},{3,11},{4,12},{5,13},{6,14},{7,15},{8,0},{9,1},... | collective-permute-start | bytes 1572872 | tf_op jit(solution)/shard_map/ppermute | solution.py:355
  23.0 0.1 pad_add_fusion.where_ref
  23.1 0.7 collective-permute-start.3
  23.7 1.3 %collective-permute-start.2 = (bf16[8,64,128]{2,1,0:T(8,128)(2,1)S(1)}, bf16[8,64,128]{2,1,0:T(8,128)(2,1)S(1)}, u32[]{:S(2)}, u32[]{:S(2)}) collective-permute-start(bf16[8,64,128]{2,1,0:T(8,128)(2,1)S(1)} %slice.9), channel_id=1, source_target_pairs={{0,32},{16,48},{1,33},{17,49},{2,34},{18,50},{3,35},{19,51},{36,68... | collective-permute-start | bytes 393224 | tf_op jit(solution)/shard_map/ppermute | solution.py:333
  25.0 3.2 %collective-permute-start.1 = (bf16[8,64,128]{2,1,0:T(8,128)(2,1)S(1)}, bf16[8,64,128]{2,1,0:T(8,128)(2,1)S(1)}, u32[]{:S(2)}, u32[]{:S(2)}) collective-permute-start(bf16[8,64,128]{2,1,0:T(8,128)(2,1)S(1)} %slice.9), channel_id=1, source_target_pairs={{0,16},{16,32},{32,48},{1,17},{17,33},{33,49},{2,18},{18,34},{34,5... | collective-permute-start | bytes 393224 | tf_op jit(solution)/shard_map/ppermute | solution.py:333
  28.3 0.0 collective-permute-done.swapped_ref
  28.3 1.3 %shard_map.85 = (bf16[128,2048]{1,0:T(8,128)(2,1)S(1)}, bf16[128,2048]{1,0:T(8,128)(2,1)S(1)}, f32[256,2048]{1,0:T(8,128)S(1)}, f32[256,2048]{1,0:T(8,128)S(1)}, f32[8,2048]{1,0:T(8,128)S(1)}) custom-call(s32[2]{0:T(128)S(1)} %pad_add_fusion.where_ref, bf16[8,320,128]{2,1,0:T(8,128)(2,1)S(1)} %all_to_all.10.all_ref, ...), custom_call_target="tpu_custom_call" | custom-call | flops 10000000000 | bytes 1048576 | tf_op jit(solution)/shard_map/pallas_call | solution.py:289
  29.6 0.0 collective-permute-done.3.a3
  29.6 5.6 %collective-permute-done.2.a2 = bf16[8,64,128]{2,1,0:T(8,128)(2,1)S(1)} collective-permute-done((bf16[8,64,128]{2,1,0:T(8,128)(2,1)S(1)}, bf16[8,64,128]{2,1,0:T(8,128)(2,1)S(1)}, u32[]{:S(2)}, u32[]{:S(2)}) %collective-permute-start.2) | collective-permute-done | bytes 131104 | tf_op jit(solution)/shard_map/ppermute | solution.py:333
  35.1 5.2 %collective-permute-done.1.a1 = bf16[8,64,128]{2,1,0:T(8,128)(2,1)S(1)} collective-permute-done((bf16[8,64,128]{2,1,0:T(8,128)(2,1)S(1)}, bf16[8,64,128]{2,1,0:T(8,128)(2,1)S(1)}, u32[]{:S(2)}, u32[]{:S(2)}) %collective-permute-start.1) | collective-permute-done | bytes 131104 | tf_op jit(solution)/shard_map/ppermute | solution.py:333
  40.3 3.1 %shard_map.86 = (f32[4,256,2048]{2,1,0:T(8,128)S(1)}, f32[3,256,2048]{2,1,0:T(8,128)S(1)}, f32[8,2048]{1,0:T(8,128)S(1)}) custom-call(s32[2]{0:T(128)S(1)} %pad_add_fusion.where_ref, bf16[128,2048]{1,0:T(8,128)(2,1)S(1)} %get-tuple-element.24.qt_ref, bf16[128,2048]{1,0:T(8,128)(2,1)S(1)} %get-tuple-element.25.dt_ref, ...), custom_call_target="tpu_custom_call" | custom-call | tf_op jit(solution)/shard_map/pallas_call | solution.py:289
  43.5 2.0 %collective-permute-start.4 = (f32[8,2048]{1,0:T(8,128)S(1)}, f32[8,2048]{1,0:T(8,128)S(1)}, u32[]{:S(2)}, u32[]{:S(2)}) collective-permute-start(f32[8,2048]{1,0:T(8,128)S(1)} %get-tuple-element.29.stats_ref), channel_id=1, source_target_pairs={{0,8},{1,9},{2,10},{3,11},{4,12},{5,13},{6,14},{7,15},{8,0},{9,1},... | collective-permute-start | bytes 196616 | tf_op jit(solution)/shard_map/ppermute | solution.py:370
  45.5 1.5 %shard_map.89.o_ref = f32[128,2048]{1,0:T(8,128)S(1)} custom-call(s32[2]{0:T(128)S(1)} %pad_add_fusion.where_ref, bf16[8,320,128]{2,1,0:T(8,128)(2,1)S(1)} %all_to_all.10.all_ref, bf16[8,64,128]{2,1,0:T(8,128)(2,1)S(1)} %collective-permute-done.1.a1, bf16[8,64,128]{2,1,0:T(8,128)(2,1)S(1)} %collective-permute-done.2.a2, ...), custom_call_target="tpu_custom_call" | custom-call | flops 10000000000 | bytes 1048576 | tf_op jit(solution)/shard_map/pallas_call | solution.py:289
  47.0 0.0 collective-permute-done.4.swapped_stats_ref
  47.0 3.2 %shard_map.87 = (f32[8,64,128]{2,1,0:T(8,128)S(1)}, bf16[8,64,128]{2,1,0:T(8,128)(2,1)S(1)}, bf16[8,64,128]{2,1,0:T(8,128)(2,1)S(1)}, bf16[8,64,128]{2,1,0:T(8,1...) custom-call(s32[2]{0:T(128)S(1)} %pad_add_fusion.where_ref, ...), custom_call_target="tpu_custom_call" | custom-call | tf_op jit(solution)/shard_map/pallas_call | solution.py:289
  50.2 1.9 %collective-permute-start.5 = (bf16[8,64,128]{2,1,0:T(8,128)(2,1)S(1)}, bf16[8,64,128]{2,1,0:T(8,128)(2,1)S(1)}, u32[]{:S(2)}, u32[]{:S(2)}) collective-permute-start(bf16[8,64,128]{2,1,0:T(8,128)(2,1)S(1)} %get-tuple-element.33), channel_id=1, source_target_pairs={{16,0},{32,16},{48,32},{17,1},{33,17},{49,33},{18,2},{34,18},{50,3... | collective-permute-start | bytes 393224 | tf_op jit(solution)/shard_map/ppermute | solution.py:337
  52.1 1.3 %collective-permute-start.6 = (bf16[8,64,128]{2,1,0:T(8,128)(2,1)S(1)}, bf16[8,64,128]{2,1,0:T(8,128)(2,1)S(1)}, u32[]{:S(2)}, u32[]{:S(2)}) collective-permute-start(bf16[8,64,128]{2,1,0:T(8,128)(2,1)S(1)} %get-tuple-element.34), channel_id=1, source_target_pairs={{32,0},{48,16},{33,1},{49,17},{34,2},{50,18},{35,3},{51,19},{68,36... | collective-permute-start | bytes 393224 | tf_op jit(solution)/shard_map/ppermute | solution.py:337
  53.5 0.7 collective-permute-start.7
  54.1 2.0 %shard_map.90 = (f32[8,256,128]{2,1,0:T(8,128)S(1)}, bf16[8,256,128]{2,1,0:T(8,128)(2,1)S(1)}) custom-call(s32[2]{0:T(128)S(1)} %pad_add_fusion.where_ref, bf16[8,320,128]{2,1,0:T(8,128)(2,1)S(1)} %all_to_all.10.all_ref, bf16[8,64,128]{2,1,0:T(8,128)(2,1)S(1)} %collective-permute-done.1.a1, bf16[8,64,128]{2,1,0:T(8,128)(2,1)S(1)} %collective-permute-done.2.a2, ...), custom_call_target="tpu_custom_call" | custom-call | flops 10000000000 | bytes 1048576 | tf_op jit(solution)/shard_map/pallas_call | solution.py:289
  56.1 2.3 %collective-permute-start.8 = (bf16[8,256,128]{2,1,0:T(8,128)(2,1)S(1)}, bf16[8,256,128]{2,1,0:T(8,128)(2,1)S(1)}, u32[]{:S(2)}, u32[]{:S(2)}) collective-permute-start(bf16[8,256,128]{2,1,0:T(8,128)(2,1)S(1)} %get-tuple-element.39), channel_id=1, source_target_pairs={{0,8},{1,9},{2,10},{3,11},{4,12},{5,13},{6,14},{7,15},{8,0},{9,1},... | collective-permute-start | bytes 1572872 | tf_op jit(solution)/shard_map/ppermute | solution.py:393
  58.4 0.0 collective-permute-done.5.c1
  58.5 5.7 %collective-permute-done.6.c2 = bf16[8,64,128]{2,1,0:T(8,128)(2,1)S(1)} collective-permute-done((bf16[8,64,128]{2,1,0:T(8,128)(2,1)S(1)}, bf16[8,64,128]{2,1,0:T(8,128)(2,1)S(1)}, u32[]{:S(2)}, u32[]{:S(2)}) %collective-permute-start.6) | collective-permute-done | bytes 131104 | tf_op jit(solution)/shard_map/ppermute | solution.py:337
  64.2 0.0 collective-permute-done.7.c3
  64.2 0.1 shard_map.88
  64.2 0.0 collective-permute-done.8
  64.2 0.0 copy-start
  64.3 0.1 add_convert_fusion
  64.4 23.4 %all_to_all.11.in_ref = bf16[8,320,128]{2,1,0:T(8,128)(2,1)S(1)} all-to-all(bf16[8,320,128]{2,1,0:T(8,128)(2,1)S(1)} %pad_maximum_fusion), channel_id=1, replica_groups=mesh['seq'=64,'head'=8] {'head'}, dimensions={0} | all-to-all | bytes 1310720 | tf_op jit(solution)/shard_map/all_to_all | solution.py:395
  87.8 0.0 copy-done
  87.8 1.9 %shard_map.91 = (bf16[1024,128]{1,0:T(8,128)(2,1)}, bf16[1024,128]{1,0:T(8,128)(2,1)}, bf16[256,128]{1,0:T(8,128)(2,1)}, bf16[256,128]{1,0:T(8,128)(2,1)}) custom-call(s32[8]{0:T(128)S(1)} %copy-done, bf16[8,320,128]{2,1,0:T(8,128)(2,1)S(1)} %all_to_all.11.in_ref), custom_call_target="tpu_custom_call" | custom-call | tf_op jit(solution)/shard_map/pallas_call | solution.py:289
  (3 shorter events, 0.1 us)
Async XLA Ops:
  21.0 7.2 %collective-permute-start = (bf16[8,256,128]{2,1,0:T(8,128)(2,1)S(1)}, bf16[8,256,128]{2,1,0:T(8,128)(2,1)S(1)}, u32[]{:S(2)}, u32[]{:S(2)}) collective-permute-start(bf16[8,256,128]{2,1,0:T(8,128)(2,1)S(1)} %slice.8), channel_id=1, source_target_pairs={{0,8},{1,9},{2,10},{3,11},{4,12},{5,13},{6,14},{7,15},{8,0},{9,1},... | collective-permute-start | bytes 1572872 | tf_op jit(solution)/shard_map/ppermute | solution.py:355
  23.1 6.5 %collective-permute-start.3 = (bf16[8,64,128]{2,1,0:T(8,128)(2,1)S(1)}, bf16[8,64,128]{2,1,0:T(8,128)(2,1)S(1)}, u32[]{:S(2)}, u32[]{:S(2)}) collective-permute-start(bf16[8,64,128]{2,1,0:T(8,128)(2,1)S(1)} %slice.9), channel_id=1, source_target_pairs={{0,48},{1,49},{2,50},{3,51},{36,84},{37,85},{38,86},{39,87},{8,56}... | collective-permute-start | bytes 393224 | tf_op jit(solution)/shard_map/ppermute | solution.py:333
  23.7 11.4 %collective-permute-start.2 = (bf16[8,64,128]{2,1,0:T(8,128)(2,1)S(1)}, bf16[8,64,128]{2,1,0:T(8,128)(2,1)S(1)}, u32[]{:S(2)}, u32[]{:S(2)}) collective-permute-start(bf16[8,64,128]{2,1,0:T(8,128)(2,1)S(1)} %slice.9), channel_id=1, source_target_pairs={{0,32},{16,48},{1,33},{17,49},{2,34},{18,50},{3,35},{19,51},{36,68... | collective-permute-start | bytes 393224 | tf_op jit(solution)/shard_map/ppermute | solution.py:333
  25.0 15.3 %collective-permute-start.1 = (bf16[8,64,128]{2,1,0:T(8,128)(2,1)S(1)}, bf16[8,64,128]{2,1,0:T(8,128)(2,1)S(1)}, u32[]{:S(2)}, u32[]{:S(2)}) collective-permute-start(bf16[8,64,128]{2,1,0:T(8,128)(2,1)S(1)} %slice.9), channel_id=1, source_target_pairs={{0,16},{16,32},{32,48},{1,17},{17,33},{33,49},{2,18},{18,34},{34,5... | collective-permute-start | bytes 393224 | tf_op jit(solution)/shard_map/ppermute | solution.py:333
  43.5 3.5 %collective-permute-start.4 = (f32[8,2048]{1,0:T(8,128)S(1)}, f32[8,2048]{1,0:T(8,128)S(1)}, u32[]{:S(2)}, u32[]{:S(2)}) collective-permute-start(f32[8,2048]{1,0:T(8,128)S(1)} %get-tuple-element.29.stats_ref), channel_id=1, source_target_pairs={{0,8},{1,9},{2,10},{3,11},{4,12},{5,13},{6,14},{7,15},{8,0},{9,1},... | collective-permute-start | bytes 196616 | tf_op jit(solution)/shard_map/ppermute | solution.py:370
  50.2 8.2 %collective-permute-start.5 = (bf16[8,64,128]{2,1,0:T(8,128)(2,1)S(1)}, bf16[8,64,128]{2,1,0:T(8,128)(2,1)S(1)}, u32[]{:S(2)}, u32[]{:S(2)}) collective-permute-start(bf16[8,64,128]{2,1,0:T(8,128)(2,1)S(1)} %get-tuple-element.33), channel_id=1, source_target_pairs={{16,0},{32,16},{48,32},{17,1},{33,17},{49,33},{18,2},{34,18},{50,3... | collective-permute-start | bytes 393224 | tf_op jit(solution)/shard_map/ppermute | solution.py:337
  52.1 12.0 %collective-permute-start.6 = (bf16[8,64,128]{2,1,0:T(8,128)(2,1)S(1)}, bf16[8,64,128]{2,1,0:T(8,128)(2,1)S(1)}, u32[]{:S(2)}, u32[]{:S(2)}) collective-permute-start(bf16[8,64,128]{2,1,0:T(8,128)(2,1)S(1)} %get-tuple-element.34), channel_id=1, source_target_pairs={{32,0},{48,16},{33,1},{49,17},{34,2},{50,18},{35,3},{51,19},{68,36... | collective-permute-start | bytes 393224 | tf_op jit(solution)/shard_map/ppermute | solution.py:337
  53.5 10.7 %collective-permute-start.7 = (bf16[8,64,128]{2,1,0:T(8,128)(2,1)S(1)}, bf16[8,64,128]{2,1,0:T(8,128)(2,1)S(1)}, u32[]{:S(2)}, u32[]{:S(2)}) collective-permute-start(bf16[8,64,128]{2,1,0:T(8,128)(2,1)S(1)} %get-tuple-element.35), channel_id=1, source_target_pairs={{48,0},{49,1},{50,2},{51,3},{84,36},{85,37},{86,38},{87,39},{56,8}... | collective-permute-start | bytes 393224 | tf_op jit(solution)/shard_map/ppermute | solution.py:337
  56.1 8.1 %collective-permute-start.8 = (bf16[8,256,128]{2,1,0:T(8,128)(2,1)S(1)}, bf16[8,256,128]{2,1,0:T(8,128)(2,1)S(1)}, u32[]{:S(2)}, u32[]{:S(2)}) collective-permute-start(bf16[8,256,128]{2,1,0:T(8,128)(2,1)S(1)} %get-tuple-element.39), channel_id=1, source_target_pairs={{0,8},{1,9},{2,10},{3,11},{4,12},{5,13},{6,14},{7,15},{8,0},{9,1},... | collective-permute-start | bytes 1572872 | tf_op jit(solution)/shard_map/ppermute | solution.py:393
  64.2 23.6 %copy-start = (s32[8]{0:T(128)S(1)}, s32[8]{0:T(128)}, u32[]{:S(2)}) copy-start(s32[8]{0:T(128)} %shift_ref.1) | copy-start | bytes 100

commit v6 on v5

--- a/solution.py
+++ b/solution.py
@@ -123,10 +123,12 @@
     return mine, swapped_ref[:, at : at + 128, :].reshape(ROWS, HD)
 
 
-def first_kernel(where_ref, all_ref, swapped_ref, qt_ref, dt_ref, s_ref, dp_ref, m_ref):
+def first_kernel(where_ref, all_ref, swapped_ref, qt_ref, dt_ref, s_ref, dp_ref, m_ref, q_ref, d_ref):
     core = where_ref[1]
-    for ref, at in ((qt_ref, 0), (dt_ref, 128)):
+    for ref, rows_ref, at in ((qt_ref, q_ref, 0), (dt_ref, d_ref, 128)):
         mine, other = rows_of(all_ref, swapped_ref, at)
+        rows_ref[0:ROWS, :] = mine
+        rows_ref[ROWS:BOTH, :] = other
         ref[:, 0:ROWS] = mine.T
         ref[:, ROWS:BOTH] = other.T
     keys = all_ref[:, 0:SUB, :].reshape(TOK, HD)
@@ -144,12 +146,34 @@
         dp_ref[:, at] = dot(vals, dt_ref[:, at])
 
 
-def probs_kernel(where_ref, qt_ref, dt_ref, s0_ref, dp0_ref, m0_ref, a1, a2, a3, p_ref, dp_ref, stats_ref, k_s, v_s, m_s, l_s, r_s):
+def early_kernel(where_ref, qt_ref, dt_ref, a3, s_ref, dp_ref, m_ref):
     chips = where_ref[0]
-    for n, ref in enumerate((a1, a2, a3)):
+
+    @pl.when(chips == 3)
+    def _():
+        keys = a3[:, 0:SUB, :].reshape(TOK, HD)
+        vals = a3[:, SUB : 2 * SUB, :].reshape(TOK, HD)
+        for at in columns():
+            s = dot(keys, qt_ref[:, at])
+            s_ref[:, at] = s
+            m_ref[:, at] = fold(s, jnp.max)
+            dp_ref[:, at] = dot(vals, dt_ref[:, at])
+
+    @pl.when(chips < 3)
+    def _():
+        m_ref[...] = jnp.full((8, BOTH), NEG, F32)
+
+
+def probs_kernel(
+    where_ref, qt_ref, dt_ref, s0_ref, dp0_ref, m0_ref, s3_ref, dp3_ref, m3_ref, a1, a2,
+    p_ref, dp_ref, stats_ref, k_s, v_s, m_s, l_s, r_s,
+):
+    chips = where_ref[0]
+    last = jnp.minimum(chips, 2) + 1
+    for n, ref in enumerate((a1, a2)):
         k_s[n] = ref[:, 0:SUB, :].reshape(TOK, HD)
         v_s[n] = ref[:, SUB : 2 * SUB, :].reshape(TOK, HD)
-    m_s[...] = m0_ref[...]
+    m_s[...] = jnp.maximum(m0_ref[...], m3_ref[...])
 
     def scores(b, _):
         for at in columns():
@@ -158,7 +182,7 @@
             m_s[:, at] = jnp.maximum(m_s[:, at], fold(s, jnp.max))
         return 0
 
-    lax.fori_loop(1, chips + 1, scores, 0)
+    lax.fori_loop(1, last, scores, 0)
     top = jnp.max(m_s[...], axis=0, keepdims=True)
     m_s[...] = jnp.broadcast_to(top, (8, BOTH))
 
@@ -178,7 +202,16 @@
             r_s[:, at] += fold(p * dp, jnp.sum)
         return 0
 
-    lax.fori_loop(1, chips + 1, forward, 0)
+    lax.fori_loop(1, last, forward, 0)
+
+    @pl.when(chips == 3)
+    def _():
+        for at in columns():
+            p = jnp.exp2((s3_ref[:, at] - m_s[0:1, at]) * EXPONENT)
+            p_ref[3, :, at] = p
+            l_s[:, at] += fold(p, jnp.sum)
+            r_s[:, at] += fold(p * dp3_ref[:, at], jnp.sum)
+
     stats_ref[0:1, :] = top
     stats_ref[1:2, :] = jnp.sum(l_s[...], axis=0, keepdims=True)
     stats_ref[2:3, :] = jnp.sum(r_s[...], axis=0, keepdims=True)
@@ -200,13 +233,23 @@
     lax.fori_loop(1, chips + 1, add, 0)
 
 
+def key_grads(p_ref, dp_ref, ds_ref, f_ref, r_ref, q_ref, d_ref):
+    dk = jnp.zeros((TOK, HD), F32)
+    dv = jnp.zeros((TOK, HD), F32)
+    for at in columns():
+        p = p_ref[:, at] * f_ref[0:1, at]
+        ds = (p * (dp_ref[:, at] - r_ref[0:1, at])).astype(BF16)
+        ds_ref[:, at] = ds
+        dk = dk + dot(ds, q_ref[at, :])
+        dv = dv + dot(p.astype(BF16), d_ref[at, :])
+    return dk * SCALING, dv
+
+
 def grads_kernel(
-    where_ref, stats_ref, swapped_stats_ref, all_ref, swapped_ref, p_ref, dp0_ref, dp_ref,
-    own_ref, c1, c2, c3, ds_ref, f_ref, q_s, d_s, g_s, r_s,
+    where_ref, stats_ref, swapped_stats_ref, q_s, d_s, p_ref, dp_ref, dp3_ref,
+    c1, c2, c3, ds_ref, f_ref, r_s, g_s,
 ):
     chips = where_ref[0]
-    q_s[0:ROWS, :], q_s[ROWS:BOTH, :] = rows_of(all_ref, swapped_ref, 0)
-    d_s[0:ROWS, :], d_s[ROWS:BOTH, :] = rows_of(all_ref, swapped_ref, 128)
     for half in range(2):
         at = slice(half * ROWS, (half + 1) * ROWS)
         there = slice((1 - half) * ROWS, (2 - half) * ROWS)
@@ -220,28 +263,18 @@
         f_ref[:, at] = jnp.broadcast_to(f * inv, (8, ROWS))
         r_s[:, at] = jnp.broadcast_to(row_dot, (8, ROWS))
 
-    def grads(b, dp):
-        dk = jnp.zeros((TOK, HD), F32)
-        dv = jnp.zeros((TOK, HD), F32)
-        for at in columns():
-            p = p_ref[b, :, at] * f_ref[0:1, at]
-            ds = (p * (dp[:, at] - r_s[0:1, at])).astype(BF16)
-            ds_ref[b, :, at] = ds
-            dk = dk + dot(ds, q_s[at, :])
-            dv = dv + dot(p.astype(BF16), d_s[at, :])
-        return dk * SCALING, dv
-
-    dk, dv = grads(0, dp0_ref)
-    own_ref[:, 0:SUB, :] = dk.reshape(HEADS, SUB, HD)
-    own_ref[:, SUB : 2 * SUB, :] = dv.reshape(HEADS, SUB, HD)
-
-    def far(b, _):
-        dk, dv = grads(b, dp_ref.at[b - 1])
+    def far(b, dp):
+        dk, dv = key_grads(p_ref.at[b], dp, ds_ref.at[b - 1], f_ref, r_s, q_s, d_s)
         g_s[b - 1, :, 0:SUB, :] = dk.astype(BF16).reshape(HEADS, SUB, HD)
         g_s[b - 1, :, SUB : 2 * SUB, :] = dv.astype(BF16).reshape(HEADS, SUB, HD)
         return 0
 
-    lax.fori_loop(1, chips + 1, far, 0)
+    lax.fori_loop(1, jnp.minimum(chips, 2) + 1, lambda b, _: far(b, dp_ref.at[b - 1]), 0)
+
+    @pl.when(chips == 3)
+    def _():
+        far(3, dp3_ref)
+
     for dist, ref in ((1, c1), (2, c2), (3, c3)):
 
         @pl.when(chips >= dist)
@@ -253,16 +286,22 @@
             ref[...] = jnp.zeros((HEADS, 2 * SUB, HD), BF16)
 
 
-def query_kernel(where_ref, all_ref, a1, a2, a3, ds_ref, o_ref, f_ref, mine_ref, other_ref, kt_s, g_s):
+def query_kernel(
+    where_ref, all_ref, a1, a2, a3, ds_ref, o_ref, f_ref, r_ref, q_ref, d_ref, p_ref, dp0_ref,
+    mine_ref, other_ref, own_ref, kt_s, g_s, ds0_s,
+):
     chips = where_ref[0]
+    dk, dv = key_grads(p_ref.at[0], dp0_ref, ds0_s, f_ref, r_ref, q_ref, d_ref)
+    own_ref[:, 0:SUB, :] = dk.reshape(HEADS, SUB, HD)
+    own_ref[:, SUB : 2 * SUB, :] = dv.reshape(HEADS, SUB, HD)
     for n, ref in enumerate((all_ref, a1, a2, a3)):
         kt_s[n] = ref[:, 0:SUB, :].reshape(TOK, HD).T
     for at in columns():
-        g_s[:, at] = dot(kt_s[0], ds_ref[0, :, at])
+        g_s[:, at] = dot(kt_s[0], ds0_s[:, at])
 
     def add(b, _):
         for at in columns():
-            g_s[:, at] += dot(kt_s[b], ds_ref[b, :, at])
+            g_s[:, at] += dot(kt_s[b], ds_ref[b - 1, :, at])
         return 0
 
     lax.fori_loop(1, chips + 1, add, 0)
@@ -354,18 +393,21 @@
     a = [ahead(own, dist) for dist in (1, 2, 3)]
     swapped = lax.ppermute(everything[:, QAT:WIDE], AXES, SWAP)
     rows = pltpu.VMEM((8, BOTH), F32)
-    qt, dt, s0, dp0, m0 = run(
+    wide, tall, flat = shape(TOK, BOTH, dtype=F32), shape(BOTH, HD), shape(8, BOTH, dtype=F32)
+    qt, dt, s0, dp0, m0, q_rows, d_rows = run(
         first_kernel,
-        (shape(HD, BOTH), shape(HD, BOTH), shape(TOK, BOTH, dtype=F32), shape(TOK, BOTH, dtype=F32), shape(8, BOTH, dtype=F32)),
+        (shape(HD, BOTH), shape(HD, BOTH), wide, wide, flat, tall, tall),
         [],
         where, everything, swapped,
         cost=LONG,
     )
+    s3, dp3, m3 = run(early_kernel, (wide, wide, flat), [], where, qt, dt, a[2], cost=LONG)
+    held = pltpu.VMEM((2, TOK, HD), BF16)
     probs, dp, stats = run(
         probs_kernel,
-        (shape(4, TOK, BOTH, dtype=F32), shape(3, TOK, BOTH, dtype=F32), shape(8, BOTH, dtype=F32)),
-        [pltpu.VMEM((3, TOK, HD), BF16), pltpu.VMEM((3, TOK, HD), BF16), rows, rows, rows],
-        where, qt, dt, s0, dp0, m0, *a,
+        (shape(4, TOK, BOTH, dtype=F32), shape(2, TOK, BOTH, dtype=F32), flat),
+        [held, held, rows, rows, rows],
+        where, qt, dt, s0, dp0, m0, s3, dp3, m3, a[0], a[1],
     )
     swapped_stats = lax.ppermute(stats, AXES, SWAP)
     (o,) = run(
@@ -376,18 +418,18 @@
         cost=LONG,
     )
     block = shape(HEADS, 2 * SUB, HD)
-    grads, c1, c2, c3, ds, f = run(
+    c1, c2, c3, ds, f, row_dot = run(
         grads_kernel,
-        (shape(HEADS, 2 * SUB, HD, dtype=F32), block, block, block, shape(4, TOK, BOTH), shape(8, BOTH, dtype=F32)),
-        [pltpu.VMEM((BOTH, HD), BF16), pltpu.VMEM((BOTH, HD), BF16), pltpu.VMEM((3, HEADS, 2 * SUB, HD), BF16), rows],
-        where, stats, swapped_stats, everything, swapped, probs, dp0, dp,
+        (block, block, block, shape(3, TOK, BOTH), flat, flat),
+        [pltpu.VMEM((3, HEADS, 2 * SUB, HD), BF16)],
+        where, stats, swapped_stats, q_rows, d_rows, probs, dp, dp3,
     )
     back = [behind(part, dist) for dist, part in zip((1, 2, 3), (c1, c2, c3))]
-    mine, other = run(
+    mine, other, grads = run(
         query_kernel,
-        (shape(HEADS, 256, HD, dtype=F32), shape(HEADS, 256, HD)),
-        [pltpu.VMEM((4, HD, TOK), BF16), pltpu.VMEM((HD, BOTH), F32)],
-        where, everything, *a, ds, o, f,
+        (shape(HEADS, 256, HD, dtype=F32), shape(HEADS, 256, HD), shape(HEADS, 2 * SUB, HD, dtype=F32)),
+        [pltpu.VMEM((4, HD, TOK), BF16), pltpu.VMEM((HD, BOTH), F32), pltpu.VMEM((TOK, BOTH), BF16)],
+        where, everything, *a, ds, o, f, row_dot, q_rows, d_rows, probs, dp0,
         cost=LONG,
     )
     oq = (mine + lax.ppermute(other, AXES, SWAP).astype(F32)).astype(BF16)

time: 90.1 us -> 89.2 us (0.990)
  waiting for transfers between devices: 16.5 us -> 15.3 us
    pallas_call x7 -> x8, Pallas kernels: 13.1 us -> 13.3 us  [run(): pl.pallas_call(kernel, out_shape=outs, in_specs=[first] + [VM] * (len(ope...]
  transfers between devices with their start and end apart: 9 -> 9, of which waited for: 3 -> 3; matrix products, arithmetic and copies ran while one was open for 0% -> 0% of each run, Pallas kernels for 5% -> 7%
where the time goes in v6:
time: 89.2 us; the launch traced here: 88.7 us
  blocking collectives  41 us (46%)
  Pallas kernels  16 us (18%)
  starting transfers between devices  15.3 us (17%)
  waiting for transfers between devices  15.3 us (17%)
    all_to_all x1, blocking collectives, local(): lax.all_to_all(jnp.concatenate((grads, oq), axis=1), 'head', 0, 0, tiled=...  23.4 us
    all_to_all x1, blocking collectives, local(): everything = lax.all_to_all(packed, 'head', 0, 0, tiled=True)  17.7 us
    pallas_call x8, Pallas kernels, run(): pl.pallas_call(kernel, out_shape=outs, in_specs=[first] + [VM] * (len(ope...  13.3 us
    ppermute x3, waiting for transfers between devices, ahead(): lax.ppermute(x, AXES, [(r[i], r[i + dist]) for r in ALONG for i in range(...  10.1 us
    ppermute x3, starting transfers between devices, ahead(): lax.ppermute(x, AXES, [(r[i], r[i + dist]) for r in ALONG for i in range(...  5.17 us
    ppermute x3, waiting for transfers between devices, behind(): lax.ppermute(x, AXES, [(r[i + dist], r[i]) for r in ALONG for i in range(...  5.15 us
    ppermute x3, starting transfers between devices, behind(): lax.ppermute(x, AXES, [(r[i + dist], r[i]) for r in ALONG for i in range(...  3.89 us
    pallas_call x1, Pallas kernels, pack(): pl.pallas_call(pack_kernel, out_shape=shape(HEADS, WIDE, HD), in_specs=[p...  2.71 us
  transfers between devices with their start and end apart: 9, of which 3 were waited for; matrix products, arithmetic and copies ran while one was open for 0% of the time, Pallas kernels for 7%

profile of v6, /device:TPU:176, one launch (start us, length us, event | category | flops | bytes accessed | tf_op | source)
XLA Modules:
  0.0 88.7 jit_solution(8831347406161200082)
XLA Ops:
  0.6 2.7 %shard_map.84 = bf16[8,320,128]{2,1,0:T(8,128)(2,1)} custom-call(s32[8]{0:T(128)} %shift_ref.1, bf16[256,128]{1,0:T(8,128)(2,1)} %bitcast.12, bf16[256,128]{1,0:T(8,128)(2,1)} %bitcast.13, bf16[1024,128]{1,0:T(8,128)(2,1)} %bitcast.10, bf16[1024,128]{1,0:T(8,128)(2,1)} %bitcast.11), custom_call_target="tpu_custom_call" | custom-call | tf_op jit(solution)/shard_map/pallas_call | solution.py:340
  3.4 17.7 %all_to_all.10.all_ref = bf16[8,320,128]{2,1,0:T(8,128)(2,1)S(1)} all-to-all(bf16[8,320,128]{2,1,0:T(8,128)(2,1)} %shard_map.84), channel_id=1, replica_groups=mesh['seq'=64,'head'=8] {'head'}, dimensions={0} | all-to-all | bytes 1310720 | tf_op jit(solution)/shard_map/all_to_all | solution.py:391
  21.0 1.9 %collective-permute-start.3 = (bf16[8,256,128]{2,1,0:T(8,128)(2,1)S(1)}, bf16[8,256,128]{2,1,0:T(8,128)(2,1)S(1)}, u32[]{:S(2)}, u32[]{:S(2)}) collective-permute-start(bf16[8,256,128]{2,1,0:T(8,128)(2,1)S(1)} %slice.9), channel_id=1, source_target_pairs={{0,8},{1,9},{2,10},{3,11},{4,12},{5,13},{6,14},{7,15},{8,0},{9,1},... | collective-permute-start | bytes 1572872 | tf_op jit(solution)/shard_map/ppermute | solution.py:394
  23.0 0.1 pad_add_fusion.where_ref
  23.1 0.7 collective-permute-start.2
  23.7 1.3 %collective-permute-start.1 = (bf16[8,64,128]{2,1,0:T(8,128)(2,1)S(1)}, bf16[8,64,128]{2,1,0:T(8,128)(2,1)S(1)}, u32[]{:S(2)}, u32[]{:S(2)}) collective-permute-start(bf16[8,64,128]{2,1,0:T(8,128)(2,1)S(1)} %slice.8), channel_id=1, source_target_pairs={{0,32},{16,48},{1,33},{17,49},{2,34},{18,50},{3,35},{19,51},{36,68... | collective-permute-start | bytes 393224 | tf_op jit(solution)/shard_map/ppermute | solution.py:372
  25.0 3.2 %collective-permute-start = (bf16[8,64,128]{2,1,0:T(8,128)(2,1)S(1)}, bf16[8,64,128]{2,1,0:T(8,128)(2,1)S(1)}, u32[]{:S(2)}, u32[]{:S(2)}) collective-permute-start(bf16[8,64,128]{2,1,0:T(8,128)(2,1)S(1)} %slice.8), channel_id=1, source_target_pairs={{0,16},{16,32},{32,48},{1,17},{17,33},{33,49},{2,18},{18,34},{34,5... | collective-permute-start | bytes 393224 | tf_op jit(solution)/shard_map/ppermute | solution.py:372
  28.3 0.0 collective-permute-done.3.swapped_ref
  28.3 1.3 %shard_map.85 = (bf16[128,2048]{1,0:T(8,128)(2,1)S(1)}, bf16[128,2048]{1,0:T(8,128)(2,1)S(1)}, f32[256,2048]{1,0:T(8,128)S(1)}, f32[256,2048]{1,0:T(8,128)S(1)},...) custom-call(s32[2]{0:T(128)S(1)} %pad_add_fusion.where_ref, ...), custom_call_target="tpu_custom_call" | custom-call | flops 10000000000 | bytes 1048576 | tf_op jit(solution)/shard_map/pallas_call | solution.py:328
  29.6 0.0 collective-permute-done.2.a3
  29.6 0.6 shard_map.86
  30.2 5.0 %collective-permute-done.1.a2 = bf16[8,64,128]{2,1,0:T(8,128)(2,1)S(1)} collective-permute-done((bf16[8,64,128]{2,1,0:T(8,128)(2,1)S(1)}, bf16[8,64,128]{2,1,0:T(8,128)(2,1)S(1)}, u32[]{:S(2)}, u32[]{:S(2)}) %collective-permute-start.1) | collective-permute-done | bytes 131104 | tf_op jit(solution)/shard_map/ppermute | solution.py:372
  35.1 5.2 %collective-permute-done.a1 = bf16[8,64,128]{2,1,0:T(8,128)(2,1)S(1)} collective-permute-done((bf16[8,64,128]{2,1,0:T(8,128)(2,1)S(1)}, bf16[8,64,128]{2,1,0:T(8,128)(2,1)S(1)}, u32[]{:S(2)}, u32[]{:S(2)}) %collective-permute-start) | collective-permute-done | bytes 131104 | tf_op jit(solution)/shard_map/ppermute | solution.py:372
  40.3 3.1 %shard_map.87 = (f32[4,256,2048]{2,1,0:T(8,128)S(1)}, f32[2,256,2048]{2,1,0:T(8,128)S(1)}, f32[8,2048]{1,0:T(8,128)S(1)}) custom-call(s32[2]{0:T(128)S(1)} %pad_add_fusion.where_ref, bf16[128,2048]{1,0:T(8,128)(2,1)S(1)} %get-tuple-element.30.qt_ref, bf16[128,2048]{1,0:T(8,128)(2,1)S(1)} %get-tuple-element.31.dt_ref, ...), custom_call_target="tpu_custom_call" | custom-call | tf_op jit(solution)/shard_map/pallas_call | solution.py:328
  43.5 2.0 %collective-permute-start.4 = (f32[8,2048]{1,0:T(8,128)S(1)}, f32[8,2048]{1,0:T(8,128)S(1)}, u32[]{:S(2)}, u32[]{:S(2)}) collective-permute-start(f32[8,2048]{1,0:T(8,128)S(1)} %get-tuple-element.38.stats_ref), channel_id=1, source_target_pairs={{0,8},{1,9},{2,10},{3,11},{4,12},{5,13},{6,14},{7,15},{8,0},{9,1},... | collective-permute-start | bytes 196616 | tf_op jit(solution)/shard_map/ppermute | solution.py:412
  45.4 1.5 %shard_map.89.o_ref = f32[128,2048]{1,0:T(8,128)S(1)} custom-call(s32[2]{0:T(128)S(1)} %pad_add_fusion.where_ref, bf16[8,320,128]{2,1,0:T(8,128)(2,1)S(1)} %all_to_all.10.all_ref, bf16[8,64,128]{2,1,0:T(8,128)(2,1)S(1)} %collective-permute-done.a1, bf16[8,64,128]{2,1,0:T(8,128)(2,1)S(1)} %collective-permute-done.1.a2, ...), custom_call_target="tpu_custom_call" | custom-call | flops 10000000000 | bytes 1048576 | tf_op jit(solution)/shard_map/pallas_call | solution.py:328
  47.0 0.0 collective-permute-done.4.swapped_stats_ref
  47.0 2.3 %shard_map.88 = (bf16[8,64,128]{2,1,0:T(8,128)(2,1)S(1)}, bf16[8,64,128]{2,1,0:T(8,128)(2,1)S(1)}, bf16[8,64,128]{2,1,0:T(8,128)(2,1)S(1)}, bf16[3,256,2048]{2,1...) custom-call(s32[2]{0:T(128)S(1)} %pad_add_fusion.where_ref, ...), custom_call_target="tpu_custom_call" | custom-call | tf_op jit(solution)/shard_map/pallas_call | solution.py:328
  49.2 1.9 %collective-permute-start.5 = (bf16[8,64,128]{2,1,0:T(8,128)(2,1)S(1)}, bf16[8,64,128]{2,1,0:T(8,128)(2,1)S(1)}, u32[]{:S(2)}, u32[]{:S(2)}) collective-permute-start(bf16[8,64,128]{2,1,0:T(8,128)(2,1)S(1)} %get-tuple-element.47), channel_id=1, source_target_pairs={{16,0},{32,16},{48,32},{17,1},{33,17},{49,33},{18,2},{34,18},{50,3... | collective-permute-start | bytes 393224 | tf_op jit(solution)/shard_map/ppermute | solution.py:376
  51.2 1.3 %collective-permute-start.6 = (bf16[8,64,128]{2,1,0:T(8,128)(2,1)S(1)}, bf16[8,64,128]{2,1,0:T(8,128)(2,1)S(1)}, u32[]{:S(2)}, u32[]{:S(2)}) collective-permute-start(bf16[8,64,128]{2,1,0:T(8,128)(2,1)S(1)} %get-tuple-element.48), channel_id=1, source_target_pairs={{32,0},{48,16},{33,1},{49,17},{34,2},{50,18},{35,3},{51,19},{68,36... | collective-permute-start | bytes 393224 | tf_op jit(solution)/shard_map/ppermute | solution.py:376
  52.5 0.7 collective-permute-start.7
  53.2 2.6 %shard_map.90 = (f32[8,256,128]{2,1,0:T(8,128)S(1)}, bf16[8,256,128]{2,1,0:T(8,128)(2,1)S(1)}, f32[8,64,128]{2,1,0:T(8,128)S(1)}) custom-call(s32[2]{0:T(128)S(1)} %pad_add_fusion.where_ref, bf16[8,320,128]{2,1,0:T(8,128)(2,1)S(1)} %all_to_all.10.all_ref, bf16[8,64,128]{2,1,0:T(8,128)(2,1)S(1)} %collective-permute-done.a1, ...), custom_call_target="tpu_custom_call" | custom-call | flops 10000000000 | bytes 1048576 | tf_op jit(solution)/shard_map/pallas_call | solution.py:328
  55.7 2.4 %collective-permute-start.8 = (bf16[8,256,128]{2,1,0:T(8,128)(2,1)S(1)}, bf16[8,256,128]{2,1,0:T(8,128)(2,1)S(1)}, u32[]{:S(2)}, u32[]{:S(2)}) collective-permute-start(bf16[8,256,128]{2,1,0:T(8,128)(2,1)S(1)} %get-tuple-element.51), channel_id=1, source_target_pairs={{0,8},{1,9},{2,10},{3,11},{4,12},{5,13},{6,14},{7,15},{8,0},{9,1},... | collective-permute-start | bytes 1572872 | tf_op jit(solution)/shard_map/ppermute | solution.py:435
  58.1 0.0 collective-permute-done.5.c1
  58.1 5.1 %collective-permute-done.6.c2 = bf16[8,64,128]{2,1,0:T(8,128)(2,1)S(1)} collective-permute-done((bf16[8,64,128]{2,1,0:T(8,128)(2,1)S(1)}, bf16[8,64,128]{2,1,0:T(8,128)(2,1)S(1)}, u32[]{:S(2)}, u32[]{:S(2)}) %collective-permute-start.6) | collective-permute-done | bytes 131104 | tf_op jit(solution)/shard_map/ppermute | solution.py:376
  63.2 0.0 collective-permute-done.7.c3
  63.2 0.1 shard_map.91
  63.3 0.0 collective-permute-done.8
  63.3 0.0 copy-start
  63.3 0.1 add_convert_fusion
  63.5 23.4 %all_to_all.11.in_ref = bf16[8,320,128]{2,1,0:T(8,128)(2,1)S(1)} all-to-all(bf16[8,320,128]{2,1,0:T(8,128)(2,1)S(1)} %pad_maximum_fusion), channel_id=1, replica_groups=mesh['seq'=64,'head'=8] {'head'}, dimensions={0} | all-to-all | bytes 1310720 | tf_op jit(solution)/shard_map/all_to_all | solution.py:437
  86.9 1.9 %shard_map.92 = (bf16[1024,128]{1,0:T(8,128)(2,1)}, bf16[1024,128]{1,0:T(8,128)(2,1)}, bf16[256,128]{1,0:T(8,128)(2,1)}, bf16[256,128]{1,0:T(8,128)(2,1)}) custom-call(s32[8]{0:T(128)S(1)} %copy-done, bf16[8,320,128]{2,1,0:T(8,128)(2,1)S(1)} %all_to_all.11.in_ref), custom_call_target="tpu_custom_call" | custom-call | tf_op jit(solution)/shard_map/pallas_call | solution.py:328
  (4 shorter events, 0.1 us)
Async XLA Ops:
  21.0 7.2 %collective-permute-start.3 = (bf16[8,256,128]{2,1,0:T(8,128)(2,1)S(1)}, bf16[8,256,128]{2,1,0:T(8,128)(2,1)S(1)}, u32[]{:S(2)}, u32[]{:S(2)}) collective-permute-start(bf16[8,256,128]{2,1,0:T(8,128)(2,1)S(1)} %slice.9), channel_id=1, source_target_pairs={{0,8},{1,9},{2,10},{3,11},{4,12},{5,13},{6,14},{7,15},{8,0},{9,1},... | collective-permute-start | bytes 1572872 | tf_op jit(solution)/shard_map/ppermute | solution.py:394
  23.1 6.5 %collective-permute-start.2 = (bf16[8,64,128]{2,1,0:T(8,128)(2,1)S(1)}, bf16[8,64,128]{2,1,0:T(8,128)(2,1)S(1)}, u32[]{:S(2)}, u32[]{:S(2)}) collective-permute-start(bf16[8,64,128]{2,1,0:T(8,128)(2,1)S(1)} %slice.8), channel_id=1, source_target_pairs={{0,48},{1,49},{2,50},{3,51},{36,84},{37,85},{38,86},{39,87},{8,56}... | collective-permute-start | bytes 393224 | tf_op jit(solution)/shard_map/ppermute | solution.py:372
  23.7 11.4 %collective-permute-start.1 = (bf16[8,64,128]{2,1,0:T(8,128)(2,1)S(1)}, bf16[8,64,128]{2,1,0:T(8,128)(2,1)S(1)}, u32[]{:S(2)}, u32[]{:S(2)}) collective-permute-start(bf16[8,64,128]{2,1,0:T(8,128)(2,1)S(1)} %slice.8), channel_id=1, source_target_pairs={{0,32},{16,48},{1,33},{17,49},{2,34},{18,50},{3,35},{19,51},{36,68... | collective-permute-start | bytes 393224 | tf_op jit(solution)/shard_map/ppermute | solution.py:372
  25.0 15.3 %collective-permute-start = (bf16[8,64,128]{2,1,0:T(8,128)(2,1)S(1)}, bf16[8,64,128]{2,1,0:T(8,128)(2,1)S(1)}, u32[]{:S(2)}, u32[]{:S(2)}) collective-permute-start(bf16[8,64,128]{2,1,0:T(8,128)(2,1)S(1)} %slice.8), channel_id=1, source_target_pairs={{0,16},{16,32},{32,48},{1,17},{17,33},{33,49},{2,18},{18,34},{34,5... | collective-permute-start | bytes 393224 | tf_op jit(solution)/shard_map/ppermute | solution.py:372
  43.5 3.5 %collective-permute-start.4 = (f32[8,2048]{1,0:T(8,128)S(1)}, f32[8,2048]{1,0:T(8,128)S(1)}, u32[]{:S(2)}, u32[]{:S(2)}) collective-permute-start(f32[8,2048]{1,0:T(8,128)S(1)} %get-tuple-element.38.stats_ref), channel_id=1, source_target_pairs={{0,8},{1,9},{2,10},{3,11},{4,12},{5,13},{6,14},{7,15},{8,0},{9,1},... | collective-permute-start | bytes 196616 | tf_op jit(solution)/shard_map/ppermute | solution.py:412
  49.2 8.8 %collective-permute-start.5 = (bf16[8,64,128]{2,1,0:T(8,128)(2,1)S(1)}, bf16[8,64,128]{2,1,0:T(8,128)(2,1)S(1)}, u32[]{:S(2)}, u32[]{:S(2)}) collective-permute-start(bf16[8,64,128]{2,1,0:T(8,128)(2,1)S(1)} %get-tuple-element.47), channel_id=1, source_target_pairs={{16,0},{32,16},{48,32},{17,1},{33,17},{49,33},{18,2},{34,18},{50,3... | collective-permute-start | bytes 393224 | tf_op jit(solution)/shard_map/ppermute | solution.py:376
  51.2 12.1 %collective-permute-start.6 = (bf16[8,64,128]{2,1,0:T(8,128)(2,1)S(1)}, bf16[8,64,128]{2,1,0:T(8,128)(2,1)S(1)}, u32[]{:S(2)}, u32[]{:S(2)}) collective-permute-start(bf16[8,64,128]{2,1,0:T(8,128)(2,1)S(1)} %get-tuple-element.48), channel_id=1, source_target_pairs={{32,0},{48,16},{33,1},{49,17},{34,2},{50,18},{35,3},{51,19},{68,36... | collective-permute-start | bytes 393224 | tf_op jit(solution)/shard_map/ppermute | solution.py:376
  52.5 10.8 %collective-permute-start.7 = (bf16[8,64,128]{2,1,0:T(8,128)(2,1)S(1)}, bf16[8,64,128]{2,1,0:T(8,128)(2,1)S(1)}, u32[]{:S(2)}, u32[]{:S(2)}) collective-permute-start(bf16[8,64,128]{2,1,0:T(8,128)(2,1)S(1)} %get-tuple-element.49), channel_id=1, source_target_pairs={{48,0},{49,1},{50,2},{51,3},{84,36},{85,37},{86,38},{87,39},{56,8}... | collective-permute-start | bytes 393224 | tf_op jit(solution)/shard_map/ppermute | solution.py:376
  55.7 7.6 %collective-permute-start.8 = (bf16[8,256,128]{2,1,0:T(8,128)(2,1)S(1)}, bf16[8,256,128]{2,1,0:T(8,128)(2,1)S(1)}, u32[]{:S(2)}, u32[]{:S(2)}) collective-permute-start(bf16[8,256,128]{2,1,0:T(8,128)(2,1)S(1)} %get-tuple-element.51), channel_id=1, source_target_pairs={{0,8},{1,9},{2,10},{3,11},{4,12},{5,13},{6,14},{7,15},{8,0},{9,1},... | collective-permute-start | bytes 1572872 | tf_op jit(solution)/shard_map/ppermute | solution.py:435
  63.3 23.6 %copy-start = (s32[8]{0:T(128)S(1)}, s32[8]{0:T(128)}, u32[]{:S(2)}) copy-start(s32[8]{0:T(128)} %shift_ref.1) | copy-start | bytes 100

commit v7 on v6

--- a/solution.py
+++ b/solution.py
@@ -71,13 +71,22 @@
     return jnp.where(same & (place == (placed >> 5)), 1.0, 0.0).astype(BF16)
 
 
-def pack_kernel(shift_hbm, k_hbm, v_hbm, q_hbm, d_hbm, out_ref, shift_ref, k_ref, v_ref, q_ref, d_ref, sems):
+def pack_kernel(
+    shift_hbm, k_hbm, v_hbm, q_hbm, d_hbm, out_hbm, shift_ref, k_ref, v_ref, q_ref, d_ref, kv_s, wide_s, sems
+):
     copies = [
         pltpu.make_async_copy(src, dst, sems.at[n])
         for n, (src, dst) in enumerate(
             ((shift_hbm, shift_ref), (k_hbm, k_ref), (v_hbm, v_ref), (q_hbm, q_ref), (d_hbm, d_ref))
         )
     ]
+    out = [pltpu.make_async_copy(kv_s, out_hbm.at[:, 0:QAT, :], sems.at[5])]
+    for n in range(2):
+        out.append(
+            pltpu.make_async_copy(
+                wide_s.at[n], out_hbm.at[:, QAT + n * 128 : QAT + n * 128 + 128, :], sems.at[6 + n]
+            )
+        )
     for copy in copies:
         copy.start()
     copies[0].wait()
@@ -87,27 +96,38 @@
         copies[n + 1].wait()
         moved = dot(order, ref[...]).astype(BF16)
         for h in range(HEADS):
-            out_ref[h, n * SUB : (n + 1) * SUB, :] = moved[h * SUB : (h + 1) * SUB]
+            kv_s[h, n * SUB : (n + 1) * SUB, :] = moved[h * SUB : (h + 1) * SUB]
+    out[0].start()
     for n, ref in enumerate((q_ref, d_ref)):
         copies[n + 3].wait()
         for b in range(4):
             moved = dot(wide_order, ref[b * TOK : (b + 1) * TOK, :]).astype(BF16)
             for h in range(HEADS):
-                at = QAT + n * 128 + b * 32
-                out_ref[h, at : at + 32, :] = moved[h * 32 : (h + 1) * 32]
-
-
-def unpack_kernel(shift_ref, in_ref, o_ref, q_ref, k_ref, v_ref):
+                wide_s[n, h, b * 32 : b * 32 + 32, :] = moved[h * 32 : (h + 1) * 32]
+        out[n + 1].start()
+    for copy in out:
+        copy.wait()
+
+
+def unpack_kernel(shift_ref, in_ref, o_hbm, q_hbm, k_hbm, v_hbm, o_s, q_s, k_s, v_s, sems):
     order = kv_order(shift_ref, True)
     wide_order = q_order(shift_ref, True)
-    for n, ref in enumerate((k_ref, v_ref)):
-        held = in_ref[:, n * SUB : (n + 1) * SUB, :].reshape(TOK, HD)
-        ref[...] = dot(order, held).astype(BF16)
-    for n, ref in enumerate((o_ref, q_ref)):
+    copies = [
+        pltpu.make_async_copy(src, dst, sems.at[n])
+        for n, (src, dst) in enumerate(((o_s, o_hbm), (q_s, q_hbm), (k_s, k_hbm), (v_s, v_hbm)))
+    ]
+    for n, ref in enumerate((o_s, q_s)):
         for b in range(4):
             at = QAT + n * 128 + b * 32
             held = in_ref[:, at : at + 32, :].reshape(TOK, HD)
             ref[b * TOK : (b + 1) * TOK, :] = dot(wide_order, held).astype(BF16)
+        copies[n].start()
+    for n, ref in enumerate((k_s, v_s)):
+        held = in_ref[:, n * SUB : (n + 1) * SUB, :].reshape(TOK, HD)
+        ref[...] = dot(order, held).astype(BF16)
+        copies[n + 2].start()
+    for copy in copies:
+        copy.wait()
 
 
 def columns():
@@ -324,12 +344,12 @@
     return jax.ShapeDtypeStruct(dims, dtype)
 
 
-def run(kernel, outs, scratch, *operands, first=SM, cost=None):
+def run(kernel, outs, scratch, *operands, first=SM, out=VM, cost=None):
     return pl.pallas_call(
         kernel,
         out_shape=outs,
         in_specs=[first] + [VM] * (len(operands) - 1),
-        out_specs=tuple(VM for _ in outs),
+        out_specs=tuple(out for _ in outs),
         scratch_shapes=scratch,
         compiler_params=params(),
         cost_estimate=cost,
@@ -341,14 +361,16 @@
         pack_kernel,
         out_shape=shape(HEADS, WIDE, HD),
         in_specs=[pl.BlockSpec(memory_space=pl.ANY)] * 5,
-        out_specs=VM,
+        out_specs=pl.BlockSpec(memory_space=pl.ANY),
         scratch_shapes=[
             pltpu.SMEM((HEADS,), jnp.int32),
             pltpu.VMEM((TOK, HD), BF16),
             pltpu.VMEM((TOK, HD), BF16),
             pltpu.VMEM((ROWS, HD), BF16),
             pltpu.VMEM((ROWS, HD), BF16),
-            pltpu.SemaphoreType.DMA((5,)),
+            pltpu.VMEM((HEADS, QAT, HD), BF16),
+            pltpu.VMEM((2, HEADS, 128, HD), BF16),
+            pltpu.SemaphoreType.DMA((8,)),
         ],
         compiler_params=pltpu.CompilerParams(vmem_limit_bytes=60 * 1024 * 1024),
     )(shift, k, v, q, d)
@@ -438,9 +460,16 @@
     attended, d_queries, d_keys, d_values = run(
         unpack_kernel,
         (shape(ROWS, HD), shape(ROWS, HD), shape(TOK, HD), shape(TOK, HD)),
-        [],
+        [
+            pltpu.VMEM((ROWS, HD), BF16),
+            pltpu.VMEM((ROWS, HD), BF16),
+            pltpu.VMEM((TOK, HD), BF16),
+            pltpu.VMEM((TOK, HD), BF16),
+            pltpu.SemaphoreType.DMA((4,)),
+        ],
         shift_amounts,
         done,
+        out=pl.BlockSpec(memory_space=pl.ANY),
     )
     return (
         attended.reshape(SUB, HEADS, PER, HD),

time: 89.2 us -> 89.1 us (level)
  no operation moved by 1% of the time
where the time goes in v7:
time: 89.1 us; the launch traced here: 88.6 us
  blocking collectives  41.1 us (46%)
  Pallas kernels  15.8 us (18%)
  starting transfers between devices  15.3 us (17%)
  waiting for transfers between devices  15.3 us (17%)
    all_to_all x1, blocking collectives, local(): lax.all_to_all(jnp.concatenate((grads, oq), axis=1), 'head', 0, 0, tiled=...  23.5 us
    all_to_all x1, blocking collectives, local(): everything = lax.all_to_all(packed, 'head', 0, 0, tiled=True)  17.7 us
    pallas_call x8, Pallas kernels, run(): pl.pallas_call(kernel, out_shape=outs, in_specs=[first] + [VM] * (len(ope...  13.2 us
    ppermute x3, waiting for transfers between devices, ahead(): lax.ppermute(x, AXES, [(r[i], r[i + dist]) for r in ALONG for i in range(...  10.2 us
    ppermute x3, starting transfers between devices, ahead(): lax.ppermute(x, AXES, [(r[i], r[i + dist]) for r in ALONG for i in range(...  5.17 us
    ppermute x3, waiting for transfers between devices, behind(): lax.ppermute(x, AXES, [(r[i + dist], r[i]) for r in ALONG for i in range(...  5.14 us
    ppermute x3, starting transfers between devices, behind(): lax.ppermute(x, AXES, [(r[i + dist], r[i]) for r in ALONG for i in range(...  3.89 us
    pallas_call x1, Pallas kernels, pack(): pl.pallas_call(pack_kernel, out_shape=shape(HEADS, WIDE, HD), in_specs=[p...  2.61 us
  transfers between devices with their start and end apart: 9, of which 3 were waited for; matrix products, arithmetic and copies ran while one was open for 0% of the time, Pallas kernels for 7%

profile of v7, /device:TPU:176, one launch (start us, length us, event | category | flops | bytes accessed | tf_op | source)
XLA Modules:
  0.0 88.6 jit_solution(13666290682280217475)
XLA Ops:
  0.6 2.6 %shard_map.84 = bf16[8,320,128]{2,1,0:T(8,128)(2,1)} custom-call(s32[8]{0:T(128)} %shift_ref.1, bf16[256,128]{1,0:T(8,128)(2,1)} %bitcast.12, bf16[256,128]{1,0:T(8,128)(2,1)} %bitcast.13, bf16[1024,128]{1,0:T(8,128)(2,1)} %bitcast.10, bf16[1024,128]{1,0:T(8,128)(2,1)} %bitcast.11), custom_call_target="tpu_custom_call" | custom-call | tf_op jit(solution)/shard_map/pallas_call | solution.py:360
  3.3 17.7 %all_to_all.10.all_ref = bf16[8,320,128]{2,1,0:T(8,128)(2,1)S(1)} all-to-all(bf16[8,320,128]{2,1,0:T(8,128)(2,1)} %shard_map.84), channel_id=1, replica_groups=mesh['seq'=64,'head'=8] {'head'}, dimensions={0} | all-to-all | bytes 1310720 | tf_op jit(solution)/shard_map/all_to_all | solution.py:413
  20.9 1.9 %collective-permute-start.3 = (bf16[8,256,128]{2,1,0:T(8,128)(2,1)S(1)}, bf16[8,256,128]{2,1,0:T(8,128)(2,1)S(1)}, u32[]{:S(2)}, u32[]{:S(2)}) collective-permute-start(bf16[8,256,128]{2,1,0:T(8,128)(2,1)S(1)} %slice.9), channel_id=1, source_target_pairs={{0,8},{1,9},{2,10},{3,11},{4,12},{5,13},{6,14},{7,15},{8,0},{9,1},... | collective-permute-start | bytes 1572872 | tf_op jit(solution)/shard_map/ppermute | solution.py:416
  22.9 0.1 pad_add_fusion.where_ref
  23.0 0.7 collective-permute-start.2
  23.6 1.3 %collective-permute-start.1 = (bf16[8,64,128]{2,1,0:T(8,128)(2,1)S(1)}, bf16[8,64,128]{2,1,0:T(8,128)(2,1)S(1)}, u32[]{:S(2)}, u32[]{:S(2)}) collective-permute-start(bf16[8,64,128]{2,1,0:T(8,128)(2,1)S(1)} %slice.8), channel_id=1, source_target_pairs={{0,32},{16,48},{1,33},{17,49},{2,34},{18,50},{3,35},{19,51},{36,68... | collective-permute-start | bytes 393224 | tf_op jit(solution)/shard_map/ppermute | solution.py:394
  24.9 3.2 %collective-permute-start = (bf16[8,64,128]{2,1,0:T(8,128)(2,1)S(1)}, bf16[8,64,128]{2,1,0:T(8,128)(2,1)S(1)}, u32[]{:S(2)}, u32[]{:S(2)}) collective-permute-start(bf16[8,64,128]{2,1,0:T(8,128)(2,1)S(1)} %slice.8), channel_id=1, source_target_pairs={{0,16},{16,32},{32,48},{1,17},{17,33},{33,49},{2,18},{18,34},{34,5... | collective-permute-start | bytes 393224 | tf_op jit(solution)/shard_map/ppermute | solution.py:394
  28.2 0.0 collective-permute-done.3.swapped_ref
  28.2 1.3 %shard_map.85 = (bf16[128,2048]{1,0:T(8,128)(2,1)S(1)}, bf16[128,2048]{1,0:T(8,128)(2,1)S(1)}, f32[256,2048]{1,0:T(8,128)S(1)}, f32[256,2048]{1,0:T(8,128)S(1)},...) custom-call(s32[2]{0:T(128)S(1)} %pad_add_fusion.where_ref, ...), custom_call_target="tpu_custom_call" | custom-call | flops 10000000000 | bytes 1048576 | tf_op jit(solution)/shard_map/pallas_call | solution.py:348
  29.5 0.0 collective-permute-done.2.a3
  29.5 0.6 shard_map.86
  30.1 5.0 %collective-permute-done.1.a2 = bf16[8,64,128]{2,1,0:T(8,128)(2,1)S(1)} collective-permute-done((bf16[8,64,128]{2,1,0:T(8,128)(2,1)S(1)}, bf16[8,64,128]{2,1,0:T(8,128)(2,1)S(1)}, u32[]{:S(2)}, u32[]{:S(2)}) %collective-permute-start.1) | collective-permute-done | bytes 131104 | tf_op jit(solution)/shard_map/ppermute | solution.py:394
  35.0 5.2 %collective-permute-done.a1 = bf16[8,64,128]{2,1,0:T(8,128)(2,1)S(1)} collective-permute-done((bf16[8,64,128]{2,1,0:T(8,128)(2,1)S(1)}, bf16[8,64,128]{2,1,0:T(8,128)(2,1)S(1)}, u32[]{:S(2)}, u32[]{:S(2)}) %collective-permute-start) | collective-permute-done | bytes 131104 | tf_op jit(solution)/shard_map/ppermute | solution.py:394
  40.2 3.1 %shard_map.87 = (f32[4,256,2048]{2,1,0:T(8,128)S(1)}, f32[2,256,2048]{2,1,0:T(8,128)S(1)}, f32[8,2048]{1,0:T(8,128)S(1)}) custom-call(s32[2]{0:T(128)S(1)} %pad_add_fusion.where_ref, bf16[128,2048]{1,0:T(8,128)(2,1)S(1)} %get-tuple-element.30.qt_ref, bf16[128,2048]{1,0:T(8,128)(2,1)S(1)} %get-tuple-element.31.dt_ref, ...), custom_call_target="tpu_custom_call" | custom-call | tf_op jit(solution)/shard_map/pallas_call | solution.py:348
  43.4 2.0 %collective-permute-start.4 = (f32[8,2048]{1,0:T(8,128)S(1)}, f32[8,2048]{1,0:T(8,128)S(1)}, u32[]{:S(2)}, u32[]{:S(2)}) collective-permute-start(f32[8,2048]{1,0:T(8,128)S(1)} %get-tuple-element.38.stats_ref), channel_id=1, source_target_pairs={{0,8},{1,9},{2,10},{3,11},{4,12},{5,13},{6,14},{7,15},{8,0},{9,1},... | collective-permute-start | bytes 196616 | tf_op jit(solution)/shard_map/ppermute | solution.py:434
  45.3 1.5 %shard_map.89.o_ref = f32[128,2048]{1,0:T(8,128)S(1)} custom-call(s32[2]{0:T(128)S(1)} %pad_add_fusion.where_ref, bf16[8,320,128]{2,1,0:T(8,128)(2,1)S(1)} %all_to_all.10.all_ref, bf16[8,64,128]{2,1,0:T(8,128)(2,1)S(1)} %collective-permute-done.a1, bf16[8,64,128]{2,1,0:T(8,128)(2,1)S(1)} %collective-permute-done.1.a2, ...), custom_call_target="tpu_custom_call" | custom-call | flops 10000000000 | bytes 1048576 | tf_op jit(solution)/shard_map/pallas_call | solution.py:348
  46.9 0.0 collective-permute-done.4.swapped_stats_ref
  46.9 2.3 %shard_map.88 = (bf16[8,64,128]{2,1,0:T(8,128)(2,1)S(1)}, bf16[8,64,128]{2,1,0:T(8,128)(2,1)S(1)}, bf16[8,64,128]{2,1,0:T(8,128)(2,1)S(1)}, bf16[3,256,2048]{2,1...) custom-call(s32[2]{0:T(128)S(1)} %pad_add_fusion.where_ref, ...), custom_call_target="tpu_custom_call" | custom-call | tf_op jit(solution)/shard_map/pallas_call | solution.py:348
  49.1 1.9 %collective-permute-start.5 = (bf16[8,64,128]{2,1,0:T(8,128)(2,1)S(1)}, bf16[8,64,128]{2,1,0:T(8,128)(2,1)S(1)}, u32[]{:S(2)}, u32[]{:S(2)}) collective-permute-start(bf16[8,64,128]{2,1,0:T(8,128)(2,1)S(1)} %get-tuple-element.47), channel_id=1, source_target_pairs={{16,0},{32,16},{48,32},{17,1},{33,17},{49,33},{18,2},{34,18},{50,3... | collective-permute-start | bytes 393224 | tf_op jit(solution)/shard_map/ppermute | solution.py:398
  51.1 1.3 %collective-permute-start.6 = (bf16[8,64,128]{2,1,0:T(8,128)(2,1)S(1)}, bf16[8,64,128]{2,1,0:T(8,128)(2,1)S(1)}, u32[]{:S(2)}, u32[]{:S(2)}) collective-permute-start(bf16[8,64,128]{2,1,0:T(8,128)(2,1)S(1)} %get-tuple-element.48), channel_id=1, source_target_pairs={{32,0},{48,16},{33,1},{49,17},{34,2},{50,18},{35,3},{51,19},{68,36... | collective-permute-start | bytes 393224 | tf_op jit(solution)/shard_map/ppermute | solution.py:398
  52.4 0.7 collective-permute-start.7
  53.0 2.5 %shard_map.90 = (f32[8,256,128]{2,1,0:T(8,128)S(1)}, bf16[8,256,128]{2,1,0:T(8,128)(2,1)S(1)}, f32[8,64,128]{2,1,0:T(8,128)S(1)}) custom-call(s32[2]{0:T(128)S(1)} %pad_add_fusion.where_ref, bf16[8,320,128]{2,1,0:T(8,128)(2,1)S(1)} %all_to_all.10.all_ref, bf16[8,64,128]{2,1,0:T(8,128)(2,1)S(1)} %collective-permute-done.a1, ...), custom_call_target="tpu_custom_call" | custom-call | flops 10000000000 | bytes 1048576 | tf_op jit(solution)/shard_map/pallas_call | solution.py:348
  55.6 2.4 %collective-permute-start.8 = (bf16[8,256,128]{2,1,0:T(8,128)(2,1)S(1)}, bf16[8,256,128]{2,1,0:T(8,128)(2,1)S(1)}, u32[]{:S(2)}, u32[]{:S(2)}) collective-permute-start(bf16[8,256,128]{2,1,0:T(8,128)(2,1)S(1)} %get-tuple-element.51), channel_id=1, source_target_pairs={{0,8},{1,9},{2,10},{3,11},{4,12},{5,13},{6,14},{7,15},{8,0},{9,1},... | collective-permute-start | bytes 1572872 | tf_op jit(solution)/shard_map/ppermute | solution.py:457
  58.0 0.0 collective-permute-done.5.c1
  58.0 5.1 %collective-permute-done.6.c2 = bf16[8,64,128]{2,1,0:T(8,128)(2,1)S(1)} collective-permute-done((bf16[8,64,128]{2,1,0:T(8,128)(2,1)S(1)}, bf16[8,64,128]{2,1,0:T(8,128)(2,1)S(1)}, u32[]{:S(2)}, u32[]{:S(2)}) %collective-permute-start.6) | collective-permute-done | bytes 131104 | tf_op jit(solution)/shard_map/ppermute | solution.py:398
  63.1 0.0 collective-permute-done.7.c3
  63.1 0.1 shard_map.91
  63.2 0.0 collective-permute-done.8
  63.2 0.0 copy-start
  63.2 0.1 add_convert_fusion
  63.4 23.5 %all_to_all.11.in_ref = bf16[8,320,128]{2,1,0:T(8,128)(2,1)S(1)} all-to-all(bf16[8,320,128]{2,1,0:T(8,128)(2,1)S(1)} %pad_maximum_fusion), channel_id=1, replica_groups=mesh['seq'=64,'head'=8] {'head'}, dimensions={0} | all-to-all | bytes 1310720 | tf_op jit(solution)/shard_map/all_to_all | solution.py:459
  86.8 1.8 %shard_map.92 = (bf16[1024,128]{1,0:T(8,128)(2,1)}, bf16[1024,128]{1,0:T(8,128)(2,1)}, bf16[256,128]{1,0:T(8,128)(2,1)}, bf16[256,128]{1,0:T(8,128)(2,1)}) custom-call(s32[8]{0:T(128)S(1)} %copy-done, bf16[8,320,128]{2,1,0:T(8,128)(2,1)S(1)} %all_to_all.11.in_ref), custom_call_target="tpu_custom_call" | custom-call | tf_op jit(solution)/shard_map/pallas_call | solution.py:348
  (4 shorter events, 0.1 us)
Async XLA Ops:
  20.9 7.2 %collective-permute-start.3 = (bf16[8,256,128]{2,1,0:T(8,128)(2,1)S(1)}, bf16[8,256,128]{2,1,0:T(8,128)(2,1)S(1)}, u32[]{:S(2)}, u32[]{:S(2)}) collective-permute-start(bf16[8,256,128]{2,1,0:T(8,128)(2,1)S(1)} %slice.9), channel_id=1, source_target_pairs={{0,8},{1,9},{2,10},{3,11},{4,12},{5,13},{6,14},{7,15},{8,0},{9,1},... | collective-permute-start | bytes 1572872 | tf_op jit(solution)/shard_map/ppermute | solution.py:416
  23.0 6.5 %collective-permute-start.2 = (bf16[8,64,128]{2,1,0:T(8,128)(2,1)S(1)}, bf16[8,64,128]{2,1,0:T(8,128)(2,1)S(1)}, u32[]{:S(2)}, u32[]{:S(2)}) collective-permute-start(bf16[8,64,128]{2,1,0:T(8,128)(2,1)S(1)} %slice.8), channel_id=1, source_target_pairs={{0,48},{1,49},{2,50},{3,51},{36,84},{37,85},{38,86},{39,87},{8,56}... | collective-permute-start | bytes 393224 | tf_op jit(solution)/shard_map/ppermute | solution.py:394
  23.6 11.4 %collective-permute-start.1 = (bf16[8,64,128]{2,1,0:T(8,128)(2,1)S(1)}, bf16[8,64,128]{2,1,0:T(8,128)(2,1)S(1)}, u32[]{:S(2)}, u32[]{:S(2)}) collective-permute-start(bf16[8,64,128]{2,1,0:T(8,128)(2,1)S(1)} %slice.8), channel_id=1, source_target_pairs={{0,32},{16,48},{1,33},{17,49},{2,34},{18,50},{3,35},{19,51},{36,68... | collective-permute-start | bytes 393224 | tf_op jit(solution)/shard_map/ppermute | solution.py:394
  24.9 15.3 %collective-permute-start = (bf16[8,64,128]{2,1,0:T(8,128)(2,1)S(1)}, bf16[8,64,128]{2,1,0:T(8,128)(2,1)S(1)}, u32[]{:S(2)}, u32[]{:S(2)}) collective-permute-start(bf16[8,64,128]{2,1,0:T(8,128)(2,1)S(1)} %slice.8), channel_id=1, source_target_pairs={{0,16},{16,32},{32,48},{1,17},{17,33},{33,49},{2,18},{18,34},{34,5... | collective-permute-start | bytes 393224 | tf_op jit(solution)/shard_map/ppermute | solution.py:394
  43.4 3.5 %collective-permute-start.4 = (f32[8,2048]{1,0:T(8,128)S(1)}, f32[8,2048]{1,0:T(8,128)S(1)}, u32[]{:S(2)}, u32[]{:S(2)}) collective-permute-start(f32[8,2048]{1,0:T(8,128)S(1)} %get-tuple-element.38.stats_ref), channel_id=1, source_target_pairs={{0,8},{1,9},{2,10},{3,11},{4,12},{5,13},{6,14},{7,15},{8,0},{9,1},... | collective-permute-start | bytes 196616 | tf_op jit(solution)/shard_map/ppermute | solution.py:434
  49.1 8.8 %collective-permute-start.5 = (bf16[8,64,128]{2,1,0:T(8,128)(2,1)S(1)}, bf16[8,64,128]{2,1,0:T(8,128)(2,1)S(1)}, u32[]{:S(2)}, u32[]{:S(2)}) collective-permute-start(bf16[8,64,128]{2,1,0:T(8,128)(2,1)S(1)} %get-tuple-element.47), channel_id=1, source_target_pairs={{16,0},{32,16},{48,32},{17,1},{33,17},{49,33},{18,2},{34,18},{50,3... | collective-permute-start | bytes 393224 | tf_op jit(solution)/shard_map/ppermute | solution.py:398
  51.1 12.0 %collective-permute-start.6 = (bf16[8,64,128]{2,1,0:T(8,128)(2,1)S(1)}, bf16[8,64,128]{2,1,0:T(8,128)(2,1)S(1)}, u32[]{:S(2)}, u32[]{:S(2)}) collective-permute-start(bf16[8,64,128]{2,1,0:T(8,128)(2,1)S(1)} %get-tuple-element.48), channel_id=1, source_target_pairs={{32,0},{48,16},{33,1},{49,17},{34,2},{50,18},{35,3},{51,19},{68,36... | collective-permute-start | bytes 393224 | tf_op jit(solution)/shard_map/ppermute | solution.py:398
  52.4 10.7 %collective-permute-start.7 = (bf16[8,64,128]{2,1,0:T(8,128)(2,1)S(1)}, bf16[8,64,128]{2,1,0:T(8,128)(2,1)S(1)}, u32[]{:S(2)}, u32[]{:S(2)}) collective-permute-start(bf16[8,64,128]{2,1,0:T(8,128)(2,1)S(1)} %get-tuple-element.49), channel_id=1, source_target_pairs={{48,0},{49,1},{50,2},{51,3},{84,36},{85,37},{86,38},{87,39},{56,8}... | collective-permute-start | bytes 393224 | tf_op jit(solution)/shard_map/ppermute | solution.py:398
  55.6 7.6 %collective-permute-start.8 = (bf16[8,256,128]{2,1,0:T(8,128)(2,1)S(1)}, bf16[8,256,128]{2,1,0:T(8,128)(2,1)S(1)}, u32[]{:S(2)}, u32[]{:S(2)}) collective-permute-start(bf16[8,256,128]{2,1,0:T(8,128)(2,1)S(1)} %get-tuple-element.51), channel_id=1, source_target_pairs={{0,8},{1,9},{2,10},{3,11},{4,12},{5,13},{6,14},{7,15},{8,0},{9,1},... | collective-permute-start | bytes 1572872 | tf_op jit(solution)/shard_map/ppermute | solution.py:457
  63.2 23.6 %copy-start = (s32[8]{0:T(128)S(1)}, s32[8]{0:T(128)}, u32[]{:S(2)}) copy-start(s32[8]{0:T(128)} %shift_ref.1) | copy-start | bytes 100

commit v8 on v7

--- a/solution.py
+++ b/solution.py
@@ -138,29 +138,32 @@
     return op(x.reshape(TOK // 8, 8, COLS), axis=0)
 
 
-def rows_of(all_ref, swapped_ref, at):
-    mine = all_ref[:, QAT + at : QAT + at + 128, :].reshape(ROWS, HD)
-    return mine, swapped_ref[:, at : at + 128, :].reshape(ROWS, HD)
-
-
-def first_kernel(where_ref, all_ref, swapped_ref, qt_ref, dt_ref, s_ref, dp_ref, m_ref, q_ref, d_ref):
-    core = where_ref[1]
-    for ref, rows_ref, at in ((qt_ref, q_ref, 0), (dt_ref, d_ref, 128)):
-        mine, other = rows_of(all_ref, swapped_ref, at)
-        rows_ref[0:ROWS, :] = mine
-        rows_ref[ROWS:BOTH, :] = other
-        ref[:, 0:ROWS] = mine.T
-        ref[:, ROWS:BOTH] = other.T
+def halves():
+    return [slice(c * COLS, (c + 1) * COLS) for c in range(ROWS // COLS)]
+
+
+def past(at):
+    return slice(ROWS + at.start, ROWS + at.stop)
+
+
+def rows_at(all_ref, swapped_ref, at, which):
+    start = at.start % ROWS // 128
+    held = slice(start, start + COLS // 128)
+    if at.start < ROWS:
+        return all_ref[held, QAT + which : QAT + which + 128, :].reshape(COLS, HD)
+    return swapped_ref[held, which : which + 128, :].reshape(COLS, HD)
+
+
+def first_kernel(all_ref, qt_ref, dt_ref, s_ref, dp_ref, m_ref):
+    for ref, at in ((qt_ref, QAT), (dt_ref, QAT + 128)):
+        ref[...] = all_ref[:, at : at + 128, :].reshape(ROWS, HD).T
     keys = all_ref[:, 0:SUB, :].reshape(TOK, HD)
     vals = all_ref[:, SUB : 2 * SUB, :].reshape(TOK, HD)
-    for c, at in enumerate(columns()):
+    for at in halves():
         s = dot(keys, qt_ref[:, at])
         u = lax.broadcasted_iota(jnp.int32, (TOK, COLS), 0)
-        if c * COLS < ROWS:
-            limit = (lax.broadcasted_iota(jnp.int32, (TOK, COLS), 1) + c * COLS) >> 2
-        else:
-            limit = jnp.where(core == 0, TOK, -1)
-        s = jnp.where(u <= limit, s, NEG)
+        t = (lax.broadcasted_iota(jnp.int32, (TOK, COLS), 1) + at.start) >> 2
+        s = jnp.where(u <= t, s, NEG)
         s_ref[:, at] = s
         m_ref[:, at] = fold(s, jnp.max)
         dp_ref[:, at] = dot(vals, dt_ref[:, at])
@@ -173,7 +176,7 @@
     def _():
         keys = a3[:, 0:SUB, :].reshape(TOK, HD)
         vals = a3[:, SUB : 2 * SUB, :].reshape(TOK, HD)
-        for at in columns():
+        for at in halves():
             s = dot(keys, qt_ref[:, at])
             s_ref[:, at] = s
             m_ref[:, at] = fold(s, jnp.max)
@@ -181,56 +184,76 @@
 
     @pl.when(chips < 3)
     def _():
-        m_ref[...] = jnp.full((8, BOTH), NEG, F32)
+        m_ref[...] = jnp.full((8, ROWS), NEG, F32)
 
 
 def probs_kernel(
-    where_ref, qt_ref, dt_ref, s0_ref, dp0_ref, m0_ref, s3_ref, dp3_ref, m3_ref, a1, a2,
-    p_ref, dp_ref, stats_ref, k_s, v_s, m_s, l_s, r_s,
+    where_ref, all_ref, sw_ref, qt_ref, dt_ref, s0_ref, dp0_ref, m0_ref, s3_ref, dp3_ref, m3_ref, a1, a2, a3,
+    p_ref, dpm_ref, dpo_ref, stats_ref, k_s, v_s, qo_s, do_s, m_s, l_s, r_s,
 ):
     chips = where_ref[0]
+    core = where_ref[1]
     last = jnp.minimum(chips, 2) + 1
-    for n, ref in enumerate((a1, a2)):
+    for n, ref in enumerate((all_ref, a1, a2, a3)):
         k_s[n] = ref[:, 0:SUB, :].reshape(TOK, HD)
         v_s[n] = ref[:, SUB : 2 * SUB, :].reshape(TOK, HD)
-    m_s[...] = jnp.maximum(m0_ref[...], m3_ref[...])
-
-    def scores(b, _):
-        for at in columns():
-            s = dot(k_s[b - 1], qt_ref[:, at])
-            p_ref[b, :, at] = s
-            m_s[:, at] = jnp.maximum(m_s[:, at], fold(s, jnp.max))
+    qo_s[...] = sw_ref[:, 0:128, :].reshape(ROWS, HD).T
+    do_s[...] = sw_ref[:, 128:256, :].reshape(ROWS, HD).T
+    m_s[:, 0:ROWS] = jnp.maximum(m0_ref[...], m3_ref[...])
+    for at in halves():
+        s = jnp.where(core == 0, dot(k_s[0], qo_s[:, at]), NEG)
+        p_ref[0, :, past(at)] = s
+        m_s[:, past(at)] = fold(s, jnp.max)
+
+    def scores(b, mine):
+        for at in halves():
+            if mine:
+                s = dot(k_s[b], qt_ref[:, at])
+                p_ref[b, :, at] = s
+                m_s[:, at] = jnp.maximum(m_s[:, at], fold(s, jnp.max))
+            s = dot(k_s[b], qo_s[:, at])
+            p_ref[b, :, past(at)] = s
+            m_s[:, past(at)] = jnp.maximum(m_s[:, past(at)], fold(s, jnp.max))
         return 0
 
-    lax.fori_loop(1, last, scores, 0)
+    lax.fori_loop(1, last, lambda b, _: scores(b, True), 0)
+
+    @pl.when(chips == 3)
+    def _():
+        scores(3, False)
+
     top = jnp.max(m_s[...], axis=0, keepdims=True)
     m_s[...] = jnp.broadcast_to(top, (8, BOTH))
 
-    for at in columns():
-        p = jnp.exp2((s0_ref[:, at] - m_s[0:1, at]) * EXPONENT)
-        p_ref[0, :, at] = p
-        l_s[:, at] = fold(p, jnp.sum)
-        r_s[:, at] = fold(p * dp0_ref[:, at], jnp.sum)
-
-    def forward(b, _):
-        for at in columns():
-            p = jnp.exp2((p_ref[b, :, at] - m_s[0:1, at]) * EXPONENT)
-            dp = dot(v_s[b - 1], dt_ref[:, at])
-            p_ref[b, :, at] = p
-            dp_ref[b - 1, :, at] = dp
-            l_s[:, at] += fold(p, jnp.sum)
-            r_s[:, at] += fold(p * dp, jnp.sum)
+    def probs(b, at, s, dp, begin=False):
+        p = jnp.exp2((s - m_s[0:1, at]) * EXPONENT)
+        p_ref[b, :, at] = p
+        total = fold(p, jnp.sum)
+        row = fold(p * dp, jnp.sum)
+        l_s[:, at] = total if begin else l_s[:, at] + total
+        r_s[:, at] = row if begin else r_s[:, at] + row
+
+    def forward(b, mine, begin=False):
+        for at in halves():
+            if mine:
+                dp = dot(v_s[b], dt_ref[:, at])
+                dpm_ref[b - 1, :, at] = dp
+                probs(b, at, p_ref[b, :, at], dp)
+            dp = dot(v_s[b], do_s[:, at])
+            dpo_ref[b, :, at] = dp
+            probs(b, past(at), p_ref[b, :, past(at)], dp, begin)
         return 0
 
-    lax.fori_loop(1, last, forward, 0)
+    for at in halves():
+        probs(0, at, s0_ref[:, at], dp0_ref[:, at], True)
+    forward(0, False, True)
+    lax.fori_loop(1, last, lambda b, _: forward(b, True), 0)
 
     @pl.when(chips == 3)
     def _():
-        for at in columns():
-            p = jnp.exp2((s3_ref[:, at] - m_s[0:1, at]) * EXPONENT)
-            p_ref[3, :, at] = p
-            l_s[:, at] += fold(p, jnp.sum)
-            r_s[:, at] += fold(p * dp3_ref[:, at], jnp.sum)
+        forward(3, False)
+        for at in halves():
+            probs(3, at, s3_ref[:, at], dp3_ref[:, at])
 
     stats_ref[0:1, :] = top
     stats_ref[1:2, :] = jnp.sum(l_s[...], axis=0, keepdims=True)
@@ -253,20 +276,21 @@
     lax.fori_loop(1, chips + 1, add, 0)
 
 
-def key_grads(p_ref, dp_ref, ds_ref, f_ref, r_ref, q_ref, d_ref):
+def key_grads(p_ref, dp_ref, dpo_ref, ds_ref, f_ref, r_ref, all_ref, sw_ref):
     dk = jnp.zeros((TOK, HD), F32)
     dv = jnp.zeros((TOK, HD), F32)
     for at in columns():
+        dp = dp_ref[:, at] if at.start < ROWS else dpo_ref[:, at.start - ROWS : at.stop - ROWS]
         p = p_ref[:, at] * f_ref[0:1, at]
-        ds = (p * (dp_ref[:, at] - r_ref[0:1, at])).astype(BF16)
+        ds = (p * (dp - r_ref[0:1, at])).astype(BF16)
         ds_ref[:, at] = ds
-        dk = dk + dot(ds, q_ref[at, :])
-        dv = dv + dot(p.astype(BF16), d_ref[at, :])
+        dk = dk + dot(ds, rows_at(all_ref, sw_ref, at, 0))
+        dv = dv + dot(p.astype(BF16), rows_at(all_ref, sw_ref, at, 128))
     return dk * SCALING, dv
 
 
 def grads_kernel(
-    where_ref, stats_ref, swapped_stats_ref, q_s, d_s, p_ref, dp_ref, dp3_ref,
+    where_ref, stats_ref, swapped_stats_ref, all_ref, sw_ref, p_ref, dp_ref, dp3_ref, dpo_ref,
     c1, c2, c3, ds_ref, f_ref, r_s, g_s,
 ):
     chips = where_ref[0]
@@ -284,7 +308,9 @@
         r_s[:, at] = jnp.broadcast_to(row_dot, (8, ROWS))
 
     def far(b, dp):
-        dk, dv = key_grads(p_ref.at[b], dp, ds_ref.at[b - 1], f_ref, r_s, q_s, d_s)
+        dk, dv = key_grads(
+            p_ref.at[b], dp, dpo_ref.at[b], ds_ref.at[b - 1], f_ref, r_s, all_ref, sw_ref
+        )
         g_s[b - 1, :, 0:SUB, :] = dk.astype(BF16).reshape(HEADS, SUB, HD)
         g_s[b - 1, :, SUB : 2 * SUB, :] = dv.astype(BF16).reshape(HEADS, SUB, HD)
         return 0
@@ -307,11 +333,11 @@
 
 
 def query_kernel(
-    where_ref, all_ref, a1, a2, a3, ds_ref, o_ref, f_ref, r_ref, q_ref, d_ref, p_ref, dp0_ref,
+    where_ref, all_ref, sw_ref, a1, a2, a3, ds_ref, o_ref, f_ref, r_ref, p_ref, dp0_ref, dpo_ref,
     mine_ref, other_ref, own_ref, kt_s, g_s, ds0_s,
 ):
     chips = where_ref[0]
-    dk, dv = key_grads(p_ref.at[0], dp0_ref, ds0_s, f_ref, r_ref, q_ref, d_ref)
+    dk, dv = key_grads(p_ref.at[0], dp0_ref, dpo_ref.at[0], ds0_s, f_ref, r_ref, all_ref, sw_ref)
     own_ref[:, 0:SUB, :] = dk.reshape(HEADS, SUB, HD)
     own_ref[:, SUB : 2 * SUB, :] = dv.reshape(HEADS, SUB, HD)
     for n, ref in enumerate((all_ref, a1, a2, a3)):
@@ -415,21 +441,23 @@
     a = [ahead(own, dist) for dist in (1, 2, 3)]
     swapped = lax.ppermute(everything[:, QAT:WIDE], AXES, SWAP)
     rows = pltpu.VMEM((8, BOTH), F32)
-    wide, tall, flat = shape(TOK, BOTH, dtype=F32), shape(BOTH, HD), shape(8, BOTH, dtype=F32)
-    qt, dt, s0, dp0, m0, q_rows, d_rows = run(
-        first_kernel,
-        (shape(HD, BOTH), shape(HD, BOTH), wide, wide, flat, tall, tall),
-        [],
-        where, everything, swapped,
-        cost=LONG,
-    )
-    s3, dp3, m3 = run(early_kernel, (wide, wide, flat), [], where, qt, dt, a[2], cost=LONG)
-    held = pltpu.VMEM((2, TOK, HD), BF16)
-    probs, dp, stats = run(
+    flat = shape(8, BOTH, dtype=F32)
+    part, half, top = shape(TOK, ROWS, dtype=F32), shape(HD, ROWS), shape(8, ROWS, dtype=F32)
+    qt, dt, s0, dp0, m0 = run(
+        first_kernel, (half, half, part, part, top), [], everything, first=VM, cost=LONG
+    )
+    s3, dp3, m3 = run(early_kernel, (part, part, top), [], where, qt, dt, a[2], cost=LONG)
+    held, turned = pltpu.VMEM((4, TOK, HD), BF16), pltpu.VMEM((HD, ROWS), BF16)
+    probs, dp, dpo, stats = run(
         probs_kernel,
-        (shape(4, TOK, BOTH, dtype=F32), shape(2, TOK, BOTH, dtype=F32), flat),
-        [held, held, rows, rows, rows],
-        where, qt, dt, s0, dp0, m0, s3, dp3, m3, a[0], a[1],
+        (
+            shape(4, TOK, BOTH, dtype=F32),
+            shape(2, TOK, ROWS, dtype=F32),
+            shape(4, TOK, ROWS, dtype=F32),
+            flat,
+        ),
+        [held, held, turned, turned, rows, rows, rows],
+        where, everything, swapped, qt, dt, s0, dp0, m0, s3, dp3, m3, *a,
     )
     swapped_stats = lax.ppermute(stats, AXES, SWAP)
     (o,) = run(
@@ -444,14 +472,14 @@
         grads_kernel,
         (block, block, block, shape(3, TOK, BOTH), flat, flat),
         [pltpu.VMEM((3, HEADS, 2 * SUB, HD), BF16)],
-        where, stats, swapped_stats, q_rows, d_rows, probs, dp, dp3,
+        where, stats, swapped_stats, everything, swapped, probs, dp, dp3, dpo,
     )
     back = [behind(part, dist) for dist, part in zip((1, 2, 3), (c1, c2, c3))]
     mine, other, grads = run(
         query_kernel,
         (shape(HEADS, 256, HD, dtype=F32), shape(HEADS, 256, HD), shape(HEADS, 2 * SUB, HD, dtype=F32)),
         [pltpu.VMEM((4, HD, TOK), BF16), pltpu.VMEM((HD, BOTH), F32), pltpu.VMEM((TOK, BOTH), BF16)],
-        where, everything, *a, ds, o, f, row_dot, q_rows, d_rows, probs, dp0,
+        where, everything, swapped, *a, ds, o, f, row_dot, probs, dp0, dpo,
         cost=LONG,
     )
     oq = (mine + lax.ppermute(other, AXES, SWAP).astype(F32)).astype(BF16)

time: 89.1 us -> 87 us (0.976)
  blocking collectives: 41.1 us -> 26.5 us
  waiting for transfers between devices: 15.3 us -> 22.1 us
  starting transfers between devices: 15.3 us -> 21.4 us
    all_to_all x1 -> x0, blocking collectives: 17.7 us -> none  [local(): everything = lax.all_to_all(packed, 'head', 0, 0, tiled=True)]
    all_to_all x0 -> x1, waiting for transfers between devices: none -> 10.6 us  [local(): everything = lax.all_to_all(packed, 'head', 0, 0, tiled=True)]
    all_to_all x0 -> x1, starting transfers between devices: none -> 6.12 us  [local(): everything = lax.all_to_all(packed, 'head', 0, 0, tiled=True)]
    ppermute x3, waiting for transfers between devices: 10.2 us -> 6.33 us  [ahead(): lax.ppermute(x, AXES, [(r[i], r[i + dist]) for r in ALONG for i in range(...]
    all_to_all x1, blocking collectives: 23.5 us -> 26.5 us  [local(): lax.all_to_all(jnp.concatenate((grads, oq), axis=1), 'head', 0, 0, tiled=...]
  transfers between devices with their start and end apart: 9 -> 10, of which waited for: 3 -> 4; matrix products, arithmetic and copies ran while one was open for 0% -> 0% of each run, Pallas kernels for 7% -> 6%
where the time goes in v8:
time: 87 us; the launch traced here: 86.6 us
  blocking collectives  26.5 us (30%)
  waiting for transfers between devices  22.1 us (25%)
  starting transfers between devices  21.4 us (25%)
  Pallas kernels  15.4 us (18%)
    all_to_all x1, blocking collectives, local(): lax.all_to_all(jnp.concatenate((grads, oq), axis=1), 'head', 0, 0, tiled=...  26.5 us
    pallas_call x8, Pallas kernels, run(): pl.pallas_call(kernel, out_shape=outs, in_specs=[first] + [VM] * (len(ope...  12.8 us
    all_to_all x1, waiting for transfers between devices, local(): everything = lax.all_to_all(packed, 'head', 0, 0, tiled=True)  10.6 us
    ppermute x3, waiting for transfers between devices, ahead(): lax.ppermute(x, AXES, [(r[i], r[i + dist]) for r in ALONG for i in range(...  6.33 us
    all_to_all x1, starting transfers between devices, local(): everything = lax.all_to_all(packed, 'head', 0, 0, tiled=True)  6.12 us
    ppermute x3, starting transfers between devices, ahead(): lax.ppermute(x, AXES, [(r[i], r[i + dist]) for r in ALONG for i in range(...  5.17 us
    ppermute x3, waiting for transfers between devices, behind(): lax.ppermute(x, AXES, [(r[i + dist], r[i]) for r in ALONG for i in range(...  5.15 us
    ppermute x3, starting transfers between devices, behind(): lax.ppermute(x, AXES, [(r[i + dist], r[i]) for r in ALONG for i in range(...  3.89 us
  transfers between devices with their start and end apart: 10, of which 4 were waited for; matrix products, arithmetic and copies ran while one was open for 0% of the time, Pallas kernels for 6%

profile of v8, /device:TPU:176, one launch (start us, length us, event | category | flops | bytes accessed | tf_op | source)
XLA Modules:
  0.0 86.6 jit_solution(17396114136682897699)
XLA Ops:
  0.6 2.6 %shard_map.84 = bf16[8,320,128]{2,1,0:T(8,128)(2,1)} custom-call(s32[8]{0:T(128)} %shift_ref.1, bf16[256,128]{1,0:T(8,128)(2,1)} %bitcast.12, bf16[256,128]{1,0:T(8,128)(2,1)} %bitcast.13, bf16[1024,128]{1,0:T(8,128)(2,1)} %bitcast.10, bf16[1024,128]{1,0:T(8,128)(2,1)} %bitcast.11), custom_call_target="tpu_custom_call" | custom-call | tf_op jit(solution)/shard_map/pallas_call | solution.py:386
  3.3 6.1 %all-to-all-start = ((bf16[8,320,128]{2,1,0:T(8,128)(2,1)}), bf16[8,320,128]{2,1,0:T(8,128)(2,1)S(1)}, u32[]{:S(2)}, u32[]{:S(2)}) async-start(bf16[8,320,128]{2,1,0:T(8,128)(2,1)} %shard_map.84), calls=%async_computation | async-start | bytes 1310720 | tf_op jit(solution)/shard_map/all_to_all | solution.py:439
  9.4 0.1 pad_add_fusion.where_ref
  9.5 10.6 %all-to-all-done.all_ref = bf16[8,320,128]{2,1,0:T(8,128)(2,1)S(1)} async-done(((bf16[8,320,128]{2,1,0:T(8,128)(2,1)}), bf16[8,320,128]{2,1,0:T(8,128)(2,1)S(1)}, u32[]{:S(2)}, u32[]{:S(2)}) %all-to-all-start) | async-done | bytes 655392 | tf_op jit(solution)/shard_map/all_to_all | solution.py:439
  20.1 0.7 collective-permute-start.3
  20.7 1.3 %collective-permute-start.2 = (bf16[8,64,128]{2,1,0:T(8,128)(2,1)S(1)}, bf16[8,64,128]{2,1,0:T(8,128)(2,1)S(1)}, u32[]{:S(2)}, u32[]{:S(2)}) collective-permute-start(bf16[8,64,128]{2,1,0:T(8,128)(2,1)S(1)} %slice.9), channel_id=1, source_target_pairs={{0,32},{16,48},{1,33},{17,49},{2,34},{18,50},{3,35},{19,51},{36,68... | collective-permute-start | bytes 393224 | tf_op jit(solution)/shard_map/ppermute | solution.py:420
  22.0 3.2 %collective-permute-start.1 = (bf16[8,64,128]{2,1,0:T(8,128)(2,1)S(1)}, bf16[8,64,128]{2,1,0:T(8,128)(2,1)S(1)}, u32[]{:S(2)}, u32[]{:S(2)}) collective-permute-start(bf16[8,64,128]{2,1,0:T(8,128)(2,1)S(1)} %slice.9), channel_id=1, source_target_pairs={{0,16},{16,32},{32,48},{1,17},{17,33},{33,49},{2,18},{18,34},{34,5... | collective-permute-start | bytes 393224 | tf_op jit(solution)/shard_map/ppermute | solution.py:420
  25.3 1.9 %collective-permute-start = (bf16[8,256,128]{2,1,0:T(8,128)(2,1)S(1)}, bf16[8,256,128]{2,1,0:T(8,128)(2,1)S(1)}, u32[]{:S(2)}, u32[]{:S(2)}) collective-permute-start(bf16[8,256,128]{2,1,0:T(8,128)(2,1)S(1)} %slice.8), channel_id=1, source_target_pairs={{0,8},{1,9},{2,10},{3,11},{4,12},{5,13},{6,14},{7,15},{8,0},{9,1},... | collective-permute-start | bytes 1572872 | tf_op jit(solution)/shard_map/ppermute | solution.py:442
  27.2 0.5 shard_map.85
  27.7 0.0 collective-permute-done.3.a3
  27.7 0.6 shard_map.86
  28.3 2.4 %collective-permute-done.2.a2 = bf16[8,64,128]{2,1,0:T(8,128)(2,1)S(1)} collective-permute-done((bf16[8,64,128]{2,1,0:T(8,128)(2,1)S(1)}, bf16[8,64,128]{2,1,0:T(8,128)(2,1)S(1)}, u32[]{:S(2)}, u32[]{:S(2)}) %collective-permute-start.2) | collective-permute-done | bytes 131104 | tf_op jit(solution)/shard_map/ppermute | solution.py:420
  30.7 3.9 %collective-permute-done.1.a1 = bf16[8,64,128]{2,1,0:T(8,128)(2,1)S(1)} collective-permute-done((bf16[8,64,128]{2,1,0:T(8,128)(2,1)S(1)}, bf16[8,64,128]{2,1,0:T(8,128)(2,1)S(1)}, u32[]{:S(2)}, u32[]{:S(2)}) %collective-permute-start.1) | collective-permute-done | bytes 131104 | tf_op jit(solution)/shard_map/ppermute | solution.py:420
  34.6 0.0 collective-permute-done.sw_ref
  34.6 3.5 %shard_map.87 = (f32[4,256,2048]{2,1,0:T(8,128)S(1)}, f32[2,256,1024]{2,1,0:T(8,128)S(1)}, f32[4,256,1024]{2,1,0:T(8,128)S(1)}, f32[8,2048]{1,0:T(8,128)S(1)}) custom-call(s32[2]{0:T(128)S(1)} %pad_add_fusion.where_ref, bf16[8,320,128]{2,1,0:T(8,128)(2,1)S(1)} %all-to-all-done.all_ref, bf16[8,256,128]{2,1,0:T(8,128)(2,1)S(1)} %collective-permute-done.sw_ref, ...), custom_call_target="tpu_custom_call" | custom-call | tf_op jit(solution)/shard_map/pallas_call | solution.py:374
  38.2 1.9 %collective-permute-start.4 = (f32[8,2048]{1,0:T(8,128)S(1)}, f32[8,2048]{1,0:T(8,128)S(1)}, u32[]{:S(2)}, u32[]{:S(2)}) collective-permute-start(f32[8,2048]{1,0:T(8,128)S(1)} %get-tuple-element.37.stats_ref), channel_id=1, source_target_pairs={{0,8},{1,9},{2,10},{3,11},{4,12},{5,13},{6,14},{7,15},{8,0},{9,1},... | collective-permute-start | bytes 196616 | tf_op jit(solution)/shard_map/ppermute | solution.py:462
  40.1 1.5 %shard_map.89.o_ref = f32[128,2048]{1,0:T(8,128)S(1)} custom-call(s32[2]{0:T(128)S(1)} %pad_add_fusion.where_ref, bf16[8,320,128]{2,1,0:T(8,128)(2,1)S(1)} %all-to-all-done.all_ref, bf16[8,64,128]{2,1,0:T(8,128)(2,1)S(1)} %collective-permute-done.1.a1, bf16[8,64,128]{2,1,0:T(8,128)(2,1)S(1)} %collective-permute-done.2.a2, ...), custom_call_target="tpu_custom_call" | custom-call | flops 10000000000 | bytes 1048576 | tf_op jit(solution)/shard_map/pallas_call | solution.py:374
  41.6 0.0 collective-permute-done.4.swapped_stats_ref
  41.6 2.3 %shard_map.88 = (bf16[8,64,128]{2,1,0:T(8,128)(2,1)S(1)}, bf16[8,64,128]{2,1,0:T(8,128)(2,1)S(1)}, bf16[8,64,128]{2,1,0:T(8,128)(2,1)S(1)}, bf16[3,256,2048]{2,1...) custom-call(s32[2]{0:T(128)S(1)} %pad_add_fusion.where_ref, ...), custom_call_target="tpu_custom_call" | custom-call | tf_op jit(solution)/shard_map/pallas_call | solution.py:374
  43.9 1.9 %collective-permute-start.5 = (bf16[8,64,128]{2,1,0:T(8,128)(2,1)S(1)}, bf16[8,64,128]{2,1,0:T(8,128)(2,1)S(1)}, u32[]{:S(2)}, u32[]{:S(2)}) collective-permute-start(bf16[8,64,128]{2,1,0:T(8,128)(2,1)S(1)} %get-tuple-element.45), channel_id=1, source_target_pairs={{16,0},{32,16},{48,32},{17,1},{33,17},{49,33},{18,2},{34,18},{50,3... | collective-permute-start | bytes 393224 | tf_op jit(solution)/shard_map/ppermute | solution.py:424
  45.8 1.3 %collective-permute-start.6 = (bf16[8,64,128]{2,1,0:T(8,128)(2,1)S(1)}, bf16[8,64,128]{2,1,0:T(8,128)(2,1)S(1)}, u32[]{:S(2)}, u32[]{:S(2)}) collective-permute-start(bf16[8,64,128]{2,1,0:T(8,128)(2,1)S(1)} %get-tuple-element.46), channel_id=1, source_target_pairs={{32,0},{48,16},{33,1},{49,17},{34,2},{50,18},{35,3},{51,19},{68,36... | collective-permute-start | bytes 393224 | tf_op jit(solution)/shard_map/ppermute | solution.py:424
  47.1 0.7 collective-permute-start.7
  47.8 2.6 %shard_map.90 = (f32[8,256,128]{2,1,0:T(8,128)S(1)}, bf16[8,256,128]{2,1,0:T(8,128)(2,1)S(1)}, f32[8,64,128]{2,1,0:T(8,128)S(1)}) custom-call(s32[2]{0:T(128)S(1)} %pad_add_fusion.where_ref, bf16[8,320,128]{2,1,0:T(8,128)(2,1)S(1)} %all-to-all-done.all_ref, bf16[8,256,128]{2,1,0:T(8,128)(2,1)S(1)} %collective-permute-done.sw_ref, ...), custom_call_target="tpu_custom_call" | custom-call | flops 10000000000 | bytes 1048576 | tf_op jit(solution)/shard_map/pallas_call | solution.py:374
  50.4 2.4 %collective-permute-start.8 = (bf16[8,256,128]{2,1,0:T(8,128)(2,1)S(1)}, bf16[8,256,128]{2,1,0:T(8,128)(2,1)S(1)}, u32[]{:S(2)}, u32[]{:S(2)}) collective-permute-start(bf16[8,256,128]{2,1,0:T(8,128)(2,1)S(1)} %get-tuple-element.49), channel_id=1, source_target_pairs={{0,8},{1,9},{2,10},{3,11},{4,12},{5,13},{6,14},{7,15},{8,0},{9,1},... | collective-permute-start | bytes 1572872 | tf_op jit(solution)/shard_map/ppermute | solution.py:485
  52.8 0.0 collective-permute-done.5.c1
  52.8 5.1 %collective-permute-done.6.c2 = bf16[8,64,128]{2,1,0:T(8,128)(2,1)S(1)} collective-permute-done((bf16[8,64,128]{2,1,0:T(8,128)(2,1)S(1)}, bf16[8,64,128]{2,1,0:T(8,128)(2,1)S(1)}, u32[]{:S(2)}, u32[]{:S(2)}) %collective-permute-start.6) | collective-permute-done | bytes 131104 | tf_op jit(solution)/shard_map/ppermute | solution.py:424
  57.9 0.1 shard_map.91
  58.0 0.0 collective-permute-done.8
  58.0 0.0 copy-start
  58.0 0.1 add_convert_fusion
  58.2 26.5 %all_to_all.10.in_ref = bf16[8,320,128]{2,1,0:T(8,128)(2,1)S(1)} all-to-all(bf16[8,320,128]{2,1,0:T(8,128)(2,1)S(1)} %pad_maximum_fusion), channel_id=1, replica_groups=mesh['seq'=64,'head'=8] {'head'}, dimensions={0} | all-to-all | bytes 1310720 | tf_op jit(solution)/shard_map/all_to_all | solution.py:487
  84.7 1.8 %shard_map.92 = (bf16[1024,128]{1,0:T(8,128)(2,1)}, bf16[1024,128]{1,0:T(8,128)(2,1)}, bf16[256,128]{1,0:T(8,128)(2,1)}, bf16[256,128]{1,0:T(8,128)(2,1)}) custom-call(s32[8]{0:T(128)S(1)} %copy-done, bf16[8,320,128]{2,1,0:T(8,128)(2,1)S(1)} %all_to_all.10.in_ref), custom_call_target="tpu_custom_call" | custom-call | tf_op jit(solution)/shard_map/pallas_call | solution.py:374
  (5 shorter events, 0.1 us)
Async XLA Ops:
  3.3 16.8 %all-to-all-start = ((bf16[8,320,128]{2,1,0:T(8,128)(2,1)}), bf16[8,320,128]{2,1,0:T(8,128)(2,1)S(1)}, u32[]{:S(2)}, u32[]{:S(2)}) async-start(bf16[8,320,128]{2,1,0:T(8,128)(2,1)} %shard_map.84), calls=%async_computation | async-start | bytes 1310720 | tf_op jit(solution)/shard_map/all_to_all | solution.py:439
  20.1 7.7 %collective-permute-start.3 = (bf16[8,64,128]{2,1,0:T(8,128)(2,1)S(1)}, bf16[8,64,128]{2,1,0:T(8,128)(2,1)S(1)}, u32[]{:S(2)}, u32[]{:S(2)}) collective-permute-start(bf16[8,64,128]{2,1,0:T(8,128)(2,1)S(1)} %slice.9), channel_id=1, source_target_pairs={{0,48},{1,49},{2,50},{3,51},{36,84},{37,85},{38,86},{39,87},{8,56}... | collective-permute-start | bytes 393224 | tf_op jit(solution)/shard_map/ppermute | solution.py:420
  20.7 10.0 %collective-permute-start.2 = (bf16[8,64,128]{2,1,0:T(8,128)(2,1)S(1)}, bf16[8,64,128]{2,1,0:T(8,128)(2,1)S(1)}, u32[]{:S(2)}, u32[]{:S(2)}) collective-permute-start(bf16[8,64,128]{2,1,0:T(8,128)(2,1)S(1)} %slice.9), channel_id=1, source_target_pairs={{0,32},{16,48},{1,33},{17,49},{2,34},{18,50},{3,35},{19,51},{36,68... | collective-permute-start | bytes 393224 | tf_op jit(solution)/shard_map/ppermute | solution.py:420
  22.0 12.6 %collective-permute-start.1 = (bf16[8,64,128]{2,1,0:T(8,128)(2,1)S(1)}, bf16[8,64,128]{2,1,0:T(8,128)(2,1)S(1)}, u32[]{:S(2)}, u32[]{:S(2)}) collective-permute-start(bf16[8,64,128]{2,1,0:T(8,128)(2,1)S(1)} %slice.9), channel_id=1, source_target_pairs={{0,16},{16,32},{32,48},{1,17},{17,33},{33,49},{2,18},{18,34},{34,5... | collective-permute-start | bytes 393224 | tf_op jit(solution)/shard_map/ppermute | solution.py:420
  25.3 9.3 %collective-permute-start = (bf16[8,256,128]{2,1,0:T(8,128)(2,1)S(1)}, bf16[8,256,128]{2,1,0:T(8,128)(2,1)S(1)}, u32[]{:S(2)}, u32[]{:S(2)}) collective-permute-start(bf16[8,256,128]{2,1,0:T(8,128)(2,1)S(1)} %slice.8), channel_id=1, source_target_pairs={{0,8},{1,9},{2,10},{3,11},{4,12},{5,13},{6,14},{7,15},{8,0},{9,1},... | collective-permute-start | bytes 1572872 | tf_op jit(solution)/shard_map/ppermute | solution.py:442
  38.2 3.4 %collective-permute-start.4 = (f32[8,2048]{1,0:T(8,128)S(1)}, f32[8,2048]{1,0:T(8,128)S(1)}, u32[]{:S(2)}, u32[]{:S(2)}) collective-permute-start(f32[8,2048]{1,0:T(8,128)S(1)} %get-tuple-element.37.stats_ref), channel_id=1, source_target_pairs={{0,8},{1,9},{2,10},{3,11},{4,12},{5,13},{6,14},{7,15},{8,0},{9,1},... | collective-permute-start | bytes 196616 | tf_op jit(solution)/shard_map/ppermute | solution.py:462
  43.9 8.9 %collective-permute-start.5 = (bf16[8,64,128]{2,1,0:T(8,128)(2,1)S(1)}, bf16[8,64,128]{2,1,0:T(8,128)(2,1)S(1)}, u32[]{:S(2)}, u32[]{:S(2)}) collective-permute-start(bf16[8,64,128]{2,1,0:T(8,128)(2,1)S(1)} %get-tuple-element.45), channel_id=1, source_target_pairs={{16,0},{32,16},{48,32},{17,1},{33,17},{49,33},{18,2},{34,18},{50,3... | collective-permute-start | bytes 393224 | tf_op jit(solution)/shard_map/ppermute | solution.py:424
  45.8 12.1 %collective-permute-start.6 = (bf16[8,64,128]{2,1,0:T(8,128)(2,1)S(1)}, bf16[8,64,128]{2,1,0:T(8,128)(2,1)S(1)}, u32[]{:S(2)}, u32[]{:S(2)}) collective-permute-start(bf16[8,64,128]{2,1,0:T(8,128)(2,1)S(1)} %get-tuple-element.46), channel_id=1, source_target_pairs={{32,0},{48,16},{33,1},{49,17},{34,2},{50,18},{35,3},{51,19},{68,36... | collective-permute-start | bytes 393224 | tf_op jit(solution)/shard_map/ppermute | solution.py:424
  47.1 10.8 %collective-permute-start.7 = (bf16[8,64,128]{2,1,0:T(8,128)(2,1)S(1)}, bf16[8,64,128]{2,1,0:T(8,128)(2,1)S(1)}, u32[]{:S(2)}, u32[]{:S(2)}) collective-permute-start(bf16[8,64,128]{2,1,0:T(8,128)(2,1)S(1)} %get-tuple-element.47), channel_id=1, source_target_pairs={{48,0},{49,1},{50,2},{51,3},{84,36},{85,37},{86,38},{87,39},{56,8}... | collective-permute-start | bytes 393224 | tf_op jit(solution)/shard_map/ppermute | solution.py:424
  50.4 7.6 %collective-permute-start.8 = (bf16[8,256,128]{2,1,0:T(8,128)(2,1)S(1)}, bf16[8,256,128]{2,1,0:T(8,128)(2,1)S(1)}, u32[]{:S(2)}, u32[]{:S(2)}) collective-permute-start(bf16[8,256,128]{2,1,0:T(8,128)(2,1)S(1)} %get-tuple-element.49), channel_id=1, source_target_pairs={{0,8},{1,9},{2,10},{3,11},{4,12},{5,13},{6,14},{7,15},{8,0},{9,1},... | collective-permute-start | bytes 1572872 | tf_op jit(solution)/shard_map/ppermute | solution.py:485
  58.0 26.7 %copy-start = (s32[8]{0:T(128)S(1)}, s32[8]{0:T(128)}, u32[]{:S(2)}) copy-start(s32[8]{0:T(128)} %shift_ref.1) | copy-start | bytes 100

commit v9 on v8

--- a/solution.py
+++ b/solution.py
@@ -169,6 +169,19 @@
         dp_ref[:, at] = dot(vals, dt_ref[:, at])
 
 
+def other_kernel(where_ref, all_ref, sw_ref, qt_ref, dt_ref, s_ref, dp_ref, m_ref):
+    core = where_ref[1]
+    qt_ref[...] = sw_ref[:, 0:128, :].reshape(ROWS, HD).T
+    dt_ref[...] = sw_ref[:, 128:256, :].reshape(ROWS, HD).T
+    keys = all_ref[:, 0:SUB, :].reshape(TOK, HD)
+    vals = all_ref[:, SUB : 2 * SUB, :].reshape(TOK, HD)
+    for at in halves():
+        s = jnp.where(core == 0, dot(keys, qt_ref[:, at]), NEG)
+        s_ref[:, at] = s
+        m_ref[:, at] = fold(s, jnp.max)
+        dp_ref[:, at] = dot(vals, dt_ref[:, at])
+
+
 def early_kernel(where_ref, qt_ref, dt_ref, a3, s_ref, dp_ref, m_ref):
     chips = where_ref[0]
 
@@ -188,22 +201,17 @@
 
 
 def probs_kernel(
-    where_ref, all_ref, sw_ref, qt_ref, dt_ref, s0_ref, dp0_ref, m0_ref, s3_ref, dp3_ref, m3_ref, a1, a2, a3,
-    p_ref, dpm_ref, dpo_ref, stats_ref, k_s, v_s, qo_s, do_s, m_s, l_s, r_s,
+    where_ref, qt_ref, dt_ref, s0_ref, dp0_ref, m0_ref, s3_ref, dp3_ref, m3_ref,
+    qo_s, do_s, s0o_ref, dp0o_ref, m0o_ref, a1, a2, a3,
+    p_ref, dpm_ref, dpo_ref, stats_ref, k_s, v_s, m_s, l_s, r_s,
 ):
     chips = where_ref[0]
-    core = where_ref[1]
     last = jnp.minimum(chips, 2) + 1
-    for n, ref in enumerate((all_ref, a1, a2, a3)):
-        k_s[n] = ref[:, 0:SUB, :].reshape(TOK, HD)
-        v_s[n] = ref[:, SUB : 2 * SUB, :].reshape(TOK, HD)
-    qo_s[...] = sw_ref[:, 0:128, :].reshape(ROWS, HD).T
-    do_s[...] = sw_ref[:, 128:256, :].reshape(ROWS, HD).T
+    for n, ref in enumerate((a1, a2, a3)):
+        k_s[n + 1] = ref[:, 0:SUB, :].reshape(TOK, HD)
+        v_s[n + 1] = ref[:, SUB : 2 * SUB, :].reshape(TOK, HD)
     m_s[:, 0:ROWS] = jnp.maximum(m0_ref[...], m3_ref[...])
-    for at in halves():
-        s = jnp.where(core == 0, dot(k_s[0], qo_s[:, at]), NEG)
-        p_ref[0, :, past(at)] = s
-        m_s[:, past(at)] = fold(s, jnp.max)
+    m_s[:, ROWS:BOTH] = m0o_ref[...]
 
     def scores(b, mine):
         for at in halves():
@@ -233,7 +241,7 @@
         l_s[:, at] = total if begin else l_s[:, at] + total
         r_s[:, at] = row if begin else r_s[:, at] + row
 
-    def forward(b, mine, begin=False):
+    def forward(b, mine):
         for at in halves():
             if mine:
                 dp = dot(v_s[b], dt_ref[:, at])
@@ -241,12 +249,13 @@
                 probs(b, at, p_ref[b, :, at], dp)
             dp = dot(v_s[b], do_s[:, at])
             dpo_ref[b, :, at] = dp
-            probs(b, past(at), p_ref[b, :, past(at)], dp, begin)
+            probs(b, past(at), p_ref[b, :, past(at)], dp)
         return 0
 
     for at in halves():
         probs(0, at, s0_ref[:, at], dp0_ref[:, at], True)
-    forward(0, False, True)
+        dpo_ref[0, :, at] = dp0o_ref[:, at]
+        probs(0, past(at), s0o_ref[:, at], dp0o_ref[:, at], True)
     lax.fori_loop(1, last, lambda b, _: forward(b, True), 0)
 
     @pl.when(chips == 3)
@@ -447,6 +456,9 @@
         first_kernel, (half, half, part, part, top), [], everything, first=VM, cost=LONG
     )
     s3, dp3, m3 = run(early_kernel, (part, part, top), [], where, qt, dt, a[2], cost=LONG)
+    qo, do, s0o, dp0o, m0o = run(
+        other_kernel, (half, half, part, part, top), [], where, everything, swapped, cost=None
+    )
     held, turned = pltpu.VMEM((4, TOK, HD), BF16), pltpu.VMEM((HD, ROWS), BF16)
     probs, dp, dpo, stats = run(
         probs_kernel,
@@ -456,8 +468,8 @@
             shape(4, TOK, ROWS, dtype=F32),
             flat,
         ),
-        [held, held, turned, turned, rows, rows, rows],
-        where, everything, swapped, qt, dt, s0, dp0, m0, s3, dp3, m3, *a,
+        [held, held, rows, rows, rows],
+        where, qt, dt, s0, dp0, m0, s3, dp3, m3, qo, do, s0o, dp0o, m0o, *a,
     )
     swapped_stats = lax.ppermute(stats, AXES, SWAP)
     (o,) = run(

time: 87 us -> 86.3 us (level)
  waiting for transfers between devices: 22.1 us -> 21.1 us
    ppermute x3, waiting for transfers between devices: 6.33 us -> 4.49 us  [ahead(): lax.ppermute(x, AXES, [(r[i], r[i + dist]) for r in ALONG for i in range(...]
    pallas_call x8 -> x9, Pallas kernels: 12.8 us -> 13.2 us  [run(): pl.pallas_call(kernel, out_shape=outs, in_specs=[first] + [VM] * (len(ope...]
  transfers between devices with their start and end apart: 10 -> 10, of which waited for: 4 -> 5; matrix products, arithmetic and copies ran while one was open for 0% -> 0% of each run, Pallas kernels for 6% -> 7%
where the time goes in v9:
time: 86.3 us; the launch traced here: 85.9 us
  blocking collectives  26.5 us (31%)
  starting transfers between devices  21.4 us (25%)
  waiting for transfers between devices  21.1 us (24%)
  Pallas kernels  15.8 us (18%)
    all_to_all x1, blocking collectives, local(): lax.all_to_all(jnp.concatenate((grads, oq), axis=1), 'head', 0, 0, tiled=...  26.5 us
    pallas_call x9, Pallas kernels, run(): pl.pallas_call(kernel, out_shape=outs, in_specs=[first] + [VM] * (len(ope...  13.2 us
    all_to_all x1, waiting for transfers between devices, local(): everything = lax.all_to_all(packed, 'head', 0, 0, tiled=True)  10.6 us
    all_to_all x1, starting transfers between devices, local(): everything = lax.all_to_all(packed, 'head', 0, 0, tiled=True)  6.12 us
    ppermute x3, waiting for transfers between devices, behind(): lax.ppermute(x, AXES, [(r[i + dist], r[i]) for r in ALONG for i in range(...  5.18 us
    ppermute x3, starting transfers between devices, ahead(): lax.ppermute(x, AXES, [(r[i], r[i + dist]) for r in ALONG for i in range(...  5.17 us
    ppermute x3, waiting for transfers between devices, ahead(): lax.ppermute(x, AXES, [(r[i], r[i + dist]) for r in ALONG for i in range(...  4.49 us
    ppermute x3, starting transfers between devices, behind(): lax.ppermute(x, AXES, [(r[i + dist], r[i]) for r in ALONG for i in range(...  3.89 us
  transfers between devices with their start and end apart: 10, of which 5 were waited for; matrix products, arithmetic and copies ran while one was open for 0% of the time, Pallas kernels for 7%

profile of v9, /device:TPU:176, one launch (start us, length us, event | category | flops | bytes accessed | tf_op | source)
XLA Modules:
  0.0 85.9 jit_solution(5312544226659379448)
XLA Ops:
  0.6 2.6 %shard_map.84 = bf16[8,320,128]{2,1,0:T(8,128)(2,1)} custom-call(s32[8]{0:T(128)} %shift_ref.1, bf16[256,128]{1,0:T(8,128)(2,1)} %bitcast.12, bf16[256,128]{1,0:T(8,128)(2,1)} %bitcast.13, bf16[1024,128]{1,0:T(8,128)(2,1)} %bitcast.10, bf16[1024,128]{1,0:T(8,128)(2,1)} %bitcast.11), custom_call_target="tpu_custom_call" | custom-call | tf_op jit(solution)/shard_map/pallas_call | solution.py:395
  3.2 6.1 %all-to-all-start = ((bf16[8,320,128]{2,1,0:T(8,128)(2,1)}), bf16[8,320,128]{2,1,0:T(8,128)(2,1)S(1)}, u32[]{:S(2)}, u32[]{:S(2)}) async-start(bf16[8,320,128]{2,1,0:T(8,128)(2,1)} %shard_map.84), calls=%async_computation | async-start | bytes 1310720 | tf_op jit(solution)/shard_map/all_to_all | solution.py:448
  9.4 0.1 pad_add_fusion.where_ref
  9.4 10.6 %all-to-all-done.all_ref = bf16[8,320,128]{2,1,0:T(8,128)(2,1)S(1)} async-done(((bf16[8,320,128]{2,1,0:T(8,128)(2,1)}), bf16[8,320,128]{2,1,0:T(8,128)(2,1)S(1)}, u32[]{:S(2)}, u32[]{:S(2)}) %all-to-all-start) | async-done | bytes 655392 | tf_op jit(solution)/shard_map/all_to_all | solution.py:448
  20.0 0.7 collective-permute-start.3
  20.7 1.3 %collective-permute-start.2 = (bf16[8,64,128]{2,1,0:T(8,128)(2,1)S(1)}, bf16[8,64,128]{2,1,0:T(8,128)(2,1)S(1)}, u32[]{:S(2)}, u32[]{:S(2)}) collective-permute-start(bf16[8,64,128]{2,1,0:T(8,128)(2,1)S(1)} %slice.9), channel_id=1, source_target_pairs={{0,32},{16,48},{1,33},{17,49},{2,34},{18,50},{3,35},{19,51},{36,68... | collective-permute-start | bytes 393224 | tf_op jit(solution)/shard_map/ppermute | solution.py:429
  22.0 3.2 %collective-permute-start.1 = (bf16[8,64,128]{2,1,0:T(8,128)(2,1)S(1)}, bf16[8,64,128]{2,1,0:T(8,128)(2,1)S(1)}, u32[]{:S(2)}, u32[]{:S(2)}) collective-permute-start(bf16[8,64,128]{2,1,0:T(8,128)(2,1)S(1)} %slice.9), channel_id=1, source_target_pairs={{0,16},{16,32},{32,48},{1,17},{17,33},{33,49},{2,18},{18,34},{34,5... | collective-permute-start | bytes 393224 | tf_op jit(solution)/shard_map/ppermute | solution.py:429
  25.3 1.9 %collective-permute-start = (bf16[8,256,128]{2,1,0:T(8,128)(2,1)S(1)}, bf16[8,256,128]{2,1,0:T(8,128)(2,1)S(1)}, u32[]{:S(2)}, u32[]{:S(2)}) collective-permute-start(bf16[8,256,128]{2,1,0:T(8,128)(2,1)S(1)} %slice.8), channel_id=1, source_target_pairs={{0,8},{1,9},{2,10},{3,11},{4,12},{5,13},{6,14},{7,15},{8,0},{9,1},... | collective-permute-start | bytes 1572872 | tf_op jit(solution)/shard_map/ppermute | solution.py:451
  27.2 0.5 shard_map.85
  27.7 0.0 collective-permute-done.3.a3
  27.7 0.6 shard_map.86
  28.3 0.8 collective-permute-done.sw_ref
  29.1 1.0 %shard_map.87 = (bf16[128,1024]{1,0:T(8,128)(2,1)S(1)}, bf16[128,1024]{1,0:T(8,128)(2,1)S(1)}, f32[256,1024]{1,0:T(8,128)S(1)}, f32[256,1024]{1,0:T(8,128)S(1)}, f32[8,1024]{1,0:T(8,128)S(1)}) custom-call(s32[2]{0:T(128)S(1)} %pad_add_fusion.where_ref, bf16[8,320,128]{2,1,0:T(8,128)(2,1)S(1)} %all-to-all-done.all_ref, ...), custom_call_target="tpu_custom_call" | custom-call | tf_op jit(solution)/shard_map/pallas_call | solution.py:383
  30.1 0.6 collective-permute-done.2.a2
  30.7 3.9 %collective-permute-done.1.a1 = bf16[8,64,128]{2,1,0:T(8,128)(2,1)S(1)} collective-permute-done((bf16[8,64,128]{2,1,0:T(8,128)(2,1)S(1)}, bf16[8,64,128]{2,1,0:T(8,128)(2,1)S(1)}, u32[]{:S(2)}, u32[]{:S(2)}) %collective-permute-start.1) | collective-permute-done | bytes 131104 | tf_op jit(solution)/shard_map/ppermute | solution.py:429
  34.6 3.1 %shard_map.88 = (f32[4,256,2048]{2,1,0:T(8,128)S(1)}, f32[2,256,1024]{2,1,0:T(8,128)S(1)}, f32[4,256,1024]{2,1,0:T(8,128)S(1)}, f32[8,2048]{1,0:T(8,128)S(1)}) custom-call(s32[2]{0:T(128)S(1)} %pad_add_fusion.where_ref, bf16[128,1024]{1,0:T(8,128)(2,1)S(1)} %get-tuple-element.34.qt_ref, bf16[128,1024]{1,0:T(8,128)(2,1)S(1)} %get-tuple-element.35.dt_ref, ...), custom_call_target="tpu_custom_call" | custom-call | tf_op jit(solution)/shard_map/pallas_call | solution.py:383
  37.7 1.9 %collective-permute-start.4 = (f32[8,2048]{1,0:T(8,128)S(1)}, f32[8,2048]{1,0:T(8,128)S(1)}, u32[]{:S(2)}, u32[]{:S(2)}) collective-permute-start(f32[8,2048]{1,0:T(8,128)S(1)} %get-tuple-element.47.stats_ref), channel_id=1, source_target_pairs={{0,8},{1,9},{2,10},{3,11},{4,12},{5,13},{6,14},{7,15},{8,0},{9,1},... | collective-permute-start | bytes 196616 | tf_op jit(solution)/shard_map/ppermute | solution.py:474
  39.6 1.5 %shard_map.90.o_ref = f32[128,2048]{1,0:T(8,128)S(1)} custom-call(s32[2]{0:T(128)S(1)} %pad_add_fusion.where_ref, bf16[8,320,128]{2,1,0:T(8,128)(2,1)S(1)} %all-to-all-done.all_ref, bf16[8,64,128]{2,1,0:T(8,128)(2,1)S(1)} %collective-permute-done.1.a1, bf16[8,64,128]{2,1,0:T(8,128)(2,1)S(1)} %collective-permute-done.2.a2, ...), custom_call_target="tpu_custom_call" | custom-call | flops 10000000000 | bytes 1048576 | tf_op jit(solution)/shard_map/pallas_call | solution.py:383
  41.1 0.0 collective-permute-done.4.swapped_stats_ref
  41.1 2.2 %shard_map.89 = (bf16[8,64,128]{2,1,0:T(8,128)(2,1)S(1)}, bf16[8,64,128]{2,1,0:T(8,128)(2,1)S(1)}, bf16[8,64,128]{2,1,0:T(8,128)(2,1)S(1)}, bf16[3,256,2048]{2,1...) custom-call(s32[2]{0:T(128)S(1)} %pad_add_fusion.where_ref, ...), custom_call_target="tpu_custom_call" | custom-call | tf_op jit(solution)/shard_map/pallas_call | solution.py:383
  43.3 1.9 %collective-permute-start.5 = (bf16[8,64,128]{2,1,0:T(8,128)(2,1)S(1)}, bf16[8,64,128]{2,1,0:T(8,128)(2,1)S(1)}, u32[]{:S(2)}, u32[]{:S(2)}) collective-permute-start(bf16[8,64,128]{2,1,0:T(8,128)(2,1)S(1)} %get-tuple-element.55), channel_id=1, source_target_pairs={{16,0},{32,16},{48,32},{17,1},{33,17},{49,33},{18,2},{34,18},{50,3... | collective-permute-start | bytes 393224 | tf_op jit(solution)/shard_map/ppermute | solution.py:433
  45.2 1.3 %collective-permute-start.6 = (bf16[8,64,128]{2,1,0:T(8,128)(2,1)S(1)}, bf16[8,64,128]{2,1,0:T(8,128)(2,1)S(1)}, u32[]{:S(2)}, u32[]{:S(2)}) collective-permute-start(bf16[8,64,128]{2,1,0:T(8,128)(2,1)S(1)} %get-tuple-element.56), channel_id=1, source_target_pairs={{32,0},{48,16},{33,1},{49,17},{34,2},{50,18},{35,3},{51,19},{68,36... | collective-permute-start | bytes 393224 | tf_op jit(solution)/shard_map/ppermute | solution.py:433
  46.5 0.7 collective-permute-start.7
  47.2 2.5 %shard_map.91 = (f32[8,256,128]{2,1,0:T(8,128)S(1)}, bf16[8,256,128]{2,1,0:T(8,128)(2,1)S(1)}, f32[8,64,128]{2,1,0:T(8,128)S(1)}) custom-call(s32[2]{0:T(128)S(1)} %pad_add_fusion.where_ref, bf16[8,320,128]{2,1,0:T(8,128)(2,1)S(1)} %all-to-all-done.all_ref, bf16[8,256,128]{2,1,0:T(8,128)(2,1)S(1)} %collective-permute-done.sw_ref, ...), custom_call_target="tpu_custom_call" | custom-call | flops 10000000000 | bytes 1048576 | tf_op jit(solution)/shard_map/pallas_call | solution.py:383
  49.7 2.4 %collective-permute-start.8 = (bf16[8,256,128]{2,1,0:T(8,128)(2,1)S(1)}, bf16[8,256,128]{2,1,0:T(8,128)(2,1)S(1)}, u32[]{:S(2)}, u32[]{:S(2)}) collective-permute-start(bf16[8,256,128]{2,1,0:T(8,128)(2,1)S(1)} %get-tuple-element.59), channel_id=1, source_target_pairs={{0,8},{1,9},{2,10},{3,11},{4,12},{5,13},{6,14},{7,15},{8,0},{9,1},... | collective-permute-start | bytes 1572872 | tf_op jit(solution)/shard_map/ppermute | solution.py:497
  52.1 0.0 collective-permute-done.5.c1
  52.1 5.2 %collective-permute-done.6.c2 = bf16[8,64,128]{2,1,0:T(8,128)(2,1)S(1)} collective-permute-done((bf16[8,64,128]{2,1,0:T(8,128)(2,1)S(1)}, bf16[8,64,128]{2,1,0:T(8,128)(2,1)S(1)}, u32[]{:S(2)}, u32[]{:S(2)}) %collective-permute-start.6) | collective-permute-done | bytes 131104 | tf_op jit(solution)/shard_map/ppermute | solution.py:433
  57.3 0.1 shard_map.92
  57.4 0.0 copy-start
  57.4 0.1 add_convert_fusion
  57.6 26.5 %all_to_all.10.in_ref = bf16[8,320,128]{2,1,0:T(8,128)(2,1)S(1)} all-to-all(bf16[8,320,128]{2,1,0:T(8,128)(2,1)S(1)} %pad_maximum_fusion), channel_id=1, replica_groups=mesh['seq'=64,'head'=8] {'head'}, dimensions={0} | all-to-all | bytes 1310720 | tf_op jit(solution)/shard_map/all_to_all | solution.py:499
  84.1 1.8 %shard_map.93 = (bf16[1024,128]{1,0:T(8,128)(2,1)}, bf16[1024,128]{1,0:T(8,128)(2,1)}, bf16[256,128]{1,0:T(8,128)(2,1)}, bf16[256,128]{1,0:T(8,128)(2,1)}) custom-call(s32[8]{0:T(128)S(1)} %copy-done, bf16[8,320,128]{2,1,0:T(8,128)(2,1)S(1)} %all_to_all.10.in_ref), custom_call_target="tpu_custom_call" | custom-call | tf_op jit(solution)/shard_map/pallas_call | solution.py:383
  (6 shorter events, 0.1 us)
Async XLA Ops:
  3.2 16.8 %all-to-all-start = ((bf16[8,320,128]{2,1,0:T(8,128)(2,1)}), bf16[8,320,128]{2,1,0:T(8,128)(2,1)S(1)}, u32[]{:S(2)}, u32[]{:S(2)}) async-start(bf16[8,320,128]{2,1,0:T(8,128)(2,1)} %shard_map.84), calls=%async_computation | async-start | bytes 1310720 | tf_op jit(solution)/shard_map/all_to_all | solution.py:448
  20.0 7.7 %collective-permute-start.3 = (bf16[8,64,128]{2,1,0:T(8,128)(2,1)S(1)}, bf16[8,64,128]{2,1,0:T(8,128)(2,1)S(1)}, u32[]{:S(2)}, u32[]{:S(2)}) collective-permute-start(bf16[8,64,128]{2,1,0:T(8,128)(2,1)S(1)} %slice.9), channel_id=1, source_target_pairs={{0,48},{1,49},{2,50},{3,51},{36,84},{37,85},{38,86},{39,87},{8,56}... | collective-permute-start | bytes 393224 | tf_op jit(solution)/shard_map/ppermute | solution.py:429
  20.7 10.0 %collective-permute-start.2 = (bf16[8,64,128]{2,1,0:T(8,128)(2,1)S(1)}, bf16[8,64,128]{2,1,0:T(8,128)(2,1)S(1)}, u32[]{:S(2)}, u32[]{:S(2)}) collective-permute-start(bf16[8,64,128]{2,1,0:T(8,128)(2,1)S(1)} %slice.9), channel_id=1, source_target_pairs={{0,32},{16,48},{1,33},{17,49},{2,34},{18,50},{3,35},{19,51},{36,68... | collective-permute-start | bytes 393224 | tf_op jit(solution)/shard_map/ppermute | solution.py:429
  22.0 12.6 %collective-permute-start.1 = (bf16[8,64,128]{2,1,0:T(8,128)(2,1)S(1)}, bf16[8,64,128]{2,1,0:T(8,128)(2,1)S(1)}, u32[]{:S(2)}, u32[]{:S(2)}) collective-permute-start(bf16[8,64,128]{2,1,0:T(8,128)(2,1)S(1)} %slice.9), channel_id=1, source_target_pairs={{0,16},{16,32},{32,48},{1,17},{17,33},{33,49},{2,18},{18,34},{34,5... | collective-permute-start | bytes 393224 | tf_op jit(solution)/shard_map/ppermute | solution.py:429
  25.3 3.8 %collective-permute-start = (bf16[8,256,128]{2,1,0:T(8,128)(2,1)S(1)}, bf16[8,256,128]{2,1,0:T(8,128)(2,1)S(1)}, u32[]{:S(2)}, u32[]{:S(2)}) collective-permute-start(bf16[8,256,128]{2,1,0:T(8,128)(2,1)S(1)} %slice.8), channel_id=1, source_target_pairs={{0,8},{1,9},{2,10},{3,11},{4,12},{5,13},{6,14},{7,15},{8,0},{9,1},... | collective-permute-start | bytes 1572872 | tf_op jit(solution)/shard_map/ppermute | solution.py:451
  37.7 3.4 %collective-permute-start.4 = (f32[8,2048]{1,0:T(8,128)S(1)}, f32[8,2048]{1,0:T(8,128)S(1)}, u32[]{:S(2)}, u32[]{:S(2)}) collective-permute-start(f32[8,2048]{1,0:T(8,128)S(1)} %get-tuple-element.47.stats_ref), channel_id=1, source_target_pairs={{0,8},{1,9},{2,10},{3,11},{4,12},{5,13},{6,14},{7,15},{8,0},{9,1},... | collective-permute-start | bytes 196616 | tf_op jit(solution)/shard_map/ppermute | solution.py:474
  43.3 8.8 %collective-permute-start.5 = (bf16[8,64,128]{2,1,0:T(8,128)(2,1)S(1)}, bf16[8,64,128]{2,1,0:T(8,128)(2,1)S(1)}, u32[]{:S(2)}, u32[]{:S(2)}) collective-permute-start(bf16[8,64,128]{2,1,0:T(8,128)(2,1)S(1)} %get-tuple-element.55), channel_id=1, source_target_pairs={{16,0},{32,16},{48,32},{17,1},{33,17},{49,33},{18,2},{34,18},{50,3... | collective-permute-start | bytes 393224 | tf_op jit(solution)/shard_map/ppermute | solution.py:433
  45.2 12.1 %collective-permute-start.6 = (bf16[8,64,128]{2,1,0:T(8,128)(2,1)S(1)}, bf16[8,64,128]{2,1,0:T(8,128)(2,1)S(1)}, u32[]{:S(2)}, u32[]{:S(2)}) collective-permute-start(bf16[8,64,128]{2,1,0:T(8,128)(2,1)S(1)} %get-tuple-element.56), channel_id=1, source_target_pairs={{32,0},{48,16},{33,1},{49,17},{34,2},{50,18},{35,3},{51,19},{68,36... | collective-permute-start | bytes 393224 | tf_op jit(solution)/shard_map/ppermute | solution.py:433
  46.5 10.8 %collective-permute-start.7 = (bf16[8,64,128]{2,1,0:T(8,128)(2,1)S(1)}, bf16[8,64,128]{2,1,0:T(8,128)(2,1)S(1)}, u32[]{:S(2)}, u32[]{:S(2)}) collective-permute-start(bf16[8,64,128]{2,1,0:T(8,128)(2,1)S(1)} %get-tuple-element.57), channel_id=1, source_target_pairs={{48,0},{49,1},{50,2},{51,3},{84,36},{85,37},{86,38},{87,39},{56,8}... | collective-permute-start | bytes 393224 | tf_op jit(solution)/shard_map/ppermute | solution.py:433
  49.7 7.7 %collective-permute-start.8 = (bf16[8,256,128]{2,1,0:T(8,128)(2,1)S(1)}, bf16[8,256,128]{2,1,0:T(8,128)(2,1)S(1)}, u32[]{:S(2)}, u32[]{:S(2)}) collective-permute-start(bf16[8,256,128]{2,1,0:T(8,128)(2,1)S(1)} %get-tuple-element.59), channel_id=1, source_target_pairs={{0,8},{1,9},{2,10},{3,11},{4,12},{5,13},{6,14},{7,15},{8,0},{9,1},... | collective-permute-start | bytes 1572872 | tf_op jit(solution)/shard_map/ppermute | solution.py:497
  57.4 26.7 %copy-start = (s32[8]{0:T(128)S(1)}, s32[8]{0:T(128)}, u32[]{:S(2)}) copy-start(s32[8]{0:T(128)} %shift_ref.1) | copy-start | bytes 100

commit v10 on v9

--- a/solution.py
+++ b/solution.py
@@ -202,7 +202,7 @@
 
 def probs_kernel(
     where_ref, qt_ref, dt_ref, s0_ref, dp0_ref, m0_ref, s3_ref, dp3_ref, m3_ref,
-    qo_s, do_s, s0o_ref, dp0o_ref, m0o_ref, a1, a2, a3,
+    qo_s, do_s, s0o_ref, dp0o_ref, m0o_ref, s3o_ref, dp3o_ref, m3o_ref, a1, a2, a3,
     p_ref, dpm_ref, dpo_ref, stats_ref, k_s, v_s, m_s, l_s, r_s,
 ):
     chips = where_ref[0]
@@ -211,7 +211,7 @@
         k_s[n + 1] = ref[:, 0:SUB, :].reshape(TOK, HD)
         v_s[n + 1] = ref[:, SUB : 2 * SUB, :].reshape(TOK, HD)
     m_s[:, 0:ROWS] = jnp.maximum(m0_ref[...], m3_ref[...])
-    m_s[:, ROWS:BOTH] = m0o_ref[...]
+    m_s[:, ROWS:BOTH] = jnp.maximum(m0o_ref[...], m3o_ref[...])
 
     def scores(b, mine):
         for at in halves():
@@ -226,10 +226,6 @@
 
     lax.fori_loop(1, last, lambda b, _: scores(b, True), 0)
 
-    @pl.when(chips == 3)
-    def _():
-        scores(3, False)
-
     top = jnp.max(m_s[...], axis=0, keepdims=True)
     m_s[...] = jnp.broadcast_to(top, (8, BOTH))
 
@@ -260,9 +256,10 @@
 
     @pl.when(chips == 3)
     def _():
-        forward(3, False)
         for at in halves():
             probs(3, at, s3_ref[:, at], dp3_ref[:, at])
+            dpo_ref[3, :, at] = dp3o_ref[:, at]
+            probs(3, past(at), s3o_ref[:, at], dp3o_ref[:, at])
 
     stats_ref[0:1, :] = top
     stats_ref[1:2, :] = jnp.sum(l_s[...], axis=0, keepdims=True)
@@ -459,6 +456,7 @@
     qo, do, s0o, dp0o, m0o = run(
         other_kernel, (half, half, part, part, top), [], where, everything, swapped, cost=None
     )
+    s3o, dp3o, m3o = run(early_kernel, (part, part, top), [], where, qo, do, a[2])
     held, turned = pltpu.VMEM((4, TOK, HD), BF16), pltpu.VMEM((HD, ROWS), BF16)
     probs, dp, dpo, stats = run(
         probs_kernel,
@@ -469,7 +467,7 @@
             flat,
         ),
         [held, held, rows, rows, rows],
-        where, qt, dt, s0, dp0, m0, s3, dp3, m3, qo, do, s0o, dp0o, m0o, *a,
+        where, qt, dt, s0, dp0, m0, s3, dp3, m3, qo, do, s0o, dp0o, m0o, s3o, dp3o, m3o, *a,
     )
     swapped_stats = lax.ppermute(stats, AXES, SWAP)
     (o,) = run(

time: 86.3 us -> 86.6 us (level)
  Pallas kernels: 15.8 us -> 16.7 us
    pallas_call x9 -> x10, Pallas kernels: 13.2 us -> 14 us  [run(): pl.pallas_call(kernel, out_shape=outs, in_specs=[first] + [VM] * (len(ope...]
  transfers between devices with their start and end apart: 10 -> 10, of which waited for: 5 -> 4; matrix products, arithmetic and copies ran while one was open for 0% -> 0% of each run, Pallas kernels for 7% -> 8%
where the time goes in v10:
time: 86.6 us; the launch traced here: 86.2 us
  blocking collectives  26.5 us (31%)
  starting transfers between devices  21.4 us (25%)
  waiting for transfers between devices  20.5 us (24%)
  Pallas kernels  16.7 us (19%)
    all_to_all x1, blocking collectives, local(): lax.all_to_all(jnp.concatenate((grads, oq), axis=1), 'head', 0, 0, tiled=...  26.5 us
    pallas_call x10, Pallas kernels, run(): pl.pallas_call(kernel, out_shape=outs, in_specs=[first] + [VM] * (len(ope...  14 us
    all_to_all x1, waiting for transfers between devices, local(): everything = lax.all_to_all(packed, 'head', 0, 0, tiled=True)  10.6 us
    all_to_all x1, starting transfers between devices, local(): everything = lax.all_to_all(packed, 'head', 0, 0, tiled=True)  6.12 us
    ppermute x3, starting transfers between devices, ahead(): lax.ppermute(x, AXES, [(r[i], r[i + dist]) for r in ALONG for i in range(...  5.17 us
    ppermute x3, waiting for transfers between devices, behind(): lax.ppermute(x, AXES, [(r[i + dist], r[i]) for r in ALONG for i in range(...  5.15 us
    ppermute x3, waiting for transfers between devices, ahead(): lax.ppermute(x, AXES, [(r[i], r[i + dist]) for r in ALONG for i in range(...  3.92 us
    ppermute x3, starting transfers between devices, behind(): lax.ppermute(x, AXES, [(r[i + dist], r[i]) for r in ALONG for i in range(...  3.89 us
  transfers between devices with their start and end apart: 10, of which 4 were waited for; matrix products, arithmetic and copies ran while one was open for 0% of the time, Pallas kernels for 8%

profile of v10, /device:TPU:176, one launch (start us, length us, event | category | flops | bytes accessed | tf_op | source)
XLA Modules:
  0.0 86.2 jit_solution(10302575664702844450)
XLA Ops:
  0.6 2.6 %shard_map.84 = bf16[8,320,128]{2,1,0:T(8,128)(2,1)} custom-call(s32[8]{0:T(128)} %shift_ref.1, bf16[256,128]{1,0:T(8,128)(2,1)} %bitcast.12, bf16[256,128]{1,0:T(8,128)(2,1)} %bitcast.13, bf16[1024,128]{1,0:T(8,128)(2,1)} %bitcast.10, bf16[1024,128]{1,0:T(8,128)(2,1)} %bitcast.11), custom_call_target="tpu_custom_call" | custom-call | tf_op jit(solution)/shard_map/pallas_call | solution.py:392
  3.3 6.1 %all-to-all-start = ((bf16[8,320,128]{2,1,0:T(8,128)(2,1)}), bf16[8,320,128]{2,1,0:T(8,128)(2,1)S(1)}, u32[]{:S(2)}, u32[]{:S(2)}) async-start(bf16[8,320,128]{2,1,0:T(8,128)(2,1)} %shard_map.84), calls=%async_computation | async-start | bytes 1310720 | tf_op jit(solution)/shard_map/all_to_all | solution.py:445
  9.4 0.1 pad_add_fusion.where_ref
  9.4 10.6 %all-to-all-done.all_ref = bf16[8,320,128]{2,1,0:T(8,128)(2,1)S(1)} async-done(((bf16[8,320,128]{2,1,0:T(8,128)(2,1)}), bf16[8,320,128]{2,1,0:T(8,128)(2,1)S(1)}, u32[]{:S(2)}, u32[]{:S(2)}) %all-to-all-start) | async-done | bytes 655392 | tf_op jit(solution)/shard_map/all_to_all | solution.py:445
  20.0 0.7 collective-permute-start.3
  20.7 1.3 %collective-permute-start.2 = (bf16[8,64,128]{2,1,0:T(8,128)(2,1)S(1)}, bf16[8,64,128]{2,1,0:T(8,128)(2,1)S(1)}, u32[]{:S(2)}, u32[]{:S(2)}) collective-permute-start(bf16[8,64,128]{2,1,0:T(8,128)(2,1)S(1)} %slice.9), channel_id=1, source_target_pairs={{0,32},{16,48},{1,33},{17,49},{2,34},{18,50},{3,35},{19,51},{36,68... | collective-permute-start | bytes 393224 | tf_op jit(solution)/shard_map/ppermute | solution.py:426
  22.0 3.2 %collective-permute-start.1 = (bf16[8,64,128]{2,1,0:T(8,128)(2,1)S(1)}, bf16[8,64,128]{2,1,0:T(8,128)(2,1)S(1)}, u32[]{:S(2)}, u32[]{:S(2)}) collective-permute-start(bf16[8,64,128]{2,1,0:T(8,128)(2,1)S(1)} %slice.9), channel_id=1, source_target_pairs={{0,16},{16,32},{32,48},{1,17},{17,33},{33,49},{2,18},{18,34},{34,5... | collective-permute-start | bytes 393224 | tf_op jit(solution)/shard_map/ppermute | solution.py:426
  25.3 1.9 %collective-permute-start = (bf16[8,256,128]{2,1,0:T(8,128)(2,1)S(1)}, bf16[8,256,128]{2,1,0:T(8,128)(2,1)S(1)}, u32[]{:S(2)}, u32[]{:S(2)}) collective-permute-start(bf16[8,256,128]{2,1,0:T(8,128)(2,1)S(1)} %slice.8), channel_id=1, source_target_pairs={{0,8},{1,9},{2,10},{3,11},{4,12},{5,13},{6,14},{7,15},{8,0},{9,1},... | collective-permute-start | bytes 1572872 | tf_op jit(solution)/shard_map/ppermute | solution.py:448
  27.2 0.5 shard_map.85
  27.7 0.6 shard_map.86
  28.3 0.8 collective-permute-done.sw_ref
  29.1 1.0 %shard_map.87 = (bf16[128,1024]{1,0:T(8,128)(2,1)S(1)}, bf16[128,1024]{1,0:T(8,128)(2,1)S(1)}, f32[256,1024]{1,0:T(8,128)S(1)}, f32[256,1024]{1,0:T(8,128)S(1)}, f32[8,1024]{1,0:T(8,128)S(1)}) custom-call(s32[2]{0:T(128)S(1)} %pad_add_fusion.where_ref, bf16[8,320,128]{2,1,0:T(8,128)(2,1)S(1)} %all-to-all-done.all_ref, ...), custom_call_target="tpu_custom_call" | custom-call | tf_op jit(solution)/shard_map/pallas_call | solution.py:380
  30.1 0.6 shard_map.88
  30.7 0.0 collective-permute-done.2.a2
  30.7 3.9 %collective-permute-done.1.a1 = bf16[8,64,128]{2,1,0:T(8,128)(2,1)S(1)} collective-permute-done((bf16[8,64,128]{2,1,0:T(8,128)(2,1)S(1)}, bf16[8,64,128]{2,1,0:T(8,128)(2,1)S(1)}, u32[]{:S(2)}, u32[]{:S(2)}) %collective-permute-start.1) | collective-permute-done | bytes 131104 | tf_op jit(solution)/shard_map/ppermute | solution.py:426
  34.6 3.2 %shard_map.89 = (f32[4,256,2048]{2,1,0:T(8,128)S(1)}, f32[2,256,1024]{2,1,0:T(8,128)S(1)}, f32[4,256,1024]{2,1,0:T(8,128)S(1)}, f32[8,2048]{1,0:T(8,128)S(1)}) custom-call(s32[2]{0:T(128)S(1)} %pad_add_fusion.where_ref, bf16[128,1024]{1,0:T(8,128)(2,1)S(1)} %get-tuple-element.37.qt_ref, bf16[128,1024]{1,0:T(8,128)(2,1)S(1)} %get-tuple-element.38.dt_ref, ...), custom_call_target="tpu_custom_call" | custom-call | tf_op jit(solution)/shard_map/pallas_call | solution.py:380
  37.8 1.9 %collective-permute-start.4 = (f32[8,2048]{1,0:T(8,128)S(1)}, f32[8,2048]{1,0:T(8,128)S(1)}, u32[]{:S(2)}, u32[]{:S(2)}) collective-permute-start(f32[8,2048]{1,0:T(8,128)S(1)} %get-tuple-element.53.stats_ref), channel_id=1, source_target_pairs={{0,8},{1,9},{2,10},{3,11},{4,12},{5,13},{6,14},{7,15},{8,0},{9,1},... | collective-permute-start | bytes 196616 | tf_op jit(solution)/shard_map/ppermute | solution.py:472
  39.7 1.5 %shard_map.91.o_ref = f32[128,2048]{1,0:T(8,128)S(1)} custom-call(s32[2]{0:T(128)S(1)} %pad_add_fusion.where_ref, bf16[8,320,128]{2,1,0:T(8,128)(2,1)S(1)} %all-to-all-done.all_ref, bf16[8,64,128]{2,1,0:T(8,128)(2,1)S(1)} %collective-permute-done.1.a1, bf16[8,64,128]{2,1,0:T(8,128)(2,1)S(1)} %collective-permute-done.2.a2, ...), custom_call_target="tpu_custom_call" | custom-call | flops 10000000000 | bytes 1048576 | tf_op jit(solution)/shard_map/pallas_call | solution.py:380
  41.2 0.0 collective-permute-done.4.swapped_stats_ref
  41.2 2.3 %shard_map.90 = (bf16[8,64,128]{2,1,0:T(8,128)(2,1)S(1)}, bf16[8,64,128]{2,1,0:T(8,128)(2,1)S(1)}, bf16[8,64,128]{2,1,0:T(8,128)(2,1)S(1)}, bf16[3,256,2048]{2,1...) custom-call(s32[2]{0:T(128)S(1)} %pad_add_fusion.where_ref, ...), custom_call_target="tpu_custom_call" | custom-call | tf_op jit(solution)/shard_map/pallas_call | solution.py:380
  43.5 1.9 %collective-permute-start.5 = (bf16[8,64,128]{2,1,0:T(8,128)(2,1)S(1)}, bf16[8,64,128]{2,1,0:T(8,128)(2,1)S(1)}, u32[]{:S(2)}, u32[]{:S(2)}) collective-permute-start(bf16[8,64,128]{2,1,0:T(8,128)(2,1)S(1)} %get-tuple-element.61), channel_id=1, source_target_pairs={{16,0},{32,16},{48,32},{17,1},{33,17},{49,33},{18,2},{34,18},{50,3... | collective-permute-start | bytes 393224 | tf_op jit(solution)/shard_map/ppermute | solution.py:430
  45.5 1.3 %collective-permute-start.6 = (bf16[8,64,128]{2,1,0:T(8,128)(2,1)S(1)}, bf16[8,64,128]{2,1,0:T(8,128)(2,1)S(1)}, u32[]{:S(2)}, u32[]{:S(2)}) collective-permute-start(bf16[8,64,128]{2,1,0:T(8,128)(2,1)S(1)} %get-tuple-element.62), channel_id=1, source_target_pairs={{32,0},{48,16},{33,1},{49,17},{34,2},{50,18},{35,3},{51,19},{68,36... | collective-permute-start | bytes 393224 | tf_op jit(solution)/shard_map/ppermute | solution.py:430
  46.8 0.7 collective-permute-start.7
  47.5 2.5 %shard_map.92 = (f32[8,256,128]{2,1,0:T(8,128)S(1)}, bf16[8,256,128]{2,1,0:T(8,128)(2,1)S(1)}, f32[8,64,128]{2,1,0:T(8,128)S(1)}) custom-call(s32[2]{0:T(128)S(1)} %pad_add_fusion.where_ref, bf16[8,320,128]{2,1,0:T(8,128)(2,1)S(1)} %all-to-all-done.all_ref, bf16[8,256,128]{2,1,0:T(8,128)(2,1)S(1)} %collective-permute-done.sw_ref, ...), custom_call_target="tpu_custom_call" | custom-call | flops 10000000000 | bytes 1048576 | tf_op jit(solution)/shard_map/pallas_call | solution.py:380
  50.0 2.4 %collective-permute-start.8 = (bf16[8,256,128]{2,1,0:T(8,128)(2,1)S(1)}, bf16[8,256,128]{2,1,0:T(8,128)(2,1)S(1)}, u32[]{:S(2)}, u32[]{:S(2)}) collective-permute-start(bf16[8,256,128]{2,1,0:T(8,128)(2,1)S(1)} %get-tuple-element.65), channel_id=1, source_target_pairs={{0,8},{1,9},{2,10},{3,11},{4,12},{5,13},{6,14},{7,15},{8,0},{9,1},... | collective-permute-start | bytes 1572872 | tf_op jit(solution)/shard_map/ppermute | solution.py:495
  52.4 5.1 %collective-permute-done.6.c2 = bf16[8,64,128]{2,1,0:T(8,128)(2,1)S(1)} collective-permute-done((bf16[8,64,128]{2,1,0:T(8,128)(2,1)S(1)}, bf16[8,64,128]{2,1,0:T(8,128)(2,1)S(1)}, u32[]{:S(2)}, u32[]{:S(2)}) %collective-permute-start.6) | collective-permute-done | bytes 131104 | tf_op jit(solution)/shard_map/ppermute | solution.py:430
  57.6 0.1 shard_map.93
  57.6 0.0 collective-permute-done.8
  57.7 0.0 copy-start
  57.7 0.1 add_convert_fusion
  57.8 26.5 %all_to_all.10.in_ref = bf16[8,320,128]{2,1,0:T(8,128)(2,1)S(1)} all-to-all(bf16[8,320,128]{2,1,0:T(8,128)(2,1)S(1)} %pad_maximum_fusion), channel_id=1, replica_groups=mesh['seq'=64,'head'=8] {'head'}, dimensions={0} | all-to-all | bytes 1310720 | tf_op jit(solution)/shard_map/all_to_all | solution.py:497
  84.4 1.8 %shard_map.94 = (bf16[1024,128]{1,0:T(8,128)(2,1)}, bf16[1024,128]{1,0:T(8,128)(2,1)}, bf16[256,128]{1,0:T(8,128)(2,1)}, bf16[256,128]{1,0:T(8,128)(2,1)}) custom-call(s32[8]{0:T(128)S(1)} %copy-done, bf16[8,320,128]{2,1,0:T(8,128)(2,1)S(1)} %all_to_all.10.in_ref), custom_call_target="tpu_custom_call" | custom-call | tf_op jit(solution)/shard_map/pallas_call | solution.py:380
  (7 shorter events, 0.1 us)
Async XLA Ops:
  3.3 16.8 %all-to-all-start = ((bf16[8,320,128]{2,1,0:T(8,128)(2,1)}), bf16[8,320,128]{2,1,0:T(8,128)(2,1)S(1)}, u32[]{:S(2)}, u32[]{:S(2)}) async-start(bf16[8,320,128]{2,1,0:T(8,128)(2,1)} %shard_map.84), calls=%async_computation | async-start | bytes 1310720 | tf_op jit(solution)/shard_map/all_to_all | solution.py:445
  20.0 7.7 %collective-permute-start.3 = (bf16[8,64,128]{2,1,0:T(8,128)(2,1)S(1)}, bf16[8,64,128]{2,1,0:T(8,128)(2,1)S(1)}, u32[]{:S(2)}, u32[]{:S(2)}) collective-permute-start(bf16[8,64,128]{2,1,0:T(8,128)(2,1)S(1)} %slice.9), channel_id=1, source_target_pairs={{0,48},{1,49},{2,50},{3,51},{36,84},{37,85},{38,86},{39,87},{8,56}... | collective-permute-start | bytes 393224 | tf_op jit(solution)/shard_map/ppermute | solution.py:426
  20.7 10.0 %collective-permute-start.2 = (bf16[8,64,128]{2,1,0:T(8,128)(2,1)S(1)}, bf16[8,64,128]{2,1,0:T(8,128)(2,1)S(1)}, u32[]{:S(2)}, u32[]{:S(2)}) collective-permute-start(bf16[8,64,128]{2,1,0:T(8,128)(2,1)S(1)} %slice.9), channel_id=1, source_target_pairs={{0,32},{16,48},{1,33},{17,49},{2,34},{18,50},{3,35},{19,51},{36,68... | collective-permute-start | bytes 393224 | tf_op jit(solution)/shard_map/ppermute | solution.py:426
  22.0 12.6 %collective-permute-start.1 = (bf16[8,64,128]{2,1,0:T(8,128)(2,1)S(1)}, bf16[8,64,128]{2,1,0:T(8,128)(2,1)S(1)}, u32[]{:S(2)}, u32[]{:S(2)}) collective-permute-start(bf16[8,64,128]{2,1,0:T(8,128)(2,1)S(1)} %slice.9), channel_id=1, source_target_pairs={{0,16},{16,32},{32,48},{1,17},{17,33},{33,49},{2,18},{18,34},{34,5... | collective-permute-start | bytes 393224 | tf_op jit(solution)/shard_map/ppermute | solution.py:426
  25.3 3.8 %collective-permute-start = (bf16[8,256,128]{2,1,0:T(8,128)(2,1)S(1)}, bf16[8,256,128]{2,1,0:T(8,128)(2,1)S(1)}, u32[]{:S(2)}, u32[]{:S(2)}) collective-permute-start(bf16[8,256,128]{2,1,0:T(8,128)(2,1)S(1)} %slice.8), channel_id=1, source_target_pairs={{0,8},{1,9},{2,10},{3,11},{4,12},{5,13},{6,14},{7,15},{8,0},{9,1},... | collective-permute-start | bytes 1572872 | tf_op jit(solution)/shard_map/ppermute | solution.py:448
  37.8 3.4 %collective-permute-start.4 = (f32[8,2048]{1,0:T(8,128)S(1)}, f32[8,2048]{1,0:T(8,128)S(1)}, u32[]{:S(2)}, u32[]{:S(2)}) collective-permute-start(f32[8,2048]{1,0:T(8,128)S(1)} %get-tuple-element.53.stats_ref), channel_id=1, source_target_pairs={{0,8},{1,9},{2,10},{3,11},{4,12},{5,13},{6,14},{7,15},{8,0},{9,1},... | collective-permute-start | bytes 196616 | tf_op jit(solution)/shard_map/ppermute | solution.py:472
  43.5 8.9 %collective-permute-start.5 = (bf16[8,64,128]{2,1,0:T(8,128)(2,1)S(1)}, bf16[8,64,128]{2,1,0:T(8,128)(2,1)S(1)}, u32[]{:S(2)}, u32[]{:S(2)}) collective-permute-start(bf16[8,64,128]{2,1,0:T(8,128)(2,1)S(1)} %get-tuple-element.61), channel_id=1, source_target_pairs={{16,0},{32,16},{48,32},{17,1},{33,17},{49,33},{18,2},{34,18},{50,3... | collective-permute-start | bytes 393224 | tf_op jit(solution)/shard_map/ppermute | solution.py:430
  45.5 12.1 %collective-permute-start.6 = (bf16[8,64,128]{2,1,0:T(8,128)(2,1)S(1)}, bf16[8,64,128]{2,1,0:T(8,128)(2,1)S(1)}, u32[]{:S(2)}, u32[]{:S(2)}) collective-permute-start(bf16[8,64,128]{2,1,0:T(8,128)(2,1)S(1)} %get-tuple-element.62), channel_id=1, source_target_pairs={{32,0},{48,16},{33,1},{49,17},{34,2},{50,18},{35,3},{51,19},{68,36... | collective-permute-start | bytes 393224 | tf_op jit(solution)/shard_map/ppermute | solution.py:430
  46.8 10.8 %collective-permute-start.7 = (bf16[8,64,128]{2,1,0:T(8,128)(2,1)S(1)}, bf16[8,64,128]{2,1,0:T(8,128)(2,1)S(1)}, u32[]{:S(2)}, u32[]{:S(2)}) collective-permute-start(bf16[8,64,128]{2,1,0:T(8,128)(2,1)S(1)} %get-tuple-element.63), channel_id=1, source_target_pairs={{48,0},{49,1},{50,2},{51,3},{84,36},{85,37},{86,38},{87,39},{56,8}... | collective-permute-start | bytes 393224 | tf_op jit(solution)/shard_map/ppermute | solution.py:430
  50.0 7.6 %collective-permute-start.8 = (bf16[8,256,128]{2,1,0:T(8,128)(2,1)S(1)}, bf16[8,256,128]{2,1,0:T(8,128)(2,1)S(1)}, u32[]{:S(2)}, u32[]{:S(2)}) collective-permute-start(bf16[8,256,128]{2,1,0:T(8,128)(2,1)S(1)} %get-tuple-element.65), channel_id=1, source_target_pairs={{0,8},{1,9},{2,10},{3,11},{4,12},{5,13},{6,14},{7,15},{8,0},{9,1},... | collective-permute-start | bytes 1572872 | tf_op jit(solution)/shard_map/ppermute | solution.py:495
  57.7 26.7 %copy-start = (s32[8]{0:T(128)S(1)}, s32[8]{0:T(128)}, u32[]{:S(2)}) copy-start(s32[8]{0:T(128)} %shift_ref.1) | copy-start | bytes 100
